TPU v7x, 512 devices: a whole 4x8x8 slice. The times are simulated.
512 devices in a mesh: tm: 32 (over y, x), gy: 16 (over z, core).
Axes of the slice: x: 4, y: 8, z: 8, core: 2. Of those that a mesh axis runs over, the one named last changes fastest.
Arguments:
- initial_state: float32 [3, 256, 1024], P(None, 'gy'), may hold values from -4 to 4
- guessed_ends: float32 [32, 3, 256, 1024], P('tm', None, 'gy'), may hold values from -4 to 4
- velocity: float32 [32, 2, 256, 1024], P('tm', None, 'gy'), may hold values from -1 to 1
Outputs:
- corrected: float32 [32, 3, 256, 1024], P('tm', None, 'gy')
- relaxed: float32 [32, 3, 256, 1024], P('tm', None, 'gy')
All inputs are finite; a program needn't handle non-finite values.
Results may differ from a plain program's by a relative error of at most 0.00002.
Values sent between devices are 32-bit elements; how exact they have to be, the bound alone decides.
No kernel may reach another device: no remote copies, remote signals or barrier semaphores. Data moves between devices by JAX's collectives and lax.ppermute only.
A program may use at most 64 MiB of HBM per device.

v0:
```python
import jax
import jax.numpy as jnp
from jax import lax
from jax.sharding import PartitionSpec as P

FINE = 4
GROUP = 4


diffusion = (0.05, 0.15, 0.4)
kappa_coupling = 0.1
time_step = 0.0125


def padded(block, sides, width):
    for axis, dim in sides:
        count = lax.axis_size(axis)
        forward = [(i, i + 1) for i in range(count - 1)]
        backward = [(target, source) for source, target in forward]
        low = lax.ppermute(
            lax.slice_in_dim(block, block.shape[dim] - width, None, axis=dim), axis, forward
        )
        high = lax.ppermute(lax.slice_in_dim(block, 0, width, axis=dim), axis, backward)
        block = jnp.concatenate([low, block, high], axis=dim)
    return block


def from_behind(block, axis, distance):
    devices = range(lax.axis_size(axis))
    route = [(i - distance, i) for i in devices if i - distance in devices]
    return lax.ppermute(block, axis, route)


def side_by_side(arrays, axis, dim, along):
    both = jnp.concatenate(arrays, axis=along)
    filled, at, outs = (lax.all_gather(both, axis, axis=dim, tiled=True), 0, [])
    for a in arrays:
        outs.append(lax.slice_in_dim(filled, at, at + a.shape[along], axis=along))
        at += a.shape[along]
    return tuple(outs)


def advance(extended, velocity, factor):
    center = extended[:, 1:-1]
    northern = extended[:, 2:]
    southern = extended[:, :-2]
    eastern = jnp.roll(center, -1, axis=2)
    western = jnp.roll(center, 1, axis=2)
    speed_across = velocity[0] + kappa_coupling * center[0]
    speed_along = velocity[1] + kappa_coupling * center[1]
    transport = jnp.maximum(speed_across, 0.0) * (center - western) + jnp.minimum(
        speed_across, 0.0
    ) * (eastern - center)
    transport = (
        transport
        + jnp.maximum(speed_along, 0.0) * (center - southern)
        + jnp.minimum(speed_along, 0.0) * (northern - center)
    )
    spread = northern + southern + eastern + western - 4.0 * center
    viscous = jnp.array(diffusion, jnp.float32)[:, None, None]
    return center + factor * (viscous * spread - transport)


def single(state, flow, factor):
    extended = padded(state, (("gy", 1),), 1)
    return advance(extended, flow, factor)


def from_left(state):
    return from_behind(state, "tm", 1)


def relayed(state, hops):
    for hop in range(hops):
        state = from_left(state)
    return state


def interval(state, flow, top_row, total_rows):
    extended = padded(jnp.concatenate([state, flow], axis=0), (("gy", 1),), FINE)
    height = state.shape[1]
    field = extended[:3]
    speeds = extended[3:]
    for section in range(FINE):
        kept = height + 2 * (FINE - section - 1)
        field = advance(field, speeds[:, section + 1 : section + 1 + kept], time_step)
        global_rows = top_row - (FINE - section - 1) + jnp.arange(kept)
        inside = (global_rows >= 0) & (global_rows < total_rows)
        field = jnp.where(inside[None, :, None], field, 0.0)
    return field


def per_device(initial_state, guessed_ends, velocity):
    state_here = guessed_ends[0]
    flow = velocity[0]
    groups = lax.axis_size("tm") // GROUP
    index_here = lax.axis_index("tm")
    position = index_here % GROUP
    cluster = index_here // GROUP
    height = initial_state.shape[1]
    top_row = lax.axis_index("gy") * height
    total_rows = height * lax.axis_size("gy")
    level_one = FINE * time_step
    coarsest = FINE * GROUP * time_step
    begin_state = jnp.where(index_here == 0, initial_state, from_left(state_here))
    fine_end = interval(begin_state, flow, top_row, total_rows)
    coarse_begin = single(begin_state, flow, level_one)
    sources = fine_end - coarse_begin
    current = coarse_begin + sources
    for k in range(1, GROUP):
        candidate = single(from_left(current), flow, level_one) + sources
        current = jnp.where(position == k, candidate, current)
    earlier = relayed(begin_state, GROUP - 1)
    forcing = current - single(earlier, flow, coarsest)
    all_forcing, all_flow = side_by_side((forcing[None], flow[None]), "tm", 0, 1)

    def advance_group(j, carry):
        state, owned, before = carry
        member = j * GROUP + GROUP - 1
        step_flow = lax.dynamic_index_in_dim(all_flow, member, 0, keepdims=False)
        step_forcing = lax.dynamic_index_in_dim(all_forcing, member, 0, keepdims=False)
        state = single(state, step_flow, coarsest) + step_forcing
        owned = jnp.where(j == cluster, state, owned)
        before = jnp.where(j + 1 == cluster, state, before)
        return (state, owned, before)

    carried = lax.fori_loop(0, groups, advance_group, (initial_state, initial_state, initial_state))
    settled = carried[1]
    previous = carried[2]
    current = single(previous, flow, level_one) + sources
    for k in range(1, GROUP - 1):
        candidate = single(from_left(current), flow, level_one) + sources
        current = jnp.where(position == k, candidate, current)
    corrected = jnp.where(position == GROUP - 1, settled, current)
    final_begin = jnp.where(index_here == 0, initial_state, from_left(corrected))
    relaxed = interval(final_begin, flow, top_row, total_rows)
    return (corrected[None], relaxed[None])


def solution(mesh):
    placed = (P(None, "gy", None), P("tm", None, "gy", None), P("tm", None, "gy", None))
    return jax.shard_map(
        per_device,
        mesh=mesh,
        in_specs=placed,
        out_specs=(P("tm", None, "gy", None), P("tm", None, "gy", None)),
        check_vma=False,
    )
```

profile of v0, /device:TPU:225, one launch (start us, length us, event | category | flops | bytes accessed | tf_op | source)
XLA Modules:
  0.0 383.6 jit_solution(4987371108500531343)
XLA Ops:
  7.2 3.1 collective-permute-start.2
  10.4 8.0 %collective-permute-done.2 = f32[3,16,1024]{2,1,0:T(8,128)S(1)} collective-permute-done((f32[3,16,1024]{2,1,0:T(8,128)}, f32[3,16,1024]{2,1,0:T(8,128)S(1)}, u32[]{:S(2)}, u32[]{:S(2)}) %collective-permute-start.2) | collective-permute-done | bytes 196640 | tf_op jit(solution)/shard_map/ppermute | solution.py:31
  19.5 6.6 %collective-permute-start.5 = (f32[5,4,1024]{2,1,0:T(4,128)S(1)}, f32[5,4,1024]{2,1,0:T(4,128)S(1)}, u32[]{:S(2)}, u32[]{:S(2)}) collective-permute-start(f32[5,4,1024]{2,1,0:T(4,128)S(1)} %get-tuple-element.384), channel_id=1, source_target_pairs={{0,1},{1,2},{2,3},{3,4},{4,5},{5,6},{6,7},{7,8},{8,9},{9,10},{10,1... | collective-permute-start | bytes 245768 | tf_op jit(solution)/shard_map/ppermute | solution.py:20
  26.2 1.9 collective-permute-start.6
  30.1 1.9 collective-permute-start.3
  32.0 4.9 %collective-permute-start.4 = (f32[3,1,1024]{2,1,0:T(1,128)S(1)}, f32[3,1,1024]{2,1,0:T(1,128)S(1)}, u32[]{:S(2)}, u32[]{:S(2)}) collective-permute-start(f32[3,1,1024]{2,1,0:T(1,128)S(1)} %get-tuple-element.459), channel_id=1, source_target_pairs={{0,1},{1,2},{2,3},{3,4},{4,5},{5,6},{6,7},{7,8},{8,9},{9,10},{10,1... | collective-permute-start | bytes 36872 | tf_op jit(solution)/shard_map/ppermute | solution.py:20
  41.1 2.1 collective-permute-start.7
  43.2 2.2 collective-permute-start.17
  45.4 7.9 %collective-permute-done.7 = f32[3,16,1024]{2,1,0:T(8,128)S(1)} collective-permute-done((f32[3,16,1024]{2,1,0:T(8,128)S(1)}, f32[3,16,1024]{2,1,0:T(8,128)S(1)}, u32[]{:S(2)}, u32[]{:S(2)}) %collective-permute-start.7) | collective-permute-done | bytes 196640 | tf_op jit(solution)/shard_map/ppermute | solution.py:31
  53.3 1.9 collective-permute-start.8
  55.2 4.9 %collective-permute-start.9 = (f32[3,1,1024]{2,1,0:T(1,128)S(1)}, f32[3,1,1024]{2,1,0:T(1,128)S(1)}, u32[]{:S(2)}, u32[]{:S(2)}) collective-permute-start(f32[3,1,1024]{2,1,0:T(1,128)S(1)} %get-tuple-element.453), channel_id=1, source_target_pairs={{0,1},{1,2},{2,3},{3,4},{4,5},{5,6},{6,7},{7,8},{8,9},{9,10},{10,1... | collective-permute-start | bytes 36872 | tf_op jit(solution)/shard_map/ppermute | solution.py:20
  61.1 1.9 collective-permute-start.10
  63.1 1.9 collective-permute-start.18
  65.0 8.3 %collective-permute-done.10 = f32[3,16,1024]{2,1,0:T(8,128)S(1)} collective-permute-done((f32[3,16,1024]{2,1,0:T(8,128)S(1)}, f32[3,16,1024]{2,1,0:T(8,128)S(1)}, u32[]{:S(2)}, u32[]{:S(2)}) %collective-permute-start.10) | collective-permute-done | bytes 196640 | tf_op jit(solution)/shard_map/ppermute | solution.py:31
  73.4 1.9 collective-permute-start.11
  75.3 4.9 %collective-permute-start.12 = (f32[3,1,1024]{2,1,0:T(1,128)S(1)}, f32[3,1,1024]{2,1,0:T(1,128)S(1)}, u32[]{:S(2)}, u32[]{:S(2)}) collective-permute-start(f32[3,1,1024]{2,1,0:T(1,128)S(1)} %get-tuple-element.447), channel_id=1, source_target_pairs={{0,1},{1,2},{2,3},{3,4},{4,5},{5,6},{6,7},{7,8},{8,9},{9,10},{10,1... | collective-permute-start | bytes 36872 | tf_op jit(solution)/shard_map/ppermute | solution.py:20
  81.2 1.9 collective-permute-start.13
  83.2 1.9 collective-permute-start.19
  85.1 5.4 %collective-permute-start.20 = (f32[3,1,1024]{2,1,0:T(1,128)S(1)}, f32[3,1,1024]{2,1,0:T(1,128)S(1)}, u32[]{:S(2)}, u32[]{:S(2)}) collective-permute-start(f32[3,1,1024]{2,1,0:T(1,128)S(1)} %get-tuple-element.461), channel_id=1, source_target_pairs={{0,1},{1,2},{2,3},{3,4},{4,5},{5,6},{6,7},{7,8},{8,9},{9,10},{10,1... | collective-permute-start | bytes 36872 | tf_op jit(solution)/shard_map/ppermute | solution.py:20
  91.1 1.9 collective-permute-start.14
  93.0 6.4 %collective-permute-start.15 = (f32[3,1,1024]{2,1,0:T(1,128)S(1)}, f32[3,1,1024]{2,1,0:T(1,128)S(1)}, u32[]{:S(2)}, u32[]{:S(2)}) collective-permute-start(f32[3,1,1024]{2,1,0:T(1,128)S(1)} %get-tuple-element.441), channel_id=1, source_target_pairs={{0,1},{1,2},{2,3},{3,4},{4,5},{5,6},{6,7},{7,8},{8,9},{9,10},{10,1... | collective-permute-start | bytes 36872 | tf_op jit(solution)/shard_map/ppermute | solution.py:20
  101.5 111.6 %all-gather.2.cloned.1.call-done = f32[32,5,16,1024]{3,2,1,0:T(8,128)} async-done(((f32[1,5,16,1024]{3,2,1,0:T(8,128)}), f32[32,5,16,1024]{3,2,1,0:T(8,128)}) %all-gather.2.cloned.1.call-update) | async-done | bytes 10485776 | tf_op jit(solution)/shard_map/all_gather | solution.py:36
  213.1 6.5 %slice.1111 = f32[32,3,16,1024]{3,2,1,0:T(8,128)} slice(f32[32,5,16,1024]{3,2,1,0:T(8,128)} %all-gather.2.cloned.1.call-done), slice={[0:32], [0:3], [0:16], [0:1024]} | slice | bytes 12582912 | tf_op jit(solution)/shard_map/slice | solution.py:38
  219.7 4.8 %slice.1110 = f32[32,2,16,1024]{3,2,1,0:T(8,128)} slice(f32[32,5,16,1024]{3,2,1,0:T(8,128)} %all-gather.2.cloned.1.call-done), slice={[0:32], [3:5], [0:16], [0:1024]} | slice | bytes 8388608 | tf_op jit(solution)/shard_map/slice | solution.py:38
  224.5 79.3 %while.22 = (s32[]{:T(128)}, f32[3,16,1024]{2,1,0:T(8,128)S(1)}, f32[3,16,1024]{2,1,0:T(8,128)S(1)}, f32[3,16,1024]{2,1,0:T(8,128)S(1)}, f32[32,2,16,1024]{3,2,1...) while((s32[]{:T(128)}, f32[3,16,1024]{2,1,0:T(8,128)S(1)}, ...), condition=%wide.region_1.2_spmd.clone, body=%wide.region_0.1_spmd.sunk.clone.sunk | while | flops 1458186 | bytes 4104527 | solution.py:127
  224.5 5.4 %collective-permute-start = (f32[3,1,1024]{2,1,0:T(1,128)S(1)}, f32[3,1,1024]{2,1,0:T(1,128)S(1)}, u32[]{:S(2)}, u32[]{:S(2)}) collective-permute-start(f32[3,1,1024]{2,1,0:T(1,128)S(1)} %get-tuple-element.533), channel_id=1, source_target_pairs={{0,1},{1,2},{2,3},{3,4},{4,5},{5,6},{6,7},{7,8},{8,9},{9,10},{10,1... | collective-permute-start | bytes 36872 | tf_op jit(solution)/shard_map/while/body/eval_jaxpr/ppermute | solution.py:20
  230.0 1.9 collective-permute-start.1
  233.0 3.2 collective-permute-done.1
  237.5 1.9 collective-permute-start
  239.4 2.4 collective-permute-start.1
  242.9 2.7 collective-permute-done.1
  247.0 1.9 collective-permute-start
  248.9 2.4 collective-permute-start.1
  252.4 2.7 collective-permute-done.1
  256.4 1.9 collective-permute-start
  258.4 2.4 collective-permute-start.1
  261.9 2.7 collective-permute-done.1
  265.9 1.9 collective-permute-start
  267.9 2.4 collective-permute-start.1
  271.4 2.7 collective-permute-done.1
  275.4 1.9 collective-permute-start
  277.3 2.4 collective-permute-start.1
  280.8 2.7 collective-permute-done.1
  284.9 1.9 collective-permute-start
  286.8 2.4 collective-permute-start.1
  290.3 2.7 collective-permute-done.1
  294.3 1.9 collective-permute-start
  296.3 2.4 collective-permute-start.1
  299.8 2.7 collective-permute-done.1
  303.9 1.9 collective-permute-start.21
  305.9 4.9 %collective-permute-start.22 = (f32[3,1,1024]{2,1,0:T(1,128)S(1)}, f32[3,1,1024]{2,1,0:T(1,128)S(1)}, u32[]{:S(2)}, u32[]{:S(2)}) collective-permute-start(f32[3,1,1024]{2,1,0:T(1,128)S(1)} %get-tuple-element.431), channel_id=1, source_target_pairs={{0,1},{1,2},{2,3},{3,4},{4,5},{5,6},{6,7},{7,8},{8,9},{9,10},{10,1... | collective-permute-start | bytes 36872 | tf_op jit(solution)/shard_map/ppermute | solution.py:20
  311.8 1.9 collective-permute-start.23
  313.7 9.0 %collective-permute-done.23 = f32[3,16,1024]{2,1,0:T(8,128)S(1)} collective-permute-done((f32[3,16,1024]{2,1,0:T(8,128)S(1)}, f32[3,16,1024]{2,1,0:T(8,128)S(1)}, u32[]{:S(2)}, u32[]{:S(2)}) %collective-permute-start.23) | collective-permute-done | bytes 196640 | tf_op jit(solution)/shard_map/ppermute | solution.py:31
  322.7 1.9 collective-permute-start.24
  324.6 5.4 %collective-permute-start.25 = (f32[3,1,1024]{2,1,0:T(1,128)S(1)}, f32[3,1,1024]{2,1,0:T(1,128)S(1)}, u32[]{:S(2)}, u32[]{:S(2)}) collective-permute-start(f32[3,1,1024]{2,1,0:T(1,128)S(1)} %get-tuple-element.425), channel_id=1, source_target_pairs={{0,1},{1,2},{2,3},{3,4},{4,5},{5,6},{6,7},{7,8},{8,9},{9,10},{10,1... | collective-permute-start | bytes 36872 | tf_op jit(solution)/shard_map/ppermute | solution.py:20
  331.1 1.9 collective-permute-start.26
  333.0 9.0 %collective-permute-done.26 = f32[3,16,1024]{2,1,0:T(8,128)S(1)} collective-permute-done((f32[3,16,1024]{2,1,0:T(8,128)S(1)}, f32[3,16,1024]{2,1,0:T(8,128)S(1)}, u32[]{:S(2)}, u32[]{:S(2)}) %collective-permute-start.26) | collective-permute-done | bytes 196640 | tf_op jit(solution)/shard_map/ppermute | solution.py:31
  342.0 1.9 collective-permute-start.27
  343.9 5.4 %collective-permute-start.28 = (f32[3,1,1024]{2,1,0:T(1,128)S(1)}, f32[3,1,1024]{2,1,0:T(1,128)S(1)}, u32[]{:S(2)}, u32[]{:S(2)}) collective-permute-start(f32[3,1,1024]{2,1,0:T(1,128)S(1)} %get-tuple-element.419), channel_id=1, source_target_pairs={{0,1},{1,2},{2,3},{3,4},{4,5},{5,6},{6,7},{7,8},{8,9},{9,10},{10,1... | collective-permute-start | bytes 36872 | tf_op jit(solution)/shard_map/ppermute | solution.py:20
  350.4 1.9 collective-permute-start.29
  352.3 8.9 %collective-permute-done.29 = f32[3,16,1024]{2,1,0:T(8,128)S(1)} collective-permute-done((f32[3,16,1024]{2,1,0:T(8,128)S(1)}, f32[3,16,1024]{2,1,0:T(8,128)S(1)}, u32[]{:S(2)}, u32[]{:S(2)}) %collective-permute-start.29) | collective-permute-done | bytes 196640 | tf_op jit(solution)/shard_map/ppermute | solution.py:31
  361.3 5.4 %collective-permute-start.30 = (f32[5,4,1024]{2,1,0:T(4,128)S(1)}, f32[5,4,1024]{2,1,0:T(4,128)S(1)}, u32[]{:S(2)}, u32[]{:S(2)}) collective-permute-start(f32[5,4,1024]{2,1,0:T(4,128)S(1)} %get-tuple-element.354), channel_id=1, source_target_pairs={{0,1},{1,2},{2,3},{3,4},{4,5},{5,6},{6,7},{7,8},{8,9},{9,10},{10,1... | collective-permute-start | bytes 245768 | tf_op jit(solution)/shard_map/ppermute | solution.py:20
  366.8 1.9 collective-permute-start.31
  368.7 5.0 %collective-permute-done.31 = f32[5,4,1024]{2,1,0:T(4,128)S(1)} collective-permute-done((f32[5,4,1024]{2,1,0:T(4,128)S(1)}, f32[5,4,1024]{2,1,0:T(4,128)S(1)}, u32[]{:S(2)}, u32[]{:S(2)}) %collective-permute-start.31) | collective-permute-done | bytes 81952 | tf_op jit(solution)/shard_map/ppermute | solution.py:23
  (185 shorter events, 37.1 us)
Async XLA Ops:
  7.2 32.3 %copy-start.5 = (f32[3]{0:T(128)S(1)}, f32[3]{0:T(128)}, u32[]{:S(2)}) copy-start(f32[3]{0:T(128)} %constant.195.clone) | copy-start | bytes 40
  7.2 206.0 %all-gather.2.cloned.1.call-start = ((), (), s32[]{:S(2)}) async-start(), calls=%async_computation | async-start | bytes 10813440 | tf_op jit(solution)/shard_map/all_gather | solution.py:36
  7.2 11.2 %collective-permute-start.2 = (f32[3,16,1024]{2,1,0:T(8,128)}, f32[3,16,1024]{2,1,0:T(8,128)S(1)}, u32[]{:S(2)}, u32[]{:S(2)}) collective-permute-start(f32[3,16,1024]{2,1,0:T(8,128)} %bitcast.273), channel_id=1, source_target_pairs={{0,16},{16,32},{32,48},{48,64},{64,80},{80,96},{96,112},{112,128},... | collective-permute-start | bytes 589832 | tf_op jit(solution)/shard_map/ppermute | solution.py:31
  19.5 17.4 %collective-permute-start.5 = (f32[5,4,1024]{2,1,0:T(4,128)S(1)}, f32[5,4,1024]{2,1,0:T(4,128)S(1)}, u32[]{:S(2)}, u32[]{:S(2)}) collective-permute-start(f32[5,4,1024]{2,1,0:T(4,128)S(1)} %get-tuple-element.384), channel_id=1, source_target_pairs={{0,1},{1,2},{2,3},{3,4},{4,5},{5,6},{6,7},{7,8},{8,9},{9,10},{10,1... | collective-permute-start | bytes 245768 | tf_op jit(solution)/shard_map/ppermute | solution.py:20
  26.2 10.7 %collective-permute-start.6 = (f32[5,4,1024]{2,1,0:T(4,128)S(1)}, f32[5,4,1024]{2,1,0:T(4,128)S(1)}, u32[]{:S(2)}, u32[]{:S(2)}) collective-permute-start(f32[5,4,1024]{2,1,0:T(4,128)S(1)} %get-tuple-element.385), channel_id=1, source_target_pairs={{1,0},{2,1},{3,2},{4,3},{5,4},{6,5},{7,6},{8,7},{9,8},{10,9},{11,1... | collective-permute-start | bytes 245768 | tf_op jit(solution)/shard_map/ppermute | solution.py:23
  28.2 15.0 %collective-permute-start.16 = (f32[3,16,1024]{2,1,0:T(8,128)S(1)}, f32[3,16,1024]{2,1,0:T(8,128)S(1)}, u32[]{:S(2)}, u32[]{:S(2)}) collective-permute-start(f32[3,16,1024]{2,1,0:T(8,128)S(1)} %broadcast_select_fusion.3), channel_id=1, source_target_pairs={{0,16},{16,32},{32,48},{48,64},{64,80},{80,96},{96,112},{112,128},... | collective-permute-start | bytes 589832 | tf_op jit(solution)/shard_map/ppermute | solution.py:31
  30.1 10.6 %collective-permute-start.3 = (f32[3,1,1024]{2,1,0:T(1,128)S(1)}, f32[3,1,1024]{2,1,0:T(1,128)S(1)}, u32[]{:S(2)}, u32[]{:S(2)}) collective-permute-start(f32[3,1,1024]{2,1,0:T(1,128)S(1)} %get-tuple-element.458), channel_id=1, source_target_pairs={{1,0},{2,1},{3,2},{4,3},{5,4},{6,5},{7,6},{8,7},{9,8},{10,9},{11,1... | collective-permute-start | bytes 36872 | tf_op jit(solution)/shard_map/ppermute | solution.py:23
  32.0 8.6 %collective-permute-start.4 = (f32[3,1,1024]{2,1,0:T(1,128)S(1)}, f32[3,1,1024]{2,1,0:T(1,128)S(1)}, u32[]{:S(2)}, u32[]{:S(2)}) collective-permute-start(f32[3,1,1024]{2,1,0:T(1,128)S(1)} %get-tuple-element.459), channel_id=1, source_target_pairs={{0,1},{1,2},{2,3},{3,4},{4,5},{5,6},{6,7},{7,8},{8,9},{9,10},{10,1... | collective-permute-start | bytes 36872 | tf_op jit(solution)/shard_map/ppermute | solution.py:20
  38.0 2.4 copy-start
  41.1 60.4 %copy-start.1 = (f32[3,16,1024]{2,1,0:T(8,128)S(1)}, f32[3,16,1024]{2,1,0:T(8,128)}, u32[]{:S(2)}) copy-start(f32[3,16,1024]{2,1,0:T(8,128)} %param.22) | copy-start | bytes 589828
  41.1 12.2 %collective-permute-start.7 = (f32[3,16,1024]{2,1,0:T(8,128)S(1)}, f32[3,16,1024]{2,1,0:T(8,128)S(1)}, u32[]{:S(2)}, u32[]{:S(2)}) collective-permute-start(f32[3,16,1024]{2,1,0:T(8,128)S(1)} %get-tuple-element.302), channel_id=1, source_target_pairs={{0,16},{16,32},{32,48},{48,64},{64,80},{80,96},{96,112},{112,128},... | collective-permute-start | bytes 589832 | tf_op jit(solution)/shard_map/ppermute | solution.py:31
  43.2 19.9 %collective-permute-start.17 = (f32[3,16,1024]{2,1,0:T(8,128)S(1)}, f32[3,16,1024]{2,1,0:T(8,128)S(1)}, u32[]{:S(2)}, u32[]{:S(2)}) collective-permute-start(f32[3,16,1024]{2,1,0:T(8,128)S(1)} %collective-permute-done.16), channel_id=1, source_target_pairs={{0,16},{16,32},{32,48},{48,64},{64,80},{80,96},{96,112},{112,128},... | collective-permute-start | bytes 589832 | tf_op jit(solution)/shard_map/ppermute | solution.py:31
  53.3 7.0 %collective-permute-start.8 = (f32[3,1,1024]{2,1,0:T(1,128)S(1)}, f32[3,1,1024]{2,1,0:T(1,128)S(1)}, u32[]{:S(2)}, u32[]{:S(2)}) collective-permute-start(f32[3,1,1024]{2,1,0:T(1,128)S(1)} %get-tuple-element.452), channel_id=1, source_target_pairs={{1,0},{2,1},{3,2},{4,3},{5,4},{6,5},{7,6},{8,7},{9,8},{10,9},{11,1... | collective-permute-start | bytes 36872 | tf_op jit(solution)/shard_map/ppermute | solution.py:23
  55.2 5.7 %collective-permute-start.9 = (f32[3,1,1024]{2,1,0:T(1,128)S(1)}, f32[3,1,1024]{2,1,0:T(1,128)S(1)}, u32[]{:S(2)}, u32[]{:S(2)}) collective-permute-start(f32[3,1,1024]{2,1,0:T(1,128)S(1)} %get-tuple-element.453), channel_id=1, source_target_pairs={{0,1},{1,2},{2,3},{3,4},{4,5},{5,6},{6,7},{7,8},{8,9},{9,10},{10,1... | collective-permute-start | bytes 36872 | tf_op jit(solution)/shard_map/ppermute | solution.py:20
  61.1 12.2 %collective-permute-start.10 = (f32[3,16,1024]{2,1,0:T(8,128)S(1)}, f32[3,16,1024]{2,1,0:T(8,128)S(1)}, u32[]{:S(2)}, u32[]{:S(2)}) collective-permute-start(f32[3,16,1024]{2,1,0:T(8,128)S(1)} %fusion.126), channel_id=1, source_target_pairs={{0,16},{16,32},{32,48},{48,64},{64,80},{80,96},{96,112},{112,128},... | collective-permute-start | bytes 589832 | tf_op jit(solution)/shard_map/ppermute | solution.py:31
  63.1 20.0 %collective-permute-start.18 = (f32[3,16,1024]{2,1,0:T(8,128)S(1)}, f32[3,16,1024]{2,1,0:T(8,128)S(1)}, u32[]{:S(2)}, u32[]{:S(2)}) collective-permute-start(f32[3,16,1024]{2,1,0:T(8,128)S(1)} %collective-permute-done.17), channel_id=1, source_target_pairs={{0,16},{16,32},{32,48},{48,64},{64,80},{80,96},{96,112},{112,128},... | collective-permute-start | bytes 589832 | tf_op jit(solution)/shard_map/ppermute | solution.py:31
  73.4 7.0 %collective-permute-start.11 = (f32[3,1,1024]{2,1,0:T(1,128)S(1)}, f32[3,1,1024]{2,1,0:T(1,128)S(1)}, u32[]{:S(2)}, u32[]{:S(2)}) collective-permute-start(f32[3,1,1024]{2,1,0:T(1,128)S(1)} %get-tuple-element.446), channel_id=1, source_target_pairs={{1,0},{2,1},{3,2},{4,3},{5,4},{6,5},{7,6},{8,7},{9,8},{10,9},{11,1... | collective-permute-start | bytes 36872 | tf_op jit(solution)/shard_map/ppermute | solution.py:23
  75.3 5.7 %collective-permute-start.12 = (f32[3,1,1024]{2,1,0:T(1,128)S(1)}, f32[3,1,1024]{2,1,0:T(1,128)S(1)}, u32[]{:S(2)}, u32[]{:S(2)}) collective-permute-start(f32[3,1,1024]{2,1,0:T(1,128)S(1)} %get-tuple-element.447), channel_id=1, source_target_pairs={{0,1},{1,2},{2,3},{3,4},{4,5},{5,6},{6,7},{7,8},{8,9},{9,10},{10,1... | collective-permute-start | bytes 36872 | tf_op jit(solution)/shard_map/ppermute | solution.py:20
  81.2 9.9 %collective-permute-start.13 = (f32[3,16,1024]{2,1,0:T(8,128)S(1)}, f32[3,16,1024]{2,1,0:T(8,128)S(1)}, u32[]{:S(2)}, u32[]{:S(2)}) collective-permute-start(f32[3,16,1024]{2,1,0:T(8,128)S(1)} %fusion.110), channel_id=1, source_target_pairs={{0,16},{16,32},{32,48},{48,64},{64,80},{80,96},{96,112},{112,128},... | collective-permute-start | bytes 589832 | tf_op jit(solution)/shard_map/ppermute | solution.py:31
  83.2 16.5 %collective-permute-start.19 = (f32[3,1,1024]{2,1,0:T(1,128)S(1)}, f32[3,1,1024]{2,1,0:T(1,128)S(1)}, u32[]{:S(2)}, u32[]{:S(2)}) collective-permute-start(f32[3,1,1024]{2,1,0:T(1,128)S(1)} %get-tuple-element.460), channel_id=1, source_target_pairs={{1,0},{2,1},{3,2},{4,3},{5,4},{6,5},{7,6},{8,7},{9,8},{10,9},{11,1... | collective-permute-start | bytes 36872 | tf_op jit(solution)/shard_map/ppermute | solution.py:23
  85.1 14.6 %collective-permute-start.20 = (f32[3,1,1024]{2,1,0:T(1,128)S(1)}, f32[3,1,1024]{2,1,0:T(1,128)S(1)}, u32[]{:S(2)}, u32[]{:S(2)}) collective-permute-start(f32[3,1,1024]{2,1,0:T(1,128)S(1)} %get-tuple-element.461), channel_id=1, source_target_pairs={{0,1},{1,2},{2,3},{3,4},{4,5},{5,6},{6,7},{7,8},{8,9},{9,10},{10,1... | collective-permute-start | bytes 36872 | tf_op jit(solution)/shard_map/ppermute | solution.py:20
  91.1 8.6 %collective-permute-start.14 = (f32[3,1,1024]{2,1,0:T(1,128)S(1)}, f32[3,1,1024]{2,1,0:T(1,128)S(1)}, u32[]{:S(2)}, u32[]{:S(2)}) collective-permute-start(f32[3,1,1024]{2,1,0:T(1,128)S(1)} %get-tuple-element.440), channel_id=1, source_target_pairs={{1,0},{2,1},{3,2},{4,3},{5,4},{6,5},{7,6},{8,7},{9,8},{10,9},{11,1... | collective-permute-start | bytes 36872 | tf_op jit(solution)/shard_map/ppermute | solution.py:23
  93.0 7.2 %collective-permute-start.15 = (f32[3,1,1024]{2,1,0:T(1,128)S(1)}, f32[3,1,1024]{2,1,0:T(1,128)S(1)}, u32[]{:S(2)}, u32[]{:S(2)}) collective-permute-start(f32[3,1,1024]{2,1,0:T(1,128)S(1)} %get-tuple-element.441), channel_id=1, source_target_pairs={{0,1},{1,2},{2,3},{3,4},{4,5},{5,6},{6,7},{7,8},{8,9},{9,10},{10,1... | collective-permute-start | bytes 36872 | tf_op jit(solution)/shard_map/ppermute | solution.py:20
  219.7 4.8 %copy-start.3 = (f32[3,16,1024]{2,1,0:T(8,128)S(1)}, f32[3,16,1024]{2,1,0:T(8,128)}, u32[]{:S(2)}) copy-start(f32[3,16,1024]{2,1,0:T(8,128)} %param.22) | copy-start | bytes 589828
  219.7 4.8 %copy-start.6 = (f32[3]{0:T(128)S(1)}, f32[3]{0:T(128)}, u32[]{:S(2)}) copy-start(f32[3]{0:T(128)} %constant.195.clone..sunk.2) | copy-start | bytes 40
  224.5 8.5 %collective-permute-start = (f32[3,1,1024]{2,1,0:T(1,128)S(1)}, f32[3,1,1024]{2,1,0:T(1,128)S(1)}, u32[]{:S(2)}, u32[]{:S(2)}) collective-permute-start(f32[3,1,1024]{2,1,0:T(1,128)S(1)} %get-tuple-element.533), channel_id=1, source_target_pairs={{0,1},{1,2},{2,3},{3,4},{4,5},{5,6},{6,7},{7,8},{8,9},{9,10},{10,1... | collective-permute-start | bytes 36872 | tf_op jit(solution)/shard_map/while/body/eval_jaxpr/ppermute | solution.py:20
  230.0 6.2 %collective-permute-start.1 = (f32[3,1,1024]{2,1,0:T(1,128)S(1)}, f32[3,1,1024]{2,1,0:T(1,128)S(1)}, u32[]{:S(2)}, u32[]{:S(2)}) collective-permute-start(f32[3,1,1024]{2,1,0:T(1,128)S(1)} %get-tuple-element.534), channel_id=1, source_target_pairs={{1,0},{2,1},{3,2},{4,3},{5,4},{6,5},{7,6},{8,7},{9,8},{10,9},{11,1... | collective-permute-start | bytes 36872 | tf_op jit(solution)/shard_map/while/body/eval_jaxpr/ppermute | solution.py:23
  237.5 5.5 %collective-permute-start = (f32[3,1,1024]{2,1,0:T(1,128)S(1)}, f32[3,1,1024]{2,1,0:T(1,128)S(1)}, u32[]{:S(2)}, u32[]{:S(2)}) collective-permute-start(f32[3,1,1024]{2,1,0:T(1,128)S(1)} %get-tuple-element.533), channel_id=1, source_target_pairs={{0,1},{1,2},{2,3},{3,4},{4,5},{5,6},{6,7},{7,8},{8,9},{9,10},{10,1... | collective-permute-start | bytes 36872 | tf_op jit(solution)/shard_map/while/body/eval_jaxpr/ppermute | solution.py:20
  239.4 6.2 %collective-permute-start.1 = (f32[3,1,1024]{2,1,0:T(1,128)S(1)}, f32[3,1,1024]{2,1,0:T(1,128)S(1)}, u32[]{:S(2)}, u32[]{:S(2)}) collective-permute-start(f32[3,1,1024]{2,1,0:T(1,128)S(1)} %get-tuple-element.534), channel_id=1, source_target_pairs={{1,0},{2,1},{3,2},{4,3},{5,4},{6,5},{7,6},{8,7},{9,8},{10,9},{11,1... | collective-permute-start | bytes 36872 | tf_op jit(solution)/shard_map/while/body/eval_jaxpr/ppermute | solution.py:23
  247.0 5.5 %collective-permute-start = (f32[3,1,1024]{2,1,0:T(1,128)S(1)}, f32[3,1,1024]{2,1,0:T(1,128)S(1)}, u32[]{:S(2)}, u32[]{:S(2)}) collective-permute-start(f32[3,1,1024]{2,1,0:T(1,128)S(1)} %get-tuple-element.533), channel_id=1, source_target_pairs={{0,1},{1,2},{2,3},{3,4},{4,5},{5,6},{6,7},{7,8},{8,9},{9,10},{10,1... | collective-permute-start | bytes 36872 | tf_op jit(solution)/shard_map/while/body/eval_jaxpr/ppermute | solution.py:20
  248.9 6.2 %collective-permute-start.1 = (f32[3,1,1024]{2,1,0:T(1,128)S(1)}, f32[3,1,1024]{2,1,0:T(1,128)S(1)}, u32[]{:S(2)}, u32[]{:S(2)}) collective-permute-start(f32[3,1,1024]{2,1,0:T(1,128)S(1)} %get-tuple-element.534), channel_id=1, source_target_pairs={{1,0},{2,1},{3,2},{4,3},{5,4},{6,5},{7,6},{8,7},{9,8},{10,9},{11,1... | collective-permute-start | bytes 36872 | tf_op jit(solution)/shard_map/while/body/eval_jaxpr/ppermute | solution.py:23
  256.4 5.5 %collective-permute-start = (f32[3,1,1024]{2,1,0:T(1,128)S(1)}, f32[3,1,1024]{2,1,0:T(1,128)S(1)}, u32[]{:S(2)}, u32[]{:S(2)}) collective-permute-start(f32[3,1,1024]{2,1,0:T(1,128)S(1)} %get-tuple-element.533), channel_id=1, source_target_pairs={{0,1},{1,2},{2,3},{3,4},{4,5},{5,6},{6,7},{7,8},{8,9},{9,10},{10,1... | collective-permute-start | bytes 36872 | tf_op jit(solution)/shard_map/while/body/eval_jaxpr/ppermute | solution.py:20
  258.4 6.2 %collective-permute-start.1 = (f32[3,1,1024]{2,1,0:T(1,128)S(1)}, f32[3,1,1024]{2,1,0:T(1,128)S(1)}, u32[]{:S(2)}, u32[]{:S(2)}) collective-permute-start(f32[3,1,1024]{2,1,0:T(1,128)S(1)} %get-tuple-element.534), channel_id=1, source_target_pairs={{1,0},{2,1},{3,2},{4,3},{5,4},{6,5},{7,6},{8,7},{9,8},{10,9},{11,1... | collective-permute-start | bytes 36872 | tf_op jit(solution)/shard_map/while/body/eval_jaxpr/ppermute | solution.py:23
  265.9 5.5 %collective-permute-start = (f32[3,1,1024]{2,1,0:T(1,128)S(1)}, f32[3,1,1024]{2,1,0:T(1,128)S(1)}, u32[]{:S(2)}, u32[]{:S(2)}) collective-permute-start(f32[3,1,1024]{2,1,0:T(1,128)S(1)} %get-tuple-element.533), channel_id=1, source_target_pairs={{0,1},{1,2},{2,3},{3,4},{4,5},{5,6},{6,7},{7,8},{8,9},{9,10},{10,1... | collective-permute-start | bytes 36872 | tf_op jit(solution)/shard_map/while/body/eval_jaxpr/ppermute | solution.py:20
  267.9 6.2 %collective-permute-start.1 = (f32[3,1,1024]{2,1,0:T(1,128)S(1)}, f32[3,1,1024]{2,1,0:T(1,128)S(1)}, u32[]{:S(2)}, u32[]{:S(2)}) collective-permute-start(f32[3,1,1024]{2,1,0:T(1,128)S(1)} %get-tuple-element.534), channel_id=1, source_target_pairs={{1,0},{2,1},{3,2},{4,3},{5,4},{6,5},{7,6},{8,7},{9,8},{10,9},{11,1... | collective-permute-start | bytes 36872 | tf_op jit(solution)/shard_map/while/body/eval_jaxpr/ppermute | solution.py:23
  275.4 5.5 %collective-permute-start = (f32[3,1,1024]{2,1,0:T(1,128)S(1)}, f32[3,1,1024]{2,1,0:T(1,128)S(1)}, u32[]{:S(2)}, u32[]{:S(2)}) collective-permute-start(f32[3,1,1024]{2,1,0:T(1,128)S(1)} %get-tuple-element.533), channel_id=1, source_target_pairs={{0,1},{1,2},{2,3},{3,4},{4,5},{5,6},{6,7},{7,8},{8,9},{9,10},{10,1... | collective-permute-start | bytes 36872 | tf_op jit(solution)/shard_map/while/body/eval_jaxpr/ppermute | solution.py:20
  277.3 6.2 %collective-permute-start.1 = (f32[3,1,1024]{2,1,0:T(1,128)S(1)}, f32[3,1,1024]{2,1,0:T(1,128)S(1)}, u32[]{:S(2)}, u32[]{:S(2)}) collective-permute-start(f32[3,1,1024]{2,1,0:T(1,128)S(1)} %get-tuple-element.534), channel_id=1, source_target_pairs={{1,0},{2,1},{3,2},{4,3},{5,4},{6,5},{7,6},{8,7},{9,8},{10,9},{11,1... | collective-permute-start | bytes 36872 | tf_op jit(solution)/shard_map/while/body/eval_jaxpr/ppermute | solution.py:23
  284.9 5.5 %collective-permute-start = (f32[3,1,1024]{2,1,0:T(1,128)S(1)}, f32[3,1,1024]{2,1,0:T(1,128)S(1)}, u32[]{:S(2)}, u32[]{:S(2)}) collective-permute-start(f32[3,1,1024]{2,1,0:T(1,128)S(1)} %get-tuple-element.533), channel_id=1, source_target_pairs={{0,1},{1,2},{2,3},{3,4},{4,5},{5,6},{6,7},{7,8},{8,9},{9,10},{10,1... | collective-permute-start | bytes 36872 | tf_op jit(solution)/shard_map/while/body/eval_jaxpr/ppermute | solution.py:20
  286.8 6.2 %collective-permute-start.1 = (f32[3,1,1024]{2,1,0:T(1,128)S(1)}, f32[3,1,1024]{2,1,0:T(1,128)S(1)}, u32[]{:S(2)}, u32[]{:S(2)}) collective-permute-start(f32[3,1,1024]{2,1,0:T(1,128)S(1)} %get-tuple-element.534), channel_id=1, source_target_pairs={{1,0},{2,1},{3,2},{4,3},{5,4},{6,5},{7,6},{8,7},{9,8},{10,9},{11,1... | collective-permute-start | bytes 36872 | tf_op jit(solution)/shard_map/while/body/eval_jaxpr/ppermute | solution.py:23
  294.3 5.5 %collective-permute-start = (f32[3,1,1024]{2,1,0:T(1,128)S(1)}, f32[3,1,1024]{2,1,0:T(1,128)S(1)}, u32[]{:S(2)}, u32[]{:S(2)}) collective-permute-start(f32[3,1,1024]{2,1,0:T(1,128)S(1)} %get-tuple-element.533), channel_id=1, source_target_pairs={{0,1},{1,2},{2,3},{3,4},{4,5},{5,6},{6,7},{7,8},{8,9},{9,10},{10,1... | collective-permute-start | bytes 36872 | tf_op jit(solution)/shard_map/while/body/eval_jaxpr/ppermute | solution.py:20
  296.3 6.2 %collective-permute-start.1 = (f32[3,1,1024]{2,1,0:T(1,128)S(1)}, f32[3,1,1024]{2,1,0:T(1,128)S(1)}, u32[]{:S(2)}, u32[]{:S(2)}) collective-permute-start(f32[3,1,1024]{2,1,0:T(1,128)S(1)} %get-tuple-element.534), channel_id=1, source_target_pairs={{1,0},{2,1},{3,2},{4,3},{5,4},{6,5},{7,6},{8,7},{9,8},{10,9},{11,1... | collective-permute-start | bytes 36872 | tf_op jit(solution)/shard_map/while/body/eval_jaxpr/ppermute | solution.py:23
  303.7 57.5 %copy-start.2 = (f32[3,16,1024]{2,1,0:T(8,128)S(1)}, f32[3,16,1024]{2,1,0:T(8,128)}, u32[]{:S(2)}) copy-start(f32[3,16,1024]{2,1,0:T(8,128)} %param.22) | copy-start | bytes 589828
  303.9 6.9 %collective-permute-start.21 = (f32[3,1,1024]{2,1,0:T(1,128)S(1)}, f32[3,1,1024]{2,1,0:T(1,128)S(1)}, u32[]{:S(2)}, u32[]{:S(2)}) collective-permute-start(f32[3,1,1024]{2,1,0:T(1,128)S(1)} %get-tuple-element.430), channel_id=1, source_target_pairs={{1,0},{2,1},{3,2},{4,3},{5,4},{6,5},{7,6},{8,7},{9,8},{10,9},{11,1... | collective-permute-start | bytes 36872 | tf_op jit(solution)/shard_map/ppermute | solution.py:23
  305.9 5.7 %collective-permute-start.22 = (f32[3,1,1024]{2,1,0:T(1,128)S(1)}, f32[3,1,1024]{2,1,0:T(1,128)S(1)}, u32[]{:S(2)}, u32[]{:S(2)}) collective-permute-start(f32[3,1,1024]{2,1,0:T(1,128)S(1)} %get-tuple-element.431), channel_id=1, source_target_pairs={{0,1},{1,2},{2,3},{3,4},{4,5},{5,6},{6,7},{7,8},{8,9},{9,10},{10,1... | collective-permute-start | bytes 36872 | tf_op jit(solution)/shard_map/ppermute | solution.py:20
  311.8 10.9 %collective-permute-start.23 = (f32[3,16,1024]{2,1,0:T(8,128)S(1)}, f32[3,16,1024]{2,1,0:T(8,128)S(1)}, u32[]{:S(2)}, u32[]{:S(2)}) collective-permute-start(f32[3,16,1024]{2,1,0:T(8,128)S(1)} %fusion.62), channel_id=1, source_target_pairs={{0,16},{16,32},{32,48},{48,64},{64,80},{80,96},{96,112},{112,128},... | collective-permute-start | bytes 589832 | tf_op jit(solution)/shard_map/ppermute | solution.py:31
  322.7 7.5 %collective-permute-start.24 = (f32[3,1,1024]{2,1,0:T(1,128)S(1)}, f32[3,1,1024]{2,1,0:T(1,128)S(1)}, u32[]{:S(2)}, u32[]{:S(2)}) collective-permute-start(f32[3,1,1024]{2,1,0:T(1,128)S(1)} %get-tuple-element.424), channel_id=1, source_target_pairs={{1,0},{2,1},{3,2},{4,3},{5,4},{6,5},{7,6},{8,7},{9,8},{10,9},{11,1... | collective-permute-start | bytes 36872 | tf_op jit(solution)/shard_map/ppermute | solution.py:23
  324.6 6.2 %collective-permute-start.25 = (f32[3,1,1024]{2,1,0:T(1,128)S(1)}, f32[3,1,1024]{2,1,0:T(1,128)S(1)}, u32[]{:S(2)}, u32[]{:S(2)}) collective-permute-start(f32[3,1,1024]{2,1,0:T(1,128)S(1)} %get-tuple-element.425), channel_id=1, source_target_pairs={{0,1},{1,2},{2,3},{3,4},{4,5},{5,6},{6,7},{7,8},{8,9},{9,10},{10,1... | collective-permute-start | bytes 36872 | tf_op jit(solution)/shard_map/ppermute | solution.py:20
  331.1 10.9 %collective-permute-start.26 = (f32[3,16,1024]{2,1,0:T(8,128)S(1)}, f32[3,16,1024]{2,1,0:T(8,128)S(1)}, u32[]{:S(2)}, u32[]{:S(2)}) collective-permute-start(f32[3,16,1024]{2,1,0:T(8,128)S(1)} %fusion.47), channel_id=1, source_target_pairs={{0,16},{16,32},{32,48},{48,64},{64,80},{80,96},{96,112},{112,128},... | collective-permute-start | bytes 589832 | tf_op jit(solution)/shard_map/ppermute | solution.py:31
  342.0 7.6 %collective-permute-start.27 = (f32[3,1,1024]{2,1,0:T(1,128)S(1)}, f32[3,1,1024]{2,1,0:T(1,128)S(1)}, u32[]{:S(2)}, u32[]{:S(2)}) collective-permute-start(f32[3,1,1024]{2,1,0:T(1,128)S(1)} %get-tuple-element.418), channel_id=1, source_target_pairs={{1,0},{2,1},{3,2},{4,3},{5,4},{6,5},{7,6},{8,7},{9,8},{10,9},{11,1... | collective-permute-start | bytes 36872 | tf_op jit(solution)/shard_map/ppermute | solution.py:23
  343.9 6.2 %collective-permute-start.28 = (f32[3,1,1024]{2,1,0:T(1,128)S(1)}, f32[3,1,1024]{2,1,0:T(1,128)S(1)}, u32[]{:S(2)}, u32[]{:S(2)}) collective-permute-start(f32[3,1,1024]{2,1,0:T(1,128)S(1)} %get-tuple-element.419), channel_id=1, source_target_pairs={{0,1},{1,2},{2,3},{3,4},{4,5},{5,6},{6,7},{7,8},{8,9},{9,10},{10,1... | collective-permute-start | bytes 36872 | tf_op jit(solution)/shard_map/ppermute | solution.py:20
  350.3 24.9 %copy-start.4 = (f32[3,16,1024]{2,1,0:T(8,128)}, f32[3,16,1024]{2,1,0:T(8,128)S(1)}, u32[]{:S(2)}) copy-start(f32[3,16,1024]{2,1,0:T(8,128)S(1)} %fusion.31) | copy-start | bytes 589828
  350.4 10.9 %collective-permute-start.29 = (f32[3,16,1024]{2,1,0:T(8,128)S(1)}, f32[3,16,1024]{2,1,0:T(8,128)S(1)}, u32[]{:S(2)}, u32[]{:S(2)}) collective-permute-start(f32[3,16,1024]{2,1,0:T(8,128)S(1)} %fusion.31), channel_id=1, source_target_pairs={{0,16},{16,32},{32,48},{48,64},{64,80},{80,96},{96,112},{112,128},... | collective-permute-start | bytes 589832 | tf_op jit(solution)/shard_map/ppermute | solution.py:31
  361.3 7.4 %collective-permute-start.30 = (f32[5,4,1024]{2,1,0:T(4,128)S(1)}, f32[5,4,1024]{2,1,0:T(4,128)S(1)}, u32[]{:S(2)}, u32[]{:S(2)}) collective-permute-start(f32[5,4,1024]{2,1,0:T(4,128)S(1)} %get-tuple-element.354), channel_id=1, source_target_pairs={{0,1},{1,2},{2,3},{3,4},{4,5},{5,6},{6,7},{7,8},{8,9},{9,10},{10,1... | collective-permute-start | bytes 245768 | tf_op jit(solution)/shard_map/ppermute | solution.py:20
  366.8 7.0 %collective-permute-start.31 = (f32[5,4,1024]{2,1,0:T(4,128)S(1)}, f32[5,4,1024]{2,1,0:T(4,128)S(1)}, u32[]{:S(2)}, u32[]{:S(2)}) collective-permute-start(f32[5,4,1024]{2,1,0:T(4,128)S(1)} %get-tuple-element.355), channel_id=1, source_target_pairs={{1,0},{2,1},{3,2},{4,3},{5,4},{6,5},{7,6},{8,7},{9,8},{10,9},{11,1... | collective-permute-start | bytes 245768 | tf_op jit(solution)/shard_map/ppermute | solution.py:23
Sparse Core Ops, SparseCore 0:
  101.6 111.5 all-gather.1
where the time goes:
time: 386 us; the launch traced here: 384 us
  waiting for transfers between devices  194 us (50%)
  starting transfers between devices  132 us (34%)
  other arithmetic  25.9 us (7%)
  local copies, waits for them, and re-layouts  16.5 us (4%)
  between operations  14.8 us (4%)
    all_gather x1, waiting for transfers between devices, side_by_side(): filled, at, outs = (lax.all_gather(both, axis, axis=dim, tiled=True), 0, [])  112 us
    ppermute x18, starting transfers between devices, padded(): lax.ppermute(lax.slice_in_dim(block, block.shape[dim] - width, None, axis...  73.1 us
    ppermute x10, waiting for transfers between devices, from_behind(): return lax.ppermute(block, axis, route)  51.5 us
    ppermute x18, starting transfers between devices, padded(): lax.ppermute(lax.slice_in_dim(block, 0, width, axis=dim), axis, backward)  37.8 us
    ppermute x18, waiting for transfers between devices, padded(): lax.ppermute(lax.slice_in_dim(block, 0, width, axis=dim), axis, backward)  27.3 us
    ppermute x10, starting transfers between devices, from_behind(): return lax.ppermute(block, axis, route)  20.8 us
    slice x2, local copies, waits for them, and re-layouts, side_by_side(): outs.append(lax.slice_in_dim(filled, at, at + a.shape[along], axis=along))  11.3 us
    select_n x8, other arithmetic, advance_group(): before = jnp.where(j + 1 == cluster, state, before)  9.41 us
  transfers between devices with their start and end apart: 47, of which 23 were waited for; matrix products, arithmetic and copies ran while one was open for 4% of the time, Pallas kernels for 0%

commit v1 on v0

v1 whole, which is shorter than its diff:
```python
import functools

import jax
import jax.numpy as jnp
from jax import lax
from jax.experimental import pallas as pl
from jax.experimental.pallas import tpu as pltpu
from jax.sharding import PartitionSpec as P

FINE = 4
GROUP = 4
GROUPS = 8
HALO = 16
TILE = 32
ROWS = 16
HALF = 64
BAND = 24

diffusion = (0.05, 0.15, 0.4)
kappa_coupling = 0.1
time_step = 0.0125
level_one = FINE * time_step
coarsest = FINE * GROUP * time_step

VMEM = pl.BlockSpec(memory_space=pltpu.VMEM)
SMEM = pl.BlockSpec(memory_space=pltpu.SMEM)


def lanes():
    return lax.broadcasted_iota(jnp.int32, (8, 128), 1)


def sublanes():
    return lax.broadcasted_iota(jnp.int32, (8, 128), 0)


def update(u, north, south, east, west, v0, v1, h):
    across = h * v0 + (h * kappa_coupling) * u[0]
    along = h * v1 + (h * kappa_coupling) * u[1]
    a, b = jnp.maximum(across, 0.0), jnp.minimum(across, 0.0)
    e, d = jnp.maximum(along, 0.0), jnp.minimum(along, 0.0)
    new = []
    for c in range(3):
        k = h * diffusion[c]
        x = (k - b) * (east[c] - u[c]) - (k + a) * (u[c] - west[c])
        y = (k - d) * (north[c] - u[c]) - (k + e) * (u[c] - south[c])
        new.append(u[c] + (x + y))
    return new


def cut_kernel(meta, init, ends, vel, out):
    last = meta[0] == GROUP * GROUPS - 1
    low = lanes() < HALF
    for a in range(5):
        if a < 3:
            top = jnp.where(last, init[a, 0:8, :], ends[a, 0:8, :])
            bottom = jnp.where(last, init[a, 8:16, :], ends[a, 8:16, :])
        else:
            top, bottom = vel[a - 3, 0:8, :], vel[a - 3, 8:16, :]
        for q in range(4):
            upper = pltpu.roll(top, (HALO - TILE * q) % 1024, 1)
            lower = pltpu.roll(bottom, (HALO + HALF - TILE * q) % 1024, 1)
            for b in range(8):
                at = slice(128 * b, 128 * b + 128)
                out[(4 * b + q) * 5 + a] = jnp.where(low, upper[:, at], lower[:, at])


def cycle_kernel(meta, prv, cur, nxt, out, ua, ub, vv, src, gg, ff, init, xa, xb, yy, cc):
    lane, sub = lanes(), sublanes()
    low = lane < HALF
    at_bottom = jnp.logical_and(low, meta[0] == 0)
    at_top = jnp.logical_and(jnp.logical_not(low), meta[0] == meta[1] - 1)

    def finish(buf, base):
        for c in range(3):
            buf[base + c, HALO] = jnp.where(at_bottom, 0.0, buf[base + c, HALO])
            buf[base + c, 9] = jnp.where(at_top, 0.0, buf[base + c, 9])
            buf[base + c, 0] = pltpu.roll(buf[base + c, BAND], HALF, 1)
            buf[base + c, BAND + 1] = pltpu.roll(buf[base + c, 1], HALF, 1)

    def step(buf, base, k, h, emit):
        def row(r, carry):
            u = [buf[base + c, r + 1] for c in range(3)]
            north = [buf[base + c, r + 2] for c in range(3)]
            south = [buf[base + c, r] for c in range(3)]
            east = [pltpu.roll(x, 127, 1) for x in u]
            west = [pltpu.roll(x, 1, 1) for x in u]
            emit(r, update(u, north, south, east, west, vv[2 * k, r], vv[2 * k + 1, r], h))
            return carry

        lax.fori_loop(0, BAND, row, 0, unroll=8)

    for k in range(GROUP):
        for a in range(5):
            for y in range(8):
                at = pl.ds(k * 40 + a * 8 + y, 8, stride=160)
                p, m, n = prv[at, :], cur[at, :], nxt[at, :]
                rows = (
                    (y, jnp.where(low, p, m)),
                    (y + 8, pltpu.roll(jnp.where(low, n, p), HALF, 1)),
                    (y + 16, jnp.where(low, m, n)),
                )
                for r, value in rows:
                    if a >= 3:
                        vv[2 * k + a - 3, r] = value
                    elif k == GROUP - 1:
                        value = pltpu.roll(value, 1, 0)
                        ua[a, r + 1] = value
                        init[a, r + 1] = value
                        xa[a, r + 1] = value
                    else:
                        ua[3 * (k + 1) + a, r + 1] = value

    finish(xa, 0)

    def first(k, carry):
        finish(ua, 3 * k)

        def coarse(r, new):
            for c in range(3):
                src[3 * k + c, r] = new[c]

        step(ua, 3 * k, k, level_one, coarse)
        return carry

    lax.fori_loop(0, GROUP, first, 0)

    def keep_g(r, new):
        for c in range(3):
            gg[c, r] = new[c]

    step(ua, 0, GROUP - 1, coarsest, keep_g)

    def into(buf, base):
        def emit(r, new):
            for c in range(3):
                buf[base + c, r + 1] = new[c]

        return emit

    def fine(k, carry):
        base = 3 * k

        def last(r, new):
            for c in range(3):
                ua[base + c, r + 1] = new[c]
                src[base + c, r] = new[c] - src[base + c, r]

        step(ua, base, k, time_step, into(ub, base))
        finish(ub, base)
        step(ub, base, k, time_step, into(ua, base))
        finish(ua, base)
        step(ua, base, k, time_step, into(ub, base))
        finish(ub, base)
        step(ub, base, k, time_step, last)
        finish(ua, base)
        return carry

    lax.fori_loop(0, GROUP, fine, 0)

    def plus(buf, k, base):
        def emit(r, new):
            for c in range(3):
                buf[base + c, r + 1] = new[c] + src[3 * k + c, r]

        return emit

    step(ua, 0, 1, level_one, plus(ub, 1, 0))
    finish(ub, 0)
    step(ub, 0, 2, level_one, plus(ua, 2, 0))
    finish(ua, 0)

    def forcing(r, new):
        for c in range(3):
            ff[c, r] = new[c] + src[3 * (GROUP - 1) + c, r] - gg[c, r]

    step(ua, 0, GROUP - 1, level_one, forcing)

    def settle(buf, to):
        def emit(r, new):
            for c in range(3):
                y = new[c] + ff[c, r]
                yy[c, r] = y
                to[c, r + 1] = jnp.where(sub == 0, init[c, r + 1], pltpu.roll(y, 1, 0))

        step(buf, 0, GROUP - 1, coarsest, emit)
        finish(to, 0)

    def two(i, carry):
        settle(xa, xb)
        settle(xb, xa)
        return carry

    lax.fori_loop(0, GROUPS // 2, two, 0)

    step(xa, 0, 0, level_one, plus(cc, 0, 0))
    finish(cc, 0)
    step(cc, 0, 1, level_one, plus(cc, 1, 3))
    finish(cc, 3)
    step(cc, 3, 2, level_one, plus(cc, 2, 6))

    def compact(read, c, y):
        m = jnp.where(low, read(c, y + 16), read(c, y))
        return jnp.where(lane < TILE, pltpu.roll(m, 128 - HALO, 1), pltpu.roll(m, 128 - HALO - TILE, 1))

    reads = [
        lambda c, r: xa[c, r + 1],
        lambda c, r: cc[c, r + 1],
        lambda c, r: cc[3 + c, r + 1],
        lambda c, r: cc[6 + c, r + 1],
        lambda c, r: yy[c, r],
    ]
    for c in range(3):
        for y in range(8):
            before = compact(reads[0], c, y)
            for k in range(GROUP):
                own = compact(reads[k + 1], c, y)
                value = jnp.where(low, own, pltpu.roll(before, HALF, 1))
                out[pl.ds(k * 24 + c * 8 + y, 8, stride=96), :] = value
                before = own


def join_kernel(tiles, vel, own, begin, up, down):
    lane = lanes()
    group = lane // TILE

    def rows_out(a, y0, b, value):
        begin[pl.ds((a * ROWS + y0) * 8 + b, 8, stride=8), :] = value
        if y0 == 0:
            down[pl.ds(a * FINE * 8 + b, FINE, stride=8), :] = value[0:FINE]
        else:
            up[pl.ds(a * FINE * 8 + b, FINE, stride=8), :] = value[8 - FINE : 8]

    for c in range(3):
        for b in range(8):
            t = [tiles[(4 * b + q) * 3 + c] for q in range(4)]
            for part in range(4):
                value = None
                for q in range(4):
                    shift = (TILE * (q - part)) % 128
                    x = pltpu.roll(t[q], shift, 1) if shift else t[q]
                    value = x if value is None else jnp.where(group == q, x, value)
                y0 = 8 * (part % 2)
                if part < 2:
                    own[c, y0 : y0 + 8, 128 * b : 128 * b + 128] = value
                else:
                    rows_out(c, y0, b, value)
    for c in range(2):
        for b in range(8):
            for y0 in (0, 8):
                rows_out(3 + c, y0, b, vel[c, y0 : y0 + 8, 128 * b : 128 * b + 128])


def relax_kernel(meta, mid, below, above, out, wa, wb, vv, flat):
    lane = lanes()
    tall = ROWS + 2 * FINE
    for a in range(5):
        buf, at = (wa, a * tall) if a < 3 else (vv, (a - 3) * tall)
        for r in range(FINE):
            buf[at + r] = below[a * FINE + r]
            buf[at + FINE + ROWS + r] = above[a * FINE + r]
        for r in range(ROWS):
            buf[at + FINE + r] = mid[a * ROWS + r]

    bottom, top = meta[0] == 0, meta[0] == meta[1] - 1
    buf, to = wa, wb
    for section in range(FINE):
        for r in range(section + 1, tall - section - 1):
            u = [buf[c * tall + r] for c in range(3)]
            north = [buf[c * tall + r + 1] for c in range(3)]
            south = [buf[c * tall + r - 1] for c in range(3)]
            east, west = [], []
            for x in u:
                x1 = pltpu.roll(x, 127, 1)
                east.append(jnp.where(lane == 127, pltpu.roll(x1, 7, 0), x1))
                x2 = pltpu.roll(x, 1, 1)
                west.append(jnp.where(lane == 0, pltpu.roll(x2, 1, 0), x2))
            new = update(u, north, south, east, west, vv[r], vv[tall + r], time_step)
            for c in range(3):
                if section == FINE - 1:
                    flat[(c * ROWS + r - FINE) * 8 : (c * ROWS + r - FINE) * 8 + 8, :] = new[c]
                elif r == FINE - 1:
                    to[c * tall + r] = jnp.where(bottom, 0.0, new[c])
                elif r == FINE + ROWS:
                    to[c * tall + r] = jnp.where(top, 0.0, new[c])
                else:
                    to[c * tall + r] = new[c]
        buf, to = to, buf
    for c in range(3):
        for b in range(8):
            for y0 in (0, 8):
                out[c, y0 : y0 + 8, 128 * b : 128 * b + 128] = flat[pl.ds((c * ROWS + y0) * 8 + b, 8, stride=8), :]


def f32(*shape):
    return jax.ShapeDtypeStruct(shape, jnp.float32)


def buffer(*shape):
    return pltpu.VMEM(shape, jnp.float32)


def call(kernel, n_scalars, n_arrays, outs, scratch=()):
    many = isinstance(outs, tuple)
    return pl.pallas_call(
        kernel,
        out_shape=outs,
        in_specs=[SMEM] * n_scalars + [VMEM] * n_arrays,
        out_specs=(VMEM,) * len(outs) if many else VMEM,
        scratch_shapes=list(scratch),
        compiler_params=pltpu.CompilerParams(vmem_limit_bytes=24 * 1024 * 1024),
    )


def cut(meta, init, ends, vel):
    return call(cut_kernel, 1, 3, f32(160, 8, 128))(meta, init, ends, vel)


def cycle(meta, prv, cur, nxt):
    tall = BAND + 2
    scratch = [
        buffer(12, tall, 8, 128),
        buffer(12, tall, 8, 128),
        buffer(8, BAND, 8, 128),
        buffer(12, BAND, 8, 128),
        buffer(3, BAND, 8, 128),
        buffer(3, BAND, 8, 128),
        buffer(3, tall, 8, 128),
        buffer(3, tall, 8, 128),
        buffer(3, tall, 8, 128),
        buffer(3, BAND, 8, 128),
        buffer(9, tall, 8, 128),
    ]
    return call(cycle_kernel, 1, 3, f32(768, 128), scratch)(meta, prv, cur, nxt)


def join(tiles, vel):
    halo = 5 * FINE * 8
    outs = (f32(3, ROWS, 1024), f32(5 * ROWS * 8, 128), f32(halo, 128), f32(halo, 128))
    return call(join_kernel, 0, 2, outs)(tiles, vel)


def relax(meta, mid, below, above):
    tall = ROWS + 2 * FINE
    scratch = [
        buffer(3 * tall, 8, 128),
        buffer(3 * tall, 8, 128),
        buffer(2 * tall, 8, 128),
        buffer(3 * ROWS * 8, 128),
    ]
    return call(relax_kernel, 1, 3, f32(3, ROWS, 1024), scratch)(meta, mid, below, above)


def per_device(initial_state, guessed_ends, velocity):
    slabs = lax.axis_size("gy")
    forward = [(i, i + 1) for i in range(slabs - 1)]
    backward = [(i + 1, i) for i in range(slabs - 1)]
    intervals = lax.axis_size("tm")
    here = lax.axis_index("tm").astype(jnp.int32).reshape(1)
    slab = jnp.stack([lax.axis_index("gy").astype(jnp.int32), jnp.int32(slabs)])
    flow = velocity[0]

    windows = cut(here, initial_state, guessed_ends[0], flow)
    cur = lax.all_to_all(windows.reshape(intervals, 40, 128), "tm", 0, 0)
    cur = cur.reshape(intervals * 40, 128)
    prv = lax.ppermute(cur, "gy", forward)
    nxt = lax.ppermute(cur, "gy", backward)
    tiles = cycle(slab, prv, cur, nxt)
    tiles = lax.all_to_all(tiles.reshape(intervals, 24, 128), "tm", 0, 0)
    own, mid, up, down = join(tiles.reshape(intervals * 3, 8, 128), flow)
    below = lax.ppermute(up, "gy", forward)
    above = lax.ppermute(down, "gy", backward)
    relaxed = relax(
        slab,
        mid.reshape(5 * ROWS, 8, 128),
        below.reshape(5 * FINE, 8, 128),
        above.reshape(5 * FINE, 8, 128),
    )
    return own[None], relaxed[None]


def solution(mesh):
    placed = (P(None, "gy", None), P("tm", None, "gy", None), P("tm", None, "gy", None))
    return jax.shard_map(
        per_device,
        mesh=mesh,
        in_specs=placed,
        out_specs=(P("tm", None, "gy", None), P("tm", None, "gy", None)),
        check_vma=False,
    )
```

time: 386 us -> 103 us (0.27)
  the two profiles are of different devices: /device:TPU:225 before, /device:TPU:1 now
where the time goes in v1:
time: 103 us; the launch traced here: 102 us
  blocking collectives  45.2 us (44%)
  Pallas kernels  23.2 us (23%)
  starting transfers between devices  18.8 us (18%)
  waiting for transfers between devices  11.3 us (11%)
  local copies, waits for them, and re-layouts  2.76 us (3%)
    all_to_all x1, blocking collectives, per_device(): cur = lax.all_to_all(windows.reshape(intervals, 40, 128), 'tm', 0, 0)  29 us
    pallas_call x1, Pallas kernels, cycle(): return call(cycle_kernel, 1, 3, f32(768, 128), scratch)(meta, prv, cur, nxt)  19.8 us
    all_to_all x1, blocking collectives, per_device(): tiles = lax.all_to_all(tiles.reshape(intervals, 24, 128), 'tm', 0, 0)  16.2 us
    ppermute x1, starting transfers between devices, per_device(): below = lax.ppermute(up, 'gy', forward)  8.62 us
    ppermute x1, waiting for transfers between devices, per_device(): nxt = lax.ppermute(cur, 'gy', backward)  6.25 us
    ppermute x1, starting transfers between devices, per_device(): nxt = lax.ppermute(cur, 'gy', backward)  4.35 us
    ppermute x1, starting transfers between devices, per_device(): prv = lax.ppermute(cur, 'gy', forward)  3.9 us
    ppermute x1, waiting for transfers between devices, per_device(): above = lax.ppermute(down, 'gy', backward)  3.82 us
  transfers between devices with their start and end apart: 4, of which 3 were waited for; matrix products, arithmetic and copies ran while one was open for 0% of the time, Pallas kernels for 0%

profile of v1, /device:TPU:1, one launch (start us, length us, event | category | flops | bytes accessed | tf_op | source)
XLA Modules:
  0.0 102.0 jit_solution(17677812026932969380)
XLA Ops:
  0.6 0.0 copy-start
  0.6 0.9 copy-done
  1.5 0.0 copy-start.2
  1.5 0.9 copy-done.2
  2.5 0.0 copy-start.3
  2.5 0.9 copy-done.3
  3.4 0.4 shard_map.50
  3.8 29.0 %all_to_all.10 = f32[32,40,128]{2,1,0:T(8,128)S(1)} all-to-all(f32[32,40,128]{2,1,0:T(8,128)S(1)} %bitcast.16), channel_id=1, replica_groups=mesh['tm'=32,'gy'=16] {'tm'}, dimensions={0} | all-to-all | bytes 1310720 | tf_op jit(solution)/shard_map/all_to_all | solution.py:364
  32.8 4.4 %collective-permute-start.1 = (f32[1280,128]{1,0:T(8,128)S(1)}, f32[1280,128]{1,0:T(8,128)S(1)}, u32[]{:S(2)}, u32[]{:S(2)}) collective-permute-start(f32[1280,128]{1,0:T(8,128)S(1)} %bitcast.13), channel_id=1, source_target_pairs={{1,0},{2,1},{3,2},{4,3},{5,4},{6,5},{7,6},{8,7},{9,8},{10,9},{11,1... | collective-permute-start | bytes 1966088 | tf_op jit(solution)/shard_map/ppermute | solution.py:367
  37.2 3.9 %collective-permute-start = (f32[1280,128]{1,0:T(8,128)S(1)}, f32[1280,128]{1,0:T(8,128)S(1)}, u32[]{:S(2)}, u32[]{:S(2)}) collective-permute-start(f32[1280,128]{1,0:T(8,128)S(1)} %bitcast.14), channel_id=1, source_target_pairs={{0,1},{1,2},{2,3},{3,4},{4,5},{5,6},{6,7},{7,8},{8,9},{9,10},{10,1... | collective-permute-start | bytes 1966088 | tf_op jit(solution)/shard_map/ppermute | solution.py:366
  41.1 0.1 pad_add_fusion.meta
  41.2 6.2 %collective-permute-done.1.nxt = f32[1280,128]{1,0:T(8,128)S(1)} collective-permute-done((f32[1280,128]{1,0:T(8,128)S(1)}, f32[1280,128]{1,0:T(8,128)S(1)}, u32[]{:S(2)}, u32[]{:S(2)}) %collective-permute-start.1) | collective-permute-done | bytes 655392 | tf_op jit(solution)/shard_map/ppermute | solution.py:367
  47.4 1.2 %collective-permute-done.prv = f32[1280,128]{1,0:T(8,128)S(1)} collective-permute-done((f32[1280,128]{1,0:T(8,128)S(1)}, f32[1280,128]{1,0:T(8,128)S(1)}, u32[]{:S(2)}, u32[]{:S(2)}) %collective-permute-start) | collective-permute-done | bytes 655392 | tf_op jit(solution)/shard_map/ppermute | solution.py:366
  48.6 19.8 %shard_map.51 = f32[768,128]{1,0:T(8,128)S(1)} custom-call(s32[2]{0:T(128)S(1)} %pad_add_fusion.meta, f32[1280,128]{1,0:T(8,128)S(1)} %collective-permute-done.prv, f32[1280,128]{1,0:T(8,128)S(1)} %bitcast.15, f32[1280,128]{1,0:T(8,128)S(1)} %collective-permute-done.1.nxt), custom_call_target="tpu_custom_call" | custom-call | tf_op jit(solution)/shard_map/pallas_call | solution.py:334
  68.4 0.0 copy-start.1
  68.4 16.2 %all_to_all.11 = f32[32,24,128]{2,1,0:T(8,128)S(1)} all-to-all(f32[32,24,128]{2,1,0:T(8,128)S(1)} %bitcast.18), channel_id=1, replica_groups=mesh['tm'=32,'gy'=16] {'tm'}, dimensions={0} | all-to-all | bytes 786432 | tf_op jit(solution)/shard_map/all_to_all | solution.py:369
  84.6 0.0 copy-done.1
  84.6 1.0 %shard_map.52 = (f32[3,16,1024]{2,1,0:T(8,128)}, f32[640,128]{1,0:T(8,128)S(1)}, f32[160,128]{1,0:T(8,128)S(1)}, f32[160,128]{1,0:T(8,128)S(1)}) custom-call(f32[96,8,128]{2,1,0:T(8,128)S(1)} %bitcast.17, f32[2,16,1024]{2,1,0:T(8,128)S(1)} %bitcast.20), custom_call_target="tpu_custom_call" | custom-call | tf_op jit(solution)/shard_map/pallas_call | solution.py:340
  85.7 8.6 %collective-permute-start.2 = (f32[160,128]{1,0:T(8,128)S(1)}, f32[160,128]{1,0:T(8,128)S(1)}, u32[]{:S(2)}, u32[]{:S(2)}) collective-permute-start(f32[160,128]{1,0:T(8,128)S(1)} %get-tuple-element.8), channel_id=1, source_target_pairs={{0,1},{1,2},{2,3},{3,4},{4,5},{5,6},{6,7},{7,8},{8,9},{9,10},{10,1... | collective-permute-start | bytes 245768 | tf_op jit(solution)/shard_map/ppermute | solution.py:371
  94.3 1.9 %collective-permute-start.3 = (f32[160,128]{1,0:T(8,128)S(1)}, f32[160,128]{1,0:T(8,128)S(1)}, u32[]{:S(2)}, u32[]{:S(2)}) collective-permute-start(f32[160,128]{1,0:T(8,128)S(1)} %get-tuple-element.9), channel_id=1, source_target_pairs={{1,0},{2,1},{3,2},{4,3},{5,4},{6,5},{7,6},{8,7},{9,8},{10,9},{11,1... | collective-permute-start | bytes 245768 | tf_op jit(solution)/shard_map/ppermute | solution.py:372
  96.2 0.0 collective-permute-done.2
  96.2 3.8 %collective-permute-done.3 = f32[160,128]{1,0:T(8,128)S(1)} collective-permute-done((f32[160,128]{1,0:T(8,128)S(1)}, f32[160,128]{1,0:T(8,128)S(1)}, u32[]{:S(2)}, u32[]{:S(2)}) %collective-permute-start.3) | collective-permute-done | bytes 81952 | tf_op jit(solution)/shard_map/ppermute | solution.py:372
  100.0 2.0 %shard_map.53 = f32[3,16,1024]{2,1,0:T(8,128)} custom-call(s32[2]{0:T(128)S(1)} %pad_add_fusion.meta, f32[80,8,128]{2,1,0:T(8,128)S(1)} %bitcast.21, f32[20,8,128]{2,1,0:T(8,128)S(1)} %bitcast.23, f32[20,8,128]{2,1,0:T(8,128)S(1)} %bitcast.24), custom_call_target="tpu_custom_call" | custom-call | tf_op jit(solution)/shard_map/pallas_call | solution.py:351
Async XLA Ops:
  0.6 0.9 copy-start
  1.5 0.9 copy-start.2
  2.5 0.9 copy-start.3
  32.8 14.6 %collective-permute-start.1 = (f32[1280,128]{1,0:T(8,128)S(1)}, f32[1280,128]{1,0:T(8,128)S(1)}, u32[]{:S(2)}, u32[]{:S(2)}) collective-permute-start(f32[1280,128]{1,0:T(8,128)S(1)} %bitcast.13), channel_id=1, source_target_pairs={{1,0},{2,1},{3,2},{4,3},{5,4},{6,5},{7,6},{8,7},{9,8},{10,9},{11,1... | collective-permute-start | bytes 1966088 | tf_op jit(solution)/shard_map/ppermute | solution.py:367
  37.2 11.4 %collective-permute-start = (f32[1280,128]{1,0:T(8,128)S(1)}, f32[1280,128]{1,0:T(8,128)S(1)}, u32[]{:S(2)}, u32[]{:S(2)}) collective-permute-start(f32[1280,128]{1,0:T(8,128)S(1)} %bitcast.14), channel_id=1, source_target_pairs={{0,1},{1,2},{2,3},{3,4},{4,5},{5,6},{6,7},{7,8},{8,9},{9,10},{10,1... | collective-permute-start | bytes 1966088 | tf_op jit(solution)/shard_map/ppermute | solution.py:366
  68.4 16.2 %copy-start.1 = (f32[1,2,16,1024]{3,2,1,0:T(8,128)S(1)}, f32[1,2,16,1024]{3,2,1,0:T(8,128)}, u32[]{:S(2)}) copy-start(f32[1,2,16,1024]{3,2,1,0:T(8,128)} %param.5) | copy-start | bytes 393220
  85.7 10.6 %collective-permute-start.2 = (f32[160,128]{1,0:T(8,128)S(1)}, f32[160,128]{1,0:T(8,128)S(1)}, u32[]{:S(2)}, u32[]{:S(2)}) collective-permute-start(f32[160,128]{1,0:T(8,128)S(1)} %get-tuple-element.8), channel_id=1, source_target_pairs={{0,1},{1,2},{2,3},{3,4},{4,5},{5,6},{6,7},{7,8},{8,9},{9,10},{10,1... | collective-permute-start | bytes 245768 | tf_op jit(solution)/shard_map/ppermute | solution.py:371
  94.3 5.8 %collective-permute-start.3 = (f32[160,128]{1,0:T(8,128)S(1)}, f32[160,128]{1,0:T(8,128)S(1)}, u32[]{:S(2)}, u32[]{:S(2)}) collective-permute-start(f32[160,128]{1,0:T(8,128)S(1)} %get-tuple-element.9), channel_id=1, source_target_pairs={{1,0},{2,1},{3,2},{4,3},{5,4},{6,5},{7,6},{8,7},{9,8},{10,9},{11,1... | collective-permute-start | bytes 245768 | tf_op jit(solution)/shard_map/ppermute | solution.py:372

commit v2 on v1

v2 whole, which is shorter than its diff:
```python
import jax
import jax.numpy as jnp
from jax import lax
from jax.experimental import pallas as pl
from jax.experimental.pallas import tpu as pltpu
from jax.sharding import PartitionSpec as P

FINE = 4
GROUP = 4
GROUPS = 8
HALO = 16
TILE = 32
ROWS = 16
HALF = 64
BAND = 24

diffusion = (0.05, 0.15, 0.4)
kappa_coupling = 0.1
time_step = 0.0125
level_one = FINE * time_step
coarsest = FINE * GROUP * time_step

VMEM = pl.BlockSpec(memory_space=pltpu.VMEM)
HBM = pl.BlockSpec(memory_space=pltpu.HBM)
SMEM = pl.BlockSpec(memory_space=pltpu.SMEM)


def lanes():
    return lax.broadcasted_iota(jnp.int32, (8, 128), 1)


def sublanes():
    return lax.broadcasted_iota(jnp.int32, (8, 128), 0)


def slope(u, plus, minus, east, west, across, along):
    a, b = jnp.maximum(across, 0.0), jnp.minimum(across, 0.0)
    e, d = jnp.maximum(along, 0.0), jnp.minimum(along, 0.0)
    out = []
    for c in range(3):
        k = diffusion[c]
        x = (k - b) * (east[c] - u[c]) - (k + a) * (u[c] - west[c])
        y = (k - d) * (plus[c] - u[c]) - (k + e) * (u[c] - minus[c])
        out.append(x + y)
    return out


def cut_kernel(meta, init_hbm, ends_hbm, vel_hbm, out, init, ends, vel, sems):
    copies = [
        pltpu.make_async_copy(far, near, sems.at[i])
        for i, (far, near) in enumerate(((init_hbm, init), (ends_hbm, ends), (vel_hbm, vel)))
    ]
    for copy in copies:
        copy.start()
    for copy in copies:
        copy.wait()
    last = meta[0] == GROUP * GROUPS - 1
    low = lanes() < HALF
    for a in range(5):
        if a < 3:
            top = jnp.where(last, init[a, 0:8, :], ends[a, 0:8, :])
            bottom = jnp.where(last, init[a, 8:16, :], ends[a, 8:16, :])
        else:
            top, bottom = vel[a - 3, 0:8, :], vel[a - 3, 8:16, :]
        for q in range(4):
            upper = pltpu.roll(top, (HALO - TILE * q) % 1024, 1)
            lower = pltpu.roll(bottom, (HALO + HALF - TILE * q) % 1024, 1)
            for b in range(8):
                at = slice(128 * b, 128 * b + 128)
                out[(4 * b + q) * 5 + a] = jnp.where(low, upper[:, at], lower[:, at])


def cycle_kernel(meta, mate, cur, other, out, ua, ub, vv, src, gg, ff, init, xa, xb, yy, cc):
    lane, sub = lanes(), sublanes()
    low = lane < HALF
    sign = jnp.where(low, 1.0, -1.0)
    swing = kappa_coupling * sign
    even = meta[0] % 2 == 0
    first = lane // HALF == meta[0] % 2
    outside = jnp.where(low, meta[0], meta[1] - 1 - meta[0]) == 0

    def step(buf, base, k, start, emit):
        rows = {}

        def row(r):
            if r not in rows:
                rows[r] = [buf[base + c, r] for c in range(3)]
            return rows[r]

        for r in range(start, BAND):
            u = row(r)
            east = [pltpu.roll(x, 127, 1) for x in u]
            west = [pltpu.roll(x, 1, 1) for x in u]
            across = vv[2 * k, r] + kappa_coupling * u[0]
            along = vv[2 * k + 1, r] + swing * u[1]
            emit(r, u, slope(u, row(r + 1), row(r - 1), east, west, across, along))

    def put(buf, at, r, value):
        if r == HALO - 1:
            value = jnp.where(outside, 0.0, value)
        buf[at, r] = value
        if r == BAND - 1:
            buf[at, BAND] = pltpu.roll(value, HALF, 1)

    for k in range(GROUP):
        for a in range(5):
            at = k * 40 + a * 8
            own = [cur[pl.ds(at + y, 8, stride=160), :] for y in range(8)]
            for y in range(8):
                up, down = jnp.where(even, y, 7 - y), jnp.where(even, 7 - y, y)
                o = other[pl.ds(at + up, 8, stride=160), :]
                m = mate[pl.ds(at + down, 8, stride=160), :]
                rows = (
                    (y, jnp.where(first, o, m)),
                    (y + 8, pltpu.roll(jnp.where(first, m, o), HALF, 1)),
                    (y + 16, jnp.where(low, own[y], own[7 - y])),
                )
                for r, value in rows:
                    if a == 3:
                        vv[2 * k, r] = value
                    elif a == 4:
                        vv[2 * k + 1, r] = sign * value
                    elif k == GROUP - 1:
                        value = pltpu.roll(value, 1, 0)
                        put(ua, a, r, value)
                        put(xa, a, r, value)
                        xb[a, r] = value
                        init[a, r] = value
                    else:
                        put(ua, 3 * (k + 1) + a, r, value)

    def keep_g(r, u, s):
        for c in range(3):
            gg[c, r] = u[c] + coarsest * s[c]

    step(ua, 0, GROUP - 1, 7, keep_g)

    def fine(k, carry):
        base = 3 * k

        def opening(r, u, s):
            for c in range(3):
                put(ub, base + c, r, u[c] + time_step * s[c])
                src[base + c, r] = u[c] + level_one * s[c]

        def onward(buf):
            def emit(r, u, s):
                for c in range(3):
                    put(buf, base + c, r, u[c] + time_step * s[c])

            return emit

        def closing(r, u, s):
            for c in range(3):
                end = u[c] + time_step * s[c]
                put(ua, base + c, r, end)
                src[base + c, r] = end - src[base + c, r]

        step(ua, base, k, 1, opening)
        step(ub, base, k, 2, onward(ua))
        step(ua, base, k, 3, onward(ub))
        step(ub, base, k, 4, closing)
        return carry

    lax.fori_loop(0, GROUP, fine, 0)

    def plus(buf, k, base):
        def emit(r, u, s):
            for c in range(3):
                put(buf, base + c, r, u[c] + level_one * s[c] + src[3 * k + c, r])

        return emit

    step(ua, 0, 1, 5, plus(ub, 1, 0))
    step(ub, 0, 2, 6, plus(ua, 2, 0))

    def forcing(r, u, s):
        for c in range(3):
            ff[c, r] = u[c] + level_one * s[c] + src[3 * (GROUP - 1) + c, r] - gg[c, r]

    step(ua, 0, GROUP - 1, 7, forcing)

    for t in range(GROUPS):
        buf, to = (xa, xb) if t % 2 == 0 else (xb, xa)

        def settle(r, u, s):
            for c in range(3):
                y = u[c] + coarsest * s[c] + ff[c, r]
                if t == GROUPS - 1 and r >= HALO:
                    yy[c, r] = y
                put(to, c, r, jnp.where(sub == 0, init[c, r], pltpu.roll(y, 1, 0)))

        step(buf, 0, GROUP - 1, max(7, 6 + t), settle)

    step(xa, 0, 0, 14, plus(cc, 0, 0))
    step(cc, 0, 1, 15, plus(cc, 1, 3))
    step(cc, 3, 2, 16, plus(cc, 2, 6))

    def compact(buf, base, c, y):
        m = jnp.where(low, buf[base + c, y + 16], buf[base + c, 23 - y])
        return jnp.where(lane < TILE, pltpu.roll(m, 128 - HALO, 1), pltpu.roll(m, 128 - HALO - TILE, 1))

    reads = [(xa, 0), (cc, 0), (cc, 3), (cc, 6), (yy, 0)]
    for c in range(3):
        for y in range(8):
            before = compact(*reads[0], c, y)
            for k in range(GROUP):
                own = compact(*reads[k + 1], c, y)
                value = jnp.where(low, own, pltpu.roll(before, HALF, 1))
                out[pl.ds(k * 24 + c * 8 + y, 8, stride=96), :] = value
                before = own


def join_kernel(meta, tiles, vel, own, begin, mate, other):
    group = lanes() // TILE
    even = meta[0] % 2 == 0

    def rows_out(a, b, top, bottom):
        begin[pl.ds(a * ROWS * 8 + b, 8, stride=8), :] = top
        begin[pl.ds((a * ROWS + 8) * 8 + b, 8, stride=8), :] = bottom
        down, up = top[0:FINE], bottom[8 - FINE : 8]
        at = pl.ds(a * FINE * 8 + b, FINE, stride=8)
        mate[at, :] = jnp.where(even, up, down)
        other[at, :] = jnp.where(even, down, up)

    for c in range(3):
        for b in range(8):
            t = [tiles[(4 * b + q) * 3 + c] for q in range(4)]
            parts = []
            for part in range(4):
                value = None
                for q in range(4):
                    shift = (TILE * (q - part)) % 128
                    x = pltpu.roll(t[q], shift, 1) if shift else t[q]
                    value = x if value is None else jnp.where(group == q, x, value)
                parts.append(value)
            at = slice(128 * b, 128 * b + 128)
            own[c, 0:8, at], own[c, 8:16, at] = parts[0], parts[1]
            rows_out(c, b, parts[2], parts[3])
    for c in range(2):
        for b in range(8):
            at = slice(128 * b, 128 * b + 128)
            rows_out(3 + c, b, vel[c, 0:8, at], vel[c, 8:16, at])


def relax_kernel(meta, mid, mate, other, out, wa, wb, vv, flat):
    lane = lanes()
    tall = ROWS + 2 * FINE
    even = meta[0] % 2 == 0
    for a in range(5):
        buf, at = (wa, a * tall) if a < 3 else (vv, (a - 3) * tall)
        for r in range(FINE):
            m, o = mate[a * FINE + r], other[a * FINE + r]
            buf[at + r] = jnp.where(even, o, m)
            buf[at + FINE + ROWS + r] = jnp.where(even, m, o)
        for r in range(ROWS):
            buf[at + FINE + r] = mid[a * ROWS + r]

    bottom, top = meta[0] == 0, meta[0] == meta[1] - 1
    buf, to = wa, wb
    for section in range(FINE):
        for r in range(section + 1, tall - section - 1):
            u = [buf[c * tall + r] for c in range(3)]
            north = [buf[c * tall + r + 1] for c in range(3)]
            south = [buf[c * tall + r - 1] for c in range(3)]
            east, west = [], []
            for x in u:
                x1 = pltpu.roll(x, 127, 1)
                east.append(jnp.where(lane == 127, pltpu.roll(x1, 7, 0), x1))
                x2 = pltpu.roll(x, 1, 1)
                west.append(jnp.where(lane == 0, pltpu.roll(x2, 1, 0), x2))
            across = vv[r] + kappa_coupling * u[0]
            along = vv[tall + r] + kappa_coupling * u[1]
            s = slope(u, north, south, east, west, across, along)
            for c in range(3):
                new = u[c] + time_step * s[c]
                if section == FINE - 1:
                    flat[(c * ROWS + r - FINE) * 8 : (c * ROWS + r - FINE) * 8 + 8, :] = new
                elif r == FINE - 1:
                    to[c * tall + r] = jnp.where(bottom, 0.0, new)
                elif r == FINE + ROWS:
                    to[c * tall + r] = jnp.where(top, 0.0, new)
                else:
                    to[c * tall + r] = new
        buf, to = to, buf
    for c in range(3):
        for b in range(8):
            for y0 in (0, 8):
                out[c, y0 : y0 + 8, 128 * b : 128 * b + 128] = flat[pl.ds((c * ROWS + y0) * 8 + b, 8, stride=8), :]


def f32(*shape):
    return jax.ShapeDtypeStruct(shape, jnp.float32)


def buffer(*shape):
    return pltpu.VMEM(shape, jnp.float32)


def call(kernel, n_scalars, n_arrays, outs, scratch=(), space=VMEM, mib=24):
    many = isinstance(outs, tuple)
    return pl.pallas_call(
        kernel,
        out_shape=outs,
        in_specs=[SMEM] * n_scalars + [space] * n_arrays,
        out_specs=(VMEM,) * len(outs) if many else VMEM,
        scratch_shapes=list(scratch),
        compiler_params=pltpu.CompilerParams(vmem_limit_bytes=mib * 1024 * 1024),
    )


def cut(meta, init, ends, vel):
    state, flow = buffer(3, ROWS, 1024), buffer(2, ROWS, 1024)
    scratch = [state, state, flow, pltpu.SemaphoreType.DMA((3,))]
    return call(cut_kernel, 1, 3, f32(160, 8, 128), scratch, HBM, 60)(meta, init, ends, vel)


def cycle(meta, mate, cur, other):
    tall = BAND + 1
    scratch = [
        buffer(12, tall, 8, 128),
        buffer(12, tall, 8, 128),
        buffer(8, BAND, 8, 128),
        buffer(12, BAND, 8, 128),
        buffer(3, BAND, 8, 128),
        buffer(3, BAND, 8, 128),
        buffer(3, tall, 8, 128),
        buffer(3, tall, 8, 128),
        buffer(3, tall, 8, 128),
        buffer(3, BAND, 8, 128),
        buffer(9, tall, 8, 128),
    ]
    return call(cycle_kernel, 1, 3, f32(768, 128), scratch)(meta, mate, cur, other)


def join(meta, tiles, vel):
    halo = 5 * FINE * 8
    outs = (f32(3, ROWS, 1024), f32(5 * ROWS * 8, 128), f32(halo, 128), f32(halo, 128))
    return call(join_kernel, 1, 2, outs)(meta, tiles, vel)


def relax(meta, mid, mate, other):
    tall = ROWS + 2 * FINE
    scratch = [
        buffer(3 * tall, 8, 128),
        buffer(3 * tall, 8, 128),
        buffer(2 * tall, 8, 128),
        buffer(3 * ROWS * 8, 128),
    ]
    return call(relax_kernel, 1, 3, f32(3, ROWS, 1024), scratch)(meta, mid, mate, other)


def per_device(initial_state, guessed_ends, velocity):
    slabs = lax.axis_size("gy")
    mates = [(i, i ^ 1) for i in range(slabs)]
    others = [(i, i + 1 if i % 2 else i - 1) for i in range(1, slabs - 1)]
    intervals = lax.axis_size("tm")
    here = lax.axis_index("tm").astype(jnp.int32).reshape(1)
    slab = jnp.stack([lax.axis_index("gy").astype(jnp.int32), jnp.int32(slabs)])
    flow = velocity[0]

    windows = cut(here, initial_state, guessed_ends[0], flow)
    cur = lax.all_to_all(windows.reshape(intervals, 40, 128), "tm", 0, 0)
    cur = cur.reshape(intervals * 40, 128)
    mate = lax.ppermute(cur, "gy", mates)
    other = lax.ppermute(cur, "gy", others)
    tiles = cycle(slab, mate, cur, other)
    tiles = lax.all_to_all(tiles.reshape(intervals, 24, 128), "tm", 0, 0)
    own, mid, mate, other = join(slab, tiles.reshape(intervals * 3, 8, 128), flow)
    mate = lax.ppermute(mate, "gy", mates)
    other = lax.ppermute(other, "gy", others)
    relaxed = relax(
        slab,
        mid.reshape(5 * ROWS, 8, 128),
        mate.reshape(5 * FINE, 8, 128),
        other.reshape(5 * FINE, 8, 128),
    )
    return own[None], relaxed[None]


def solution(mesh):
    placed = (P(None, "gy", None), P("tm", None, "gy", None), P("tm", None, "gy", None))
    return jax.shard_map(
        per_device,
        mesh=mesh,
        in_specs=placed,
        out_specs=(P("tm", None, "gy", None), P("tm", None, "gy", None)),
        check_vma=False,
    )
```

time: 103 us -> 90.6 us (0.88)
  Pallas kernels: 23.2 us -> 16.9 us
  waiting for transfers between devices: 11.3 us -> 8.35 us
  local copies, waits for them, and re-layouts: 2.76 us -> 0.01 us
  blocking collectives: 45.2 us -> 46.5 us
  starting transfers between devices: 18.8 us -> 17.6 us
    pallas_call x3, Pallas kernels: 21.3 us -> 14.9 us  [the longest x1 11 us: cycle(): call(cycle_kernel, 1, 3, f32(768, 128), scratch)(meta, mate, cur, other)]
    ppermute x4, waiting for transfers between devices: 11.3 us -> 8.35 us  [the longest x1 6.25 us: per_device(): other = lax.ppermute(cur, 'gy', others)]
    unnamed x8 -> x2, local copies, waits for them, and re-layouts: 2.76 us -> 0.01 us
    ppermute x4, starting transfers between devices: 18.8 us -> 17.6 us  [the longest x1 7.45 us: per_device(): other = lax.ppermute(other, 'gy', others)]
    all_to_all x1, blocking collectives: 16.2 us -> 17.3 us  [per_device(): tiles = lax.all_to_all(tiles.reshape(intervals, 24, 128), 'tm', 0, 0)]
  transfers between devices with their start and end apart: 4 -> 4, of which waited for: 3 -> 2; matrix products, arithmetic and copies ran while one was open for 0% -> 0% of each run, Pallas kernels for 0% -> 0%
where the time goes in v2:
time: 90.6 us; the launch traced here: 90.2 us
  blocking collectives  46.5 us (51%)
  starting transfers between devices  17.6 us (19%)
  Pallas kernels  16.9 us (19%)
  waiting for transfers between devices  8.35 us (9%)
    all_to_all x1, blocking collectives, per_device(): cur = lax.all_to_all(windows.reshape(intervals, 40, 128), 'tm', 0, 0)  29.2 us
    all_to_all x1, blocking collectives, per_device(): tiles = lax.all_to_all(tiles.reshape(intervals, 24, 128), 'tm', 0, 0)  17.3 us
    pallas_call x1, Pallas kernels, cycle(): call(cycle_kernel, 1, 3, f32(768, 128), scratch)(meta, mate, cur, other)  11 us
    ppermute x1, starting transfers between devices, per_device(): other = lax.ppermute(other, 'gy', others)  7.45 us
    ppermute x1, starting transfers between devices, per_device(): other = lax.ppermute(cur, 'gy', others)  6.33 us
    ppermute x1, waiting for transfers between devices, per_device(): other = lax.ppermute(cur, 'gy', others)  6.25 us
    pallas_call x1, Pallas kernels, cut(): call(cut_kernel, 1, 3, f32(160, 8, 128), scratch, HBM, 60)  2.37 us
    ppermute x1, waiting for transfers between devices, per_device(): other = lax.ppermute(other, 'gy', others)  2.1 us
  transfers between devices with their start and end apart: 4, of which 2 were waited for; matrix products, arithmetic and copies ran while one was open for 0% of the time, Pallas kernels for 0%

profile of v2, /device:TPU:1, one launch (start us, length us, event | category | flops | bytes accessed | tf_op | source)
XLA Modules:
  0.0 90.2 jit_solution(15922568763205425616)
XLA Ops:
  0.6 2.4 %shard_map.50 = f32[160,8,128]{2,1,0:T(8,128)} custom-call(s32[1]{0:T(128)} %bitcast.1.meta, f32[3,16,1024]{2,1,0:T(8,128)} %init_hbm.1, f32[3,16,1024]{2,1,0:T(8,128)} %bitcast.25, f32[2,16,1024]{2,1,0:T(8,128)} %bitcast.18), custom_call_target="tpu_custom_call" | custom-call | tf_op jit(solution)/shard_map/pallas_call | solution.py:315
  3.0 29.2 %all_to_all.10 = f32[32,40,128]{2,1,0:T(8,128)S(1)} all-to-all(f32[32,40,128]{2,1,0:T(8,128)} %bitcast.23), channel_id=1, replica_groups=mesh['tm'=32,'gy'=16] {'tm'}, dimensions={0} | all-to-all | bytes 1310720 | tf_op jit(solution)/shard_map/all_to_all | solution.py:363
  32.2 6.3 %collective-permute-start.1 = (f32[1280,128]{1,0:T(8,128)S(1)}, f32[1280,128]{1,0:T(8,128)S(1)}, u32[]{:S(2)}, u32[]{:S(2)}) collective-permute-start(f32[1280,128]{1,0:T(8,128)S(1)} %bitcast.13), channel_id=1, source_target_pairs={{1,2},{2,1},{3,4},{4,3},{5,6},{6,5},{7,8},{8,7},{9,10},{10,9},{11,... | collective-permute-start | bytes 1966088 | tf_op jit(solution)/shard_map/ppermute | solution.py:366
  38.6 1.9 %collective-permute-start = (f32[1280,128]{1,0:T(8,128)S(1)}, f32[1280,128]{1,0:T(8,128)S(1)}, u32[]{:S(2)}, u32[]{:S(2)}) collective-permute-start(f32[1280,128]{1,0:T(8,128)S(1)} %bitcast.14), channel_id=1, source_target_pairs={{0,1},{1,0},{2,3},{3,2},{4,5},{5,4},{6,7},{7,6},{8,9},{9,8},{10,11... | collective-permute-start | bytes 1966088 | tf_op jit(solution)/shard_map/ppermute | solution.py:365
  40.5 0.1 pad_add_fusion.meta
  40.6 6.2 %collective-permute-done.1.other = f32[1280,128]{1,0:T(8,128)S(1)} collective-permute-done((f32[1280,128]{1,0:T(8,128)S(1)}, f32[1280,128]{1,0:T(8,128)S(1)}, u32[]{:S(2)}, u32[]{:S(2)}) %collective-permute-start.1) | collective-permute-done | bytes 655392 | tf_op jit(solution)/shard_map/ppermute | solution.py:366
  46.8 0.0 collective-permute-done.mate
  46.8 11.0 %shard_map.51 = f32[768,128]{1,0:T(8,128)S(1)} custom-call(s32[2]{0:T(128)S(1)} %pad_add_fusion.meta, f32[1280,128]{1,0:T(8,128)S(1)} %collective-permute-done.mate, f32[1280,128]{1,0:T(8,128)S(1)} %bitcast.15, f32[1280,128]{1,0:T(8,128)S(1)} %collective-permute-done.1.other), custom_call_target="tpu_custom_call" | custom-call | tf_op jit(solution)/shard_map/pallas_call | solution.py:333
  57.8 0.0 copy-start
  57.8 17.3 %all_to_all.11 = f32[32,24,128]{2,1,0:T(8,128)S(1)} all-to-all(f32[32,24,128]{2,1,0:T(8,128)S(1)} %bitcast.17), channel_id=1, replica_groups=mesh['tm'=32,'gy'=16] {'tm'}, dimensions={0} | all-to-all | bytes 786432 | tf_op jit(solution)/shard_map/all_to_all | solution.py:368
  75.2 0.0 copy-done
  75.2 1.6 %shard_map.52 = (f32[3,16,1024]{2,1,0:T(8,128)}, f32[640,128]{1,0:T(8,128)S(1)}, f32[160,128]{1,0:T(8,128)S(1)}, f32[160,128]{1,0:T(8,128)S(1)}) custom-call(s32[2]{0:T(128)S(1)} %pad_add_fusion.meta, f32[96,8,128]{2,1,0:T(8,128)S(1)} %bitcast.16, f32[2,16,1024]{2,1,0:T(8,128)S(1)} %bitcast.19), custom_call_target="tpu_custom_call" | custom-call | tf_op jit(solution)/shard_map/pallas_call | solution.py:339
  76.7 1.9 %collective-permute-start.2 = (f32[160,128]{1,0:T(8,128)S(1)}, f32[160,128]{1,0:T(8,128)S(1)}, u32[]{:S(2)}, u32[]{:S(2)}) collective-permute-start(f32[160,128]{1,0:T(8,128)S(1)} %get-tuple-element.8), channel_id=1, source_target_pairs={{0,1},{1,0},{2,3},{3,2},{4,5},{5,4},{6,7},{7,6},{8,9},{9,8},{10,11... | collective-permute-start | bytes 245768 | tf_op jit(solution)/shard_map/ppermute | solution.py:370
  78.7 7.4 %collective-permute-start.3 = (f32[160,128]{1,0:T(8,128)S(1)}, f32[160,128]{1,0:T(8,128)S(1)}, u32[]{:S(2)}, u32[]{:S(2)}) collective-permute-start(f32[160,128]{1,0:T(8,128)S(1)} %get-tuple-element.9), channel_id=1, source_target_pairs={{1,2},{2,1},{3,4},{4,3},{5,6},{6,5},{7,8},{8,7},{9,10},{10,9},{11,... | collective-permute-start | bytes 245768 | tf_op jit(solution)/shard_map/ppermute | solution.py:371
  86.1 0.0 collective-permute-done.2
  86.1 2.1 %collective-permute-done.3 = f32[160,128]{1,0:T(8,128)S(1)} collective-permute-done((f32[160,128]{1,0:T(8,128)S(1)}, f32[160,128]{1,0:T(8,128)S(1)}, u32[]{:S(2)}, u32[]{:S(2)}) %collective-permute-start.3) | collective-permute-done | bytes 81952 | tf_op jit(solution)/shard_map/ppermute | solution.py:371
  88.2 2.0 %shard_map.53 = f32[3,16,1024]{2,1,0:T(8,128)} custom-call(s32[2]{0:T(128)S(1)} %pad_add_fusion.meta, f32[80,8,128]{2,1,0:T(8,128)S(1)} %bitcast.20, f32[20,8,128]{2,1,0:T(8,128)S(1)} %bitcast.21, f32[20,8,128]{2,1,0:T(8,128)S(1)} %bitcast.22), custom_call_target="tpu_custom_call" | custom-call | tf_op jit(solution)/shard_map/pallas_call | solution.py:350
Async XLA Ops:
  32.2 14.6 %collective-permute-start.1 = (f32[1280,128]{1,0:T(8,128)S(1)}, f32[1280,128]{1,0:T(8,128)S(1)}, u32[]{:S(2)}, u32[]{:S(2)}) collective-permute-start(f32[1280,128]{1,0:T(8,128)S(1)} %bitcast.13), channel_id=1, source_target_pairs={{1,2},{2,1},{3,4},{4,3},{5,6},{6,5},{7,8},{8,7},{9,10},{10,9},{11,... | collective-permute-start | bytes 1966088 | tf_op jit(solution)/shard_map/ppermute | solution.py:366
  38.6 8.3 %collective-permute-start = (f32[1280,128]{1,0:T(8,128)S(1)}, f32[1280,128]{1,0:T(8,128)S(1)}, u32[]{:S(2)}, u32[]{:S(2)}) collective-permute-start(f32[1280,128]{1,0:T(8,128)S(1)} %bitcast.14), channel_id=1, source_target_pairs={{0,1},{1,0},{2,3},{3,2},{4,5},{5,4},{6,7},{7,6},{8,9},{9,8},{10,11... | collective-permute-start | bytes 1966088 | tf_op jit(solution)/shard_map/ppermute | solution.py:365
  57.8 17.3 %copy-start = (f32[1,2,16,1024]{3,2,1,0:T(8,128)S(1)}, f32[1,2,16,1024]{3,2,1,0:T(8,128)}, u32[]{:S(2)}) copy-start(f32[1,2,16,1024]{3,2,1,0:T(8,128)} %param.5) | copy-start | bytes 393220
  76.7 9.4 %collective-permute-start.2 = (f32[160,128]{1,0:T(8,128)S(1)}, f32[160,128]{1,0:T(8,128)S(1)}, u32[]{:S(2)}, u32[]{:S(2)}) collective-permute-start(f32[160,128]{1,0:T(8,128)S(1)} %get-tuple-element.8), channel_id=1, source_target_pairs={{0,1},{1,0},{2,3},{3,2},{4,5},{5,4},{6,7},{7,6},{8,9},{9,8},{10,11... | collective-permute-start | bytes 245768 | tf_op jit(solution)/shard_map/ppermute | solution.py:370
  78.7 9.6 %collective-permute-start.3 = (f32[160,128]{1,0:T(8,128)S(1)}, f32[160,128]{1,0:T(8,128)S(1)}, u32[]{:S(2)}, u32[]{:S(2)}) collective-permute-start(f32[160,128]{1,0:T(8,128)S(1)} %get-tuple-element.9), channel_id=1, source_target_pairs={{1,2},{2,1},{3,4},{4,3},{5,6},{6,5},{7,8},{8,7},{9,10},{10,9},{11,... | collective-permute-start | bytes 245768 | tf_op jit(solution)/shard_map/ppermute | solution.py:371

commit v3 on v2

v3 whole, which is shorter than its diff:
```python
import jax
import jax.numpy as jnp
from jax import lax
from jax.experimental import pallas as pl
from jax.experimental.pallas import tpu as pltpu
from jax.sharding import PartitionSpec as P

FINE = 4
GROUP = 4
GROUPS = 8
HALO = 16
TILE = 32
ROWS = 16
HALF = 64
BAND = 24

diffusion = (0.05, 0.15, 0.4)
kappa_coupling = 0.1
time_step = 0.0125
coarsest = FINE * GROUP * time_step

VMEM = pl.BlockSpec(memory_space=pltpu.VMEM)
HBM = pl.BlockSpec(memory_space=pltpu.HBM)
SMEM = pl.BlockSpec(memory_space=pltpu.SMEM)


def lanes():
    return lax.broadcasted_iota(jnp.int32, (8, 128), 1)


def sublanes():
    return lax.broadcasted_iota(jnp.int32, (8, 128), 0)


def swap8(values):
    sub = sublanes()
    for s in (4, 2, 1):
        keep = sub % (2 * s) < s
        new = list(values)
        for p in range(8):
            if p % (2 * s) < s:
                a, b = values[p], values[p + s]
                new[p] = jnp.where(keep, a, pltpu.roll(b, s, 0))
                new[p + s] = jnp.where(keep, pltpu.roll(a, 8 - s, 0), b)
        values = new
    return values


def slope(west, east, below, above, across, along, scale=1.0):
    right, upward = across > 0.0, along > 0.0
    out = []
    for c in range(3):
        spread = (east[c] - west[c]) + (above[c] - below[c])
        transport = across * jnp.where(right, west[c], east[c]) + along * jnp.where(upward, below[c], above[c])
        out.append((scale * time_step * diffusion[c]) * spread - transport)
    return out


def cut_kernel(meta, init_hbm, ends_hbm, vel_hbm, out, flow, init, ends, vel, sems):
    copies = [
        pltpu.make_async_copy(far, near, sems.at[i])
        for i, (far, near) in enumerate(((init_hbm, init), (ends_hbm, ends), (vel_hbm, vel)))
    ]
    for copy in copies:
        copy.start()
    for copy in copies:
        copy.wait()
    last = meta[0] == GROUP * GROUPS - 1
    low = lanes() < HALF
    for a in range(5):
        if a < 3:
            top = jnp.where(last, init[a, 0:8, :], ends[a, 0:8, :])
            bottom = jnp.where(last, init[a, 8:16, :], ends[a, 8:16, :])
        else:
            top, bottom = vel[a - 3, 0:8, :], vel[a - 3, 8:16, :]
        for q in range(4):
            upper = pltpu.roll(top, (HALO - TILE * q) % 1024, 1)
            lower = pltpu.roll(bottom, (HALO + HALF - TILE * q) % 1024, 1)
            for b in range(8):
                at = slice(128 * b, 128 * b + 128)
                out[(4 * b + q) * 5 + a] = jnp.where(low, upper[:, at], lower[:, at])
    for c in range(2):
        for y0 in (0, 8):
            blocks = [vel[c, y0 : y0 + 8, 128 * b : 128 * b + 128] for b in range(8)]
            for y, value in enumerate(swap8(blocks)):
                flow[c * ROWS + y0 + y] = value


def cycle_kernel(meta, mate, cur, other, out, ua, ub, vv, src, gg, ff, init, xa, xb, yy, cc):
    lane, sub = lanes(), sublanes()
    low = lane < HALF
    sign = jnp.where(low, 1.0, -1.0)
    kappa = time_step * kappa_coupling
    swing = kappa * sign
    even = meta[0] % 2 == 0
    outside = jnp.where(low, meta[0], meta[1] - 1 - meta[0]) == 0

    def step(buf, base, k, start, emit, scale=1.0):
        pl.when(meta[1] > 0)(lambda: sweep(buf, base, k, start, emit, scale))

    def sweep(buf, base, k, start, emit, scale):
        rows, climbs = {}, {}

        def row(r):
            if r not in rows:
                rows[r] = [buf[base + c, r] for c in range(3)]
            return rows[r]

        def climb(r):
            if r not in climbs:
                climbs[r] = [x - y for x, y in zip(row(r + 1), row(r))]
            return climbs[r]

        for r in range(start, BAND):
            u = row(r)
            west = [x - pltpu.roll(x, 1, 1) for x in u]
            east = [pltpu.roll(x, 127, 1) - x for x in u]
            across = vv[2 * k, r] + (scale * kappa) * u[0]
            along = vv[2 * k + 1, r] + (scale * swing) * u[1]
            emit(r, u, slope(west, east, climb(r - 1), climb(r), across, along, scale))

    def put(buf, at, r, value):
        if r == HALO - 1:
            value = jnp.where(outside, 0.0, value)
        buf[at, r] = value
        if r == BAND - 1:
            buf[at, BAND] = pltpu.roll(value, HALF, 1)

    for k in range(GROUP):
        for a in range(5):
            at = [(4 * j + k) * 5 + a for j in range(8)]
            own = swap8([cur[i] for i in at])
            before = swap8([jnp.where(even, other[i], mate[i]) for i in at])
            after = swap8([jnp.where(even, mate[i], other[i]) for i in at])
            for y in range(8):
                rows = (
                    (y, jnp.where(low, before[y], after[7 - y])),
                    (y + 8, pltpu.roll(jnp.where(low, after[7 - y], before[y]), HALF, 1)),
                    (y + 16, jnp.where(low, own[y], own[7 - y])),
                )
                for r, value in rows:
                    if a == 3:
                        vv[2 * k, r] = time_step * value
                        if k == GROUP - 1:
                            vv[2 * GROUP, r] = coarsest * value
                    elif a == 4:
                        vv[2 * k + 1, r] = (time_step * sign) * value
                        if k == GROUP - 1:
                            vv[2 * GROUP + 1, r] = (coarsest * sign) * value
                    elif k == GROUP - 1:
                        value = pltpu.roll(value, 1, 0)
                        put(ua, a, r, value)
                        put(xa, a, r, value)
                        xb[a, r] = value
                        init[a, r] = value
                    else:
                        put(ua, 3 * (k + 1) + a, r, value)

    def keep_g(r, u, s):
        for c in range(3):
            gg[c, r] = u[c] + s[c]

    step(ua, 0, GROUP, 7, keep_g, float(FINE * GROUP))

    def fine(k, carry):
        base = 3 * k

        def opening(r, u, s):
            for c in range(3):
                put(ub, base + c, r, u[c] + s[c])
                src[base + c, r] = u[c] + float(FINE) * s[c]

        def onward(buf):
            def emit(r, u, s):
                for c in range(3):
                    put(buf, base + c, r, u[c] + s[c])

            return emit

        def closing(r, u, s):
            for c in range(3):
                end = u[c] + s[c]
                put(ua, base + c, r, end)
                src[base + c, r] = end - src[base + c, r]

        step(ua, base, k, 1, opening)
        step(ub, base, k, 2, onward(ua))
        step(ua, base, k, 3, onward(ub))
        step(ub, base, k, 4, closing)
        return carry

    lax.fori_loop(0, GROUP, fine, 0)

    def plus(buf, k, base):
        def emit(r, u, s):
            for c in range(3):
                put(buf, base + c, r, u[c] + float(FINE) * s[c] + src[3 * k + c, r])

        return emit

    step(ua, 0, 1, 5, plus(ub, 1, 0))
    step(ub, 0, 2, 6, plus(ua, 2, 0))

    def forcing(r, u, s):
        for c in range(3):
            ff[c, r] = u[c] + float(FINE) * s[c] + src[3 * (GROUP - 1) + c, r] - gg[c, r]

    step(ua, 0, GROUP - 1, 7, forcing)

    for t in range(GROUPS):
        buf, to = (xa, xb) if t % 2 == 0 else (xb, xa)

        def settle(r, u, s):
            for c in range(3):
                y = u[c] + s[c] + ff[c, r]
                if t == GROUPS - 1 and r >= HALO:
                    yy[c, r] = y
                put(to, c, r, jnp.where(sub == 0, init[c, r], pltpu.roll(y, 1, 0)))

        step(buf, 0, GROUP, max(7, 6 + t), settle, float(FINE * GROUP))

    step(xa, 0, 0, 14, plus(cc, 0, 0))
    step(cc, 0, 1, 15, plus(cc, 1, 3))
    step(cc, 3, 2, 16, plus(cc, 2, 6))

    def compact(buf, base, c, y):
        m = jnp.where(low, buf[base + c, y + 16], buf[base + c, 23 - y])
        return jnp.where(lane < TILE, pltpu.roll(m, 128 - HALO, 1), pltpu.roll(m, 128 - HALO - TILE, 1))

    reads = [(xa, 0), (cc, 0), (cc, 3), (cc, 6), (yy, 0)]
    for c in range(3):
        before = [compact(*reads[0], c, y) for y in range(8)]
        for k in range(GROUP):
            own = [compact(*reads[k + 1], c, y) for y in range(8)]
            values = [jnp.where(low, x, pltpu.roll(y, HALF, 1)) for x, y in zip(own, before)]
            for j, value in enumerate(swap8(values)):
                out[(4 * j + k) * 3 + c] = value
            before = own


def gathered(tiles, c, b, part):
    group = lanes() // TILE
    value = None
    for q in range(4):
        shift = (TILE * (q - part)) % 128
        x = tiles[(4 * b + q) * 3 + c]
        x = pltpu.roll(x, shift, 1) if shift else x
        value = x if value is None else jnp.where(group == q, x, value)
    return value


def begin_kernel(meta, tiles, flow, begin, mate, other):
    even = meta[0] % 2 == 0
    for c in range(5):
        if c < 3:
            rows = []
            for part in (2, 3):
                rows += swap8([gathered(tiles, c, b, part) for b in range(8)])
            for y in range(ROWS):
                begin[c * ROWS + y] = rows[y]
        else:
            rows = [flow[(c - 3) * ROWS + y] for y in range(ROWS)]
        for y in range(FINE):
            down, up = rows[y], rows[ROWS - FINE + y]
            mate[c * FINE + y] = jnp.where(even, up, down)
            other[c * FINE + y] = jnp.where(even, down, up)


def own_kernel(tiles, own):
    for c in range(3):
        for b in range(8):
            at = slice(128 * b, 128 * b + 128)
            own[c, 0:8, at] = gathered(tiles, c, b, 0)
            own[c, 8:16, at] = gathered(tiles, c, b, 1)


def relax_kernel(meta, mid, flow, mate, other, out, wa, wb, vv):
    lane = lanes()
    tall = ROWS + 2 * FINE
    kappa = time_step * kappa_coupling
    even = meta[0] % 2 == 0
    for a in range(5):
        src, buf, at = (mid, wa, a) if a < 3 else (flow, vv, a - 3)
        scale = 1.0 if a < 3 else time_step
        for r in range(FINE):
            m, o = mate[a * FINE + r], other[a * FINE + r]
            buf[at * tall + r] = scale * jnp.where(even, o, m)
            buf[at * tall + FINE + ROWS + r] = scale * jnp.where(even, m, o)
        for r in range(ROWS):
            buf[at * tall + FINE + r] = scale * src[at * ROWS + r]

    bottom, top = meta[0] == 0, meta[0] == meta[1] - 1
    def sweep(section, buf, to):
        rows = {r: [buf[c * tall + r] for c in range(3)] for r in range(section, tall - section)}
        climbs = {r: [x - y for x, y in zip(rows[r + 1], rows[r])] for r in range(section, tall - section - 1)}
        ends = []
        for r in range(section + 1, tall - section - 1):
            u = rows[r]
            west, east = [], []
            for x in u:
                y = pltpu.roll(x, 1, 1)
                west.append(x - jnp.where(lane == 0, pltpu.roll(y, 1, 0), y))
                y = pltpu.roll(x, 127, 1)
                east.append(jnp.where(lane == 127, pltpu.roll(y, 7, 0), y) - x)
            across = vv[r] + kappa * u[0]
            along = vv[tall + r] + kappa * u[1]
            s = slope(west, east, climbs[r - 1], climbs[r], across, along)
            new = [x + y for x, y in zip(u, s)]
            ends.append(new)
            for c in range(3):
                if r == FINE - 1:
                    new[c] = jnp.where(bottom, 0.0, new[c])
                elif r == FINE + ROWS:
                    new[c] = jnp.where(top, 0.0, new[c])
                if section < FINE - 1:
                    to[c * tall + r] = new[c]
        if section == FINE - 1:
            for y0 in (0, 8):
                for c in range(3):
                    for b, value in enumerate(swap8([ends[y0 + y][c] for y in range(8)])):
                        out[c, y0 : y0 + 8, 128 * b : 128 * b + 128] = value

    for section in range(FINE):
        buf, to = (wa, wb) if section % 2 == 0 else (wb, wa)
        sweep(section, buf, to)


def f32(*shape):
    return jax.ShapeDtypeStruct(shape, jnp.float32)


def buffer(*shape):
    return pltpu.VMEM(shape, jnp.float32)


def call(kernel, n_scalars, n_arrays, outs, scratch=(), space=VMEM, mib=24):
    many = isinstance(outs, tuple)
    return pl.pallas_call(
        kernel,
        out_shape=outs,
        in_specs=[SMEM] * n_scalars + [space] * n_arrays,
        out_specs=(VMEM,) * len(outs) if many else VMEM,
        scratch_shapes=list(scratch),
        compiler_params=pltpu.CompilerParams(vmem_limit_bytes=mib * 1024 * 1024),
    )


def cut(meta, init, ends, vel):
    state, flow = buffer(3, ROWS, 1024), buffer(2, ROWS, 1024)
    scratch = [state, state, flow, pltpu.SemaphoreType.DMA((3,))]
    outs = (f32(160, 8, 128), f32(2 * ROWS, 8, 128))
    return call(cut_kernel, 1, 3, outs, scratch, HBM, 60)(meta, init, ends, vel)


def cycle(meta, mate, cur, other):
    tall = BAND + 1
    scratch = [
        buffer(12, tall, 8, 128),
        buffer(12, tall, 8, 128),
        buffer(10, BAND, 8, 128),
        buffer(12, BAND, 8, 128),
        buffer(3, BAND, 8, 128),
        buffer(3, BAND, 8, 128),
        buffer(3, tall, 8, 128),
        buffer(3, tall, 8, 128),
        buffer(3, tall, 8, 128),
        buffer(3, BAND, 8, 128),
        buffer(9, tall, 8, 128),
    ]
    return call(cycle_kernel, 1, 3, f32(96, 8, 128), scratch)(meta, mate, cur, other)


def begins(meta, tiles, flow):
    halo = f32(5 * FINE, 8, 128)
    return call(begin_kernel, 1, 2, (f32(3 * ROWS, 8, 128), halo, halo))(meta, tiles, flow)


def owns(tiles):
    return call(own_kernel, 0, 1, f32(3, ROWS, 1024))(tiles)


def relax(meta, mid, flow, mate, other):
    tall = ROWS + 2 * FINE
    scratch = [buffer(3 * tall, 8, 128), buffer(3 * tall, 8, 128), buffer(2 * tall, 8, 128)]
    return call(relax_kernel, 1, 4, f32(3, ROWS, 1024), scratch)(meta, mid, flow, mate, other)


def per_device(initial_state, guessed_ends, velocity):
    slabs = lax.axis_size("gy")
    mates = [(i, i ^ 1) for i in range(slabs)]
    others = [(i, i + 1 if i % 2 else i - 1) for i in range(1, slabs - 1)]
    intervals = lax.axis_size("tm")
    here = lax.axis_index("tm").astype(jnp.int32).reshape(1)
    slab = jnp.stack([lax.axis_index("gy").astype(jnp.int32), jnp.int32(slabs)])

    windows, flow = cut(here, initial_state, guessed_ends[0], velocity[0])
    cur = lax.all_to_all(windows.reshape(intervals, 40, 128), "tm", 0, 0)
    cur = cur.reshape(intervals * 5, 8, 128)
    mate = lax.ppermute(cur, "gy", mates)
    other = lax.ppermute(cur, "gy", others)
    tiles = cycle(slab, mate, cur, other)
    tiles = lax.all_to_all(tiles.reshape(intervals, 24, 128), "tm", 0, 0)
    tiles = tiles.reshape(intervals * 3, 8, 128)
    mid, mate, other = begins(slab, tiles, flow)
    mate = lax.ppermute(mate, "gy", mates)
    other = lax.ppermute(other, "gy", others)
    own = owns(tiles)
    relaxed = relax(slab, mid, flow, mate, other)
    return own[None], relaxed[None]


def solution(mesh):
    placed = (P(None, "gy", None), P("tm", None, "gy", None), P("tm", None, "gy", None))
    return jax.shard_map(
        per_device,
        mesh=mesh,
        in_specs=placed,
        out_specs=(P("tm", None, "gy", None), P("tm", None, "gy", None)),
        check_vma=False,
    )
```

time: 90.6 us -> 86.6 us (0.956)
  Pallas kernels: 16.9 us -> 13.9 us
    pallas_call x4 -> x5, Pallas kernels: 16.9 us -> 13.9 us  [the longest x1 7.92 us: cycle(): call(cycle_kernel, 1, 3, f32(96, 8, 128), scratch)(meta, mate, cur, other)]
  transfers between devices with their start and end apart: 4 -> 4, of which waited for: 2 -> 2; matrix products, arithmetic and copies ran while one was open for 0% -> 0% of each run, Pallas kernels for 0% -> 1%
where the time goes in v3:
time: 86.6 us; the launch traced here: 86.3 us
  blocking collectives  46.5 us (54%)
  starting transfers between devices  17.6 us (20%)
  Pallas kernels  13.9 us (16%)
  waiting for transfers between devices  7.46 us (9%)
    all_to_all x1, blocking collectives, per_device(): cur = lax.all_to_all(windows.reshape(intervals, 40, 128), 'tm', 0, 0)  29.2 us
    all_to_all x1, blocking collectives, per_device(): tiles = lax.all_to_all(tiles.reshape(intervals, 24, 128), 'tm', 0, 0)  17.3 us
    pallas_call x1, Pallas kernels, cycle(): call(cycle_kernel, 1, 3, f32(96, 8, 128), scratch)(meta, mate, cur, other)  7.92 us
    ppermute x1, starting transfers between devices, per_device(): other = lax.ppermute(other, 'gy', others)  7.45 us
    ppermute x1, starting transfers between devices, per_device(): other = lax.ppermute(cur, 'gy', others)  6.33 us
    ppermute x1, waiting for transfers between devices, per_device(): other = lax.ppermute(cur, 'gy', others)  6.25 us
    pallas_call x1, Pallas kernels, cut(): return call(cut_kernel, 1, 3, outs, scratch, HBM, 60)(meta, init, ends, vel)  2.37 us
    pallas_call x1, Pallas kernels, relax(): call(relax_kernel, 1, 4, f32(3, ROWS, 1024), scratch)  1.95 us
  transfers between devices with their start and end apart: 4, of which 2 were waited for; matrix products, arithmetic and copies ran while one was open for 0% of the time, Pallas kernels for 1%

profile of v3, /device:TPU:1, one launch (start us, length us, event | category | flops | bytes accessed | tf_op | source)
XLA Modules:
  0.0 86.3 jit_solution(12084487027956026752)
XLA Ops:
  0.6 2.4 %shard_map.50 = (f32[160,8,128]{2,1,0:T(8,128)}, f32[32,8,128]{2,1,0:T(8,128)}) custom-call(s32[1]{0:T(128)} %bitcast.1.meta, f32[3,16,1024]{2,1,0:T(8,128)} %init_hbm.1, f32[3,16,1024]{2,1,0:T(8,128)} %bitcast.17, f32[2,16,1024]{2,1,0:T(8,128)} %bitcast.20), custom_call_target="tpu_custom_call" | custom-call | tf_op jit(solution)/shard_map/pallas_call | solution.py:352
  3.0 29.2 %all_to_all.10 = f32[32,40,128]{2,1,0:T(8,128)S(1)} all-to-all(f32[32,40,128]{2,1,0:T(8,128)} %bitcast.16), channel_id=1, replica_groups=mesh['tm'=32,'gy'=16] {'tm'}, dimensions={0} | all-to-all | bytes 1310720 | tf_op jit(solution)/shard_map/all_to_all | solution.py:397
  32.2 6.3 %collective-permute-start.1 = (f32[160,8,128]{2,1,0:T(8,128)S(1)}, f32[160,8,128]{2,1,0:T(8,128)S(1)}, u32[]{:S(2)}, u32[]{:S(2)}) collective-permute-start(f32[160,8,128]{2,1,0:T(8,128)S(1)} %bitcast.12), channel_id=1, source_target_pairs={{1,2},{2,1},{3,4},{4,3},{5,6},{6,5},{7,8},{8,7},{9,10},{10,9},{11,... | collective-permute-start | bytes 1966088 | tf_op jit(solution)/shard_map/ppermute | solution.py:400
  38.6 1.9 %collective-permute-start = (f32[160,8,128]{2,1,0:T(8,128)S(1)}, f32[160,8,128]{2,1,0:T(8,128)S(1)}, u32[]{:S(2)}, u32[]{:S(2)}) collective-permute-start(f32[160,8,128]{2,1,0:T(8,128)S(1)} %bitcast.13), channel_id=1, source_target_pairs={{0,1},{1,0},{2,3},{3,2},{4,5},{5,4},{6,7},{7,6},{8,9},{9,8},{10,11... | collective-permute-start | bytes 1966088 | tf_op jit(solution)/shard_map/ppermute | solution.py:399
  40.5 0.1 pad_add_fusion.meta
  40.6 6.2 %collective-permute-done.1.other = f32[160,8,128]{2,1,0:T(8,128)S(1)} collective-permute-done((f32[160,8,128]{2,1,0:T(8,128)S(1)}, f32[160,8,128]{2,1,0:T(8,128)S(1)}, u32[]{:S(2)}, u32[]{:S(2)}) %collective-permute-start.1) | collective-permute-done | bytes 655392 | tf_op jit(solution)/shard_map/ppermute | solution.py:400
  46.8 0.0 collective-permute-done.mate
  46.8 7.9 %shard_map.51 = f32[96,8,128]{2,1,0:T(8,128)S(1)} custom-call(s32[2]{0:T(128)S(1)} %pad_add_fusion.meta, f32[160,8,128]{2,1,0:T(8,128)S(1)} %collective-permute-done.mate, f32[160,8,128]{2,1,0:T(8,128)S(1)} %bitcast.14, f32[160,8,128]{2,1,0:T(8,128)S(1)} %collective-permute-done.1.other), custom_call_target="tpu_custom_call" | custom-call | tf_op jit(solution)/shard_map/pallas_call | solution.py:370
  54.7 0.0 copy-start
  54.8 17.3 %all_to_all.11 = f32[32,24,128]{2,1,0:T(8,128)S(1)} all-to-all(f32[32,24,128]{2,1,0:T(8,128)S(1)} %bitcast.15), channel_id=1, replica_groups=mesh['tm'=32,'gy'=16] {'tm'}, dimensions={0} | all-to-all | bytes 786432 | tf_op jit(solution)/shard_map/all_to_all | solution.py:402
  72.1 0.0 copy-done
  72.1 0.8 shard_map.53
  72.9 1.9 %collective-permute-start.2 = (f32[20,8,128]{2,1,0:T(8,128)S(1)}, f32[20,8,128]{2,1,0:T(8,128)S(1)}, u32[]{:S(2)}, u32[]{:S(2)}) collective-permute-start(f32[20,8,128]{2,1,0:T(8,128)S(1)} %get-tuple-element.10), channel_id=1, source_target_pairs={{0,1},{1,0},{2,3},{3,2},{4,5},{5,4},{6,7},{7,6},{8,9},{9,8},{10,11... | collective-permute-start | bytes 245768 | tf_op jit(solution)/shard_map/ppermute | solution.py:405
  74.8 7.5 %collective-permute-start.3 = (f32[20,8,128]{2,1,0:T(8,128)S(1)}, f32[20,8,128]{2,1,0:T(8,128)S(1)}, u32[]{:S(2)}, u32[]{:S(2)}) collective-permute-start(f32[20,8,128]{2,1,0:T(8,128)S(1)} %get-tuple-element.11), channel_id=1, source_target_pairs={{1,2},{2,1},{3,4},{4,3},{5,6},{6,5},{7,8},{8,7},{9,10},{10,9},{11,... | collective-permute-start | bytes 245768 | tf_op jit(solution)/shard_map/ppermute | solution.py:406
  82.2 0.9 %shard_map.52 = f32[3,16,1024]{2,1,0:T(8,128)} custom-call(f32[96,8,128]{2,1,0:T(8,128)S(1)} %bitcast.11), custom_call_target="tpu_custom_call" | custom-call | tf_op jit(solution)/shard_map/pallas_call | solution.py:379
  83.1 0.0 collective-permute-done.2.mate
  83.1 1.2 %collective-permute-done.3.other = f32[20,8,128]{2,1,0:T(8,128)S(1)} collective-permute-done((f32[20,8,128]{2,1,0:T(8,128)S(1)}, f32[20,8,128]{2,1,0:T(8,128)S(1)}, u32[]{:S(2)}, u32[]{:S(2)}) %collective-permute-start.3) | collective-permute-done | bytes 81952 | tf_op jit(solution)/shard_map/ppermute | solution.py:406
  84.4 1.9 %shard_map.54 = f32[3,16,1024]{2,1,0:T(8,128)} custom-call(s32[2]{0:T(128)S(1)} %pad_add_fusion.meta, f32[48,8,128]{2,1,0:T(8,128)S(1)} %get-tuple-element.9.mid, f32[32,8,128]{2,1,0:T(8,128)S(1)} %copy-done, f32[20,8,128]{2,1,0:T(8,128)S(1)} %collective-permute-done.2.mate, f32[20,8,128]{2,1,0:T(8,128)S(1)} %collective-permute-done.3.other), custom_call_target="tpu_custom_call" | custom-call | tf_op jit(solution)/shard_map/pallas_call | solution.py:385
Async XLA Ops:
  32.2 14.6 %collective-permute-start.1 = (f32[160,8,128]{2,1,0:T(8,128)S(1)}, f32[160,8,128]{2,1,0:T(8,128)S(1)}, u32[]{:S(2)}, u32[]{:S(2)}) collective-permute-start(f32[160,8,128]{2,1,0:T(8,128)S(1)} %bitcast.12), channel_id=1, source_target_pairs={{1,2},{2,1},{3,4},{4,3},{5,6},{6,5},{7,8},{8,7},{9,10},{10,9},{11,... | collective-permute-start | bytes 1966088 | tf_op jit(solution)/shard_map/ppermute | solution.py:400
  38.6 8.3 %collective-permute-start = (f32[160,8,128]{2,1,0:T(8,128)S(1)}, f32[160,8,128]{2,1,0:T(8,128)S(1)}, u32[]{:S(2)}, u32[]{:S(2)}) collective-permute-start(f32[160,8,128]{2,1,0:T(8,128)S(1)} %bitcast.13), channel_id=1, source_target_pairs={{0,1},{1,0},{2,3},{3,2},{4,5},{5,4},{6,7},{7,6},{8,9},{9,8},{10,11... | collective-permute-start | bytes 1966088 | tf_op jit(solution)/shard_map/ppermute | solution.py:399
  54.7 17.3 %copy-start = (f32[32,8,128]{2,1,0:T(8,128)S(1)}, f32[32,8,128]{2,1,0:T(8,128)}, u32[]{:S(2)}) copy-start(f32[32,8,128]{2,1,0:T(8,128)} %get-tuple-element.8.flow) | copy-start | bytes 393220
  72.9 10.3 %collective-permute-start.2 = (f32[20,8,128]{2,1,0:T(8,128)S(1)}, f32[20,8,128]{2,1,0:T(8,128)S(1)}, u32[]{:S(2)}, u32[]{:S(2)}) collective-permute-start(f32[20,8,128]{2,1,0:T(8,128)S(1)} %get-tuple-element.10), channel_id=1, source_target_pairs={{0,1},{1,0},{2,3},{3,2},{4,5},{5,4},{6,7},{7,6},{8,9},{9,8},{10,11... | collective-permute-start | bytes 245768 | tf_op jit(solution)/shard_map/ppermute | solution.py:405
  74.8 9.6 %collective-permute-start.3 = (f32[20,8,128]{2,1,0:T(8,128)S(1)}, f32[20,8,128]{2,1,0:T(8,128)S(1)}, u32[]{:S(2)}, u32[]{:S(2)}) collective-permute-start(f32[20,8,128]{2,1,0:T(8,128)S(1)} %get-tuple-element.11), channel_id=1, source_target_pairs={{1,2},{2,1},{3,4},{4,3},{5,6},{6,5},{7,8},{8,7},{9,10},{10,9},{11,... | collective-permute-start | bytes 245768 | tf_op jit(solution)/shard_map/ppermute | solution.py:406

commit v4 on v3

--- a/solution.py
+++ b/solution.py
@@ -1,3 +1,5 @@
+import functools
+
 import jax
 import jax.numpy as jnp
 from jax import lax
@@ -86,39 +88,29 @@
                 flow[c * ROWS + y0 + y] = value
 
 
-def cycle_kernel(meta, mate, cur, other, out, ua, ub, vv, src, gg, ff, init, xa, xb, yy, cc):
-    lane, sub = lanes(), sublanes()
-    low = lane < HALF
+def sort_kernel(cur, both, one, two):
+    for k in range(GROUP):
+        for a in range(5):
+            values = swap8([cur[(4 * j + k) * 5 + a] for j in range(8)])
+            to = k
+            if a < 3:
+                to = (k + 1) % GROUP
+                if to == 0:
+                    values = [pltpu.roll(value, 1, 0) for value in values]
+            half = one if to < 2 else two
+            for y in range(8):
+                half[(to % 2 * 5 + a) * 8 + y] = values[y]
+                both[(to * 5 + a) * 8 + y] = values[y]
+
+
+def masks(meta):
+    low = lanes() < HALF
     sign = jnp.where(low, 1.0, -1.0)
-    kappa = time_step * kappa_coupling
-    swing = kappa * sign
-    even = meta[0] % 2 == 0
     outside = jnp.where(low, meta[0], meta[1] - 1 - meta[0]) == 0
-
-    def step(buf, base, k, start, emit, scale=1.0):
-        pl.when(meta[1] > 0)(lambda: sweep(buf, base, k, start, emit, scale))
-
-    def sweep(buf, base, k, start, emit, scale):
-        rows, climbs = {}, {}
-
-        def row(r):
-            if r not in rows:
-                rows[r] = [buf[base + c, r] for c in range(3)]
-            return rows[r]
-
-        def climb(r):
-            if r not in climbs:
-                climbs[r] = [x - y for x, y in zip(row(r + 1), row(r))]
-            return climbs[r]
-
-        for r in range(start, BAND):
-            u = row(r)
-            west = [x - pltpu.roll(x, 1, 1) for x in u]
-            east = [pltpu.roll(x, 127, 1) - x for x in u]
-            across = vv[2 * k, r] + (scale * kappa) * u[0]
-            along = vv[2 * k + 1, r] + (scale * swing) * u[1]
-            emit(r, u, slope(west, east, climb(r - 1), climb(r), across, along, scale))
-
+    return low, sign, outside
+
+
+def putter(outside):
     def put(buf, at, r, value):
         if r == HALO - 1:
             value = jnp.where(outside, 0.0, value)
@@ -126,41 +118,69 @@
         if r == BAND - 1:
             buf[at, BAND] = pltpu.roll(value, HALF, 1)
 
-    for k in range(GROUP):
+    return put
+
+
+def stepper(meta, sign):
+    kappa = time_step * kappa_coupling
+    swing = kappa * sign
+
+    def sweep(buf, base, flow, at, start, emit, scale):
+        rows, climbs = {}, {}
+
+        def row(r):
+            if r not in rows:
+                rows[r] = [buf[base + c, r] for c in range(3)]
+            return rows[r]
+
+        def climb(r):
+            if r not in climbs:
+                climbs[r] = [x - y for x, y in zip(row(r + 1), row(r))]
+            return climbs[r]
+
+        for r in range(start, BAND):
+            u = row(r)
+            west = [x - pltpu.roll(x, 1, 1) for x in u]
+            east = [pltpu.roll(x, 127, 1) - x for x in u]
+            across = flow[at, r] + (scale * kappa) * u[0]
+            along = flow[at + 1, r] + (scale * swing) * u[1]
+            emit(r, u, slope(west, east, climb(r - 1), climb(r), across, along, scale))
+
+    def step(buf, base, flow, at, start, emit, scale=1.0):
+        pl.when(meta[1] > 0)(lambda: sweep(buf, base, flow, at, start, emit, scale))
+
+    return step
+
+
+def fine_kernel(pair, meta, own, mate, other, vv, src, ua, *more):
+    ub = more[-1]
+    low, sign, outside = masks(meta)
+    put, step = putter(outside), stepper(meta, sign)
+    even = meta[0] % 2 == 0
+    for k in range(2):
         for a in range(5):
-            at = [(4 * j + k) * 5 + a for j in range(8)]
-            own = swap8([cur[i] for i in at])
-            before = swap8([jnp.where(even, other[i], mate[i]) for i in at])
-            after = swap8([jnp.where(even, mate[i], other[i]) for i in at])
+            at = (k * 5 + a) * 8
+            mine = [own[at + y] for y in range(8)]
+            m = [mate[pair * 80 + at + y] for y in range(8)]
+            o = [other[at + y] for y in range(8)]
+            before = [jnp.where(even, x, y) for x, y in zip(o, m)]
+            after = [jnp.where(even, y, x) for x, y in zip(o, m)]
             for y in range(8):
                 rows = (
                     (y, jnp.where(low, before[y], after[7 - y])),
                     (y + 8, pltpu.roll(jnp.where(low, after[7 - y], before[y]), HALF, 1)),
-                    (y + 16, jnp.where(low, own[y], own[7 - y])),
+                    (y + 16, jnp.where(low, mine[y], mine[7 - y])),
                 )
                 for r, value in rows:
-                    if a == 3:
-                        vv[2 * k, r] = time_step * value
-                        if k == GROUP - 1:
-                            vv[2 * GROUP, r] = coarsest * value
-                    elif a == 4:
-                        vv[2 * k + 1, r] = (time_step * sign) * value
-                        if k == GROUP - 1:
-                            vv[2 * GROUP + 1, r] = (coarsest * sign) * value
-                    elif k == GROUP - 1:
-                        value = pltpu.roll(value, 1, 0)
-                        put(ua, a, r, value)
-                        put(xa, a, r, value)
-                        xb[a, r] = value
-                        init[a, r] = value
-                    else:
-                        put(ua, 3 * (k + 1) + a, r, value)
-
-    def keep_g(r, u, s):
-        for c in range(3):
-            gg[c, r] = u[c] + s[c]
-
-    step(ua, 0, GROUP, 7, keep_g, float(FINE * GROUP))
+                    if a < 3:
+                        put(ua, 3 * k + a, r, value)
+                        if pair == 0 and k == 0:
+                            put(more[0], a, r, value)
+                        continue
+                    way = 1.0 if a == 3 else sign
+                    vv[2 * k + a - 3, r] = (time_step * way) * value
+                    if pair == 1 and k == 1:
+                        vv[4 + a - 3, r] = (coarsest * way) * value
 
     def fine(k, carry):
         base = 3 * k
@@ -183,45 +203,64 @@
                 put(ua, base + c, r, end)
                 src[base + c, r] = end - src[base + c, r]
 
-        step(ua, base, k, 1, opening)
-        step(ub, base, k, 2, onward(ua))
-        step(ua, base, k, 3, onward(ub))
-        step(ub, base, k, 4, closing)
+        step(ua, base, vv, 2 * k, 1, opening)
+        step(ub, base, vv, 2 * k, 2, onward(ua))
+        step(ua, base, vv, 2 * k, 3, onward(ub))
+        step(ub, base, vv, 2 * k, 4, closing)
         return carry
 
-    lax.fori_loop(0, GROUP, fine, 0)
+    lax.fori_loop(0, 2, fine, 0)
+
+
+def coarse_kernel(meta, ends, vv0, src0, begin, vv1, src1, out, ua, ub, gg, ff, xa, xb, yy, cc):
+    lane, sub = lanes(), sublanes()
+    low, sign, outside = masks(meta)
+    put, step = putter(outside), stepper(meta, sign)
+    flows = [(vv0, 0), (vv0, 2), (vv1, 0), (vv1, 2)]
+    wide = (vv1, 4)
+    srcs = [(src0, 0), (src0, 3), (src1, 0), (src1, 3)]
+
+    def keep_g(r, u, s):
+        for c in range(3):
+            gg[c, r] = u[c] + s[c]
+
+    step(begin, 0, *wide, 7, keep_g, float(FINE * GROUP))
 
     def plus(buf, k, base):
+        src, at = srcs[k]
+
         def emit(r, u, s):
             for c in range(3):
-                put(buf, base + c, r, u[c] + float(FINE) * s[c] + src[3 * k + c, r])
+                put(buf, base + c, r, u[c] + float(FINE) * s[c] + src[at + c, r])
 
         return emit
 
-    step(ua, 0, 1, 5, plus(ub, 1, 0))
-    step(ub, 0, 2, 6, plus(ua, 2, 0))
+    step(ends, 0, *flows[1], 5, plus(ub, 1, 0))
+    step(ub, 0, *flows[2], 6, plus(ua, 2, 0))
 
     def forcing(r, u, s):
         for c in range(3):
-            ff[c, r] = u[c] + float(FINE) * s[c] + src[3 * (GROUP - 1) + c, r] - gg[c, r]
-
-    step(ua, 0, GROUP - 1, 7, forcing)
-
+            ff[c, r] = u[c] + float(FINE) * s[c] + src1[3 + c, r] - gg[c, r]
+
+    step(ua, 0, *flows[3], 7, forcing)
+
+    for c in range(3):
+        xb[c, 6] = begin[c, 6]
     for t in range(GROUPS):
-        buf, to = (xa, xb) if t % 2 == 0 else (xb, xa)
+        buf, to = (xa if t else begin, xb) if t % 2 == 0 else (xb, xa)
 
         def settle(r, u, s):
             for c in range(3):
                 y = u[c] + s[c] + ff[c, r]
                 if t == GROUPS - 1 and r >= HALO:
                     yy[c, r] = y
-                put(to, c, r, jnp.where(sub == 0, init[c, r], pltpu.roll(y, 1, 0)))
-
-        step(buf, 0, GROUP, max(7, 6 + t), settle, float(FINE * GROUP))
-
-    step(xa, 0, 0, 14, plus(cc, 0, 0))
-    step(cc, 0, 1, 15, plus(cc, 1, 3))
-    step(cc, 3, 2, 16, plus(cc, 2, 6))
+                put(to, c, r, jnp.where(sub == 0, begin[c, r], pltpu.roll(y, 1, 0)))
+
+        step(buf, 0, *wide, max(7, 6 + t), settle, float(FINE * GROUP))
+
+    step(xa, 0, *flows[0], 14, plus(cc, 0, 0))
+    step(cc, 0, *flows[1], 15, plus(cc, 1, 3))
+    step(cc, 3, *flows[2], 16, plus(cc, 2, 6))
 
     def compact(buf, base, c, y):
         m = jnp.where(low, buf[base + c, y + 16], buf[base + c, 23 - y])
@@ -352,22 +391,35 @@
     return call(cut_kernel, 1, 3, outs, scratch, HBM, 60)(meta, init, ends, vel)
 
 
-def cycle(meta, mate, cur, other):
+def sort(cur):
+    return call(sort_kernel, 0, 1, (f32(160, 8, 128), f32(80, 8, 128), f32(80, 8, 128)))(cur)
+
+
+def fine(pair, meta, own, mate, other):
+    tall = BAND + 1
+    outs = [f32(4 + 2 * pair, BAND, 8, 128), f32(6, BAND, 8, 128)]
+    scratch = [buffer(6, tall, 8, 128)]
+    if pair == 0:
+        outs += [f32(6, tall, 8, 128), f32(3, tall, 8, 128)]
+    else:
+        scratch *= 2
+    kernel = functools.partial(fine_kernel, pair)
+    return call(kernel, 1, 3, tuple(outs), scratch)(meta, own, mate, other)
+
+
+def coarse(meta, *arrays):
     tall = BAND + 1
     scratch = [
-        buffer(12, tall, 8, 128),
-        buffer(12, tall, 8, 128),
-        buffer(10, BAND, 8, 128),
-        buffer(12, BAND, 8, 128),
+        buffer(3, tall, 8, 128),
+        buffer(3, tall, 8, 128),
         buffer(3, BAND, 8, 128),
         buffer(3, BAND, 8, 128),
-        buffer(3, tall, 8, 128),
         buffer(3, tall, 8, 128),
         buffer(3, tall, 8, 128),
         buffer(3, BAND, 8, 128),
         buffer(9, tall, 8, 128),
     ]
-    return call(cycle_kernel, 1, 3, f32(96, 8, 128), scratch)(meta, mate, cur, other)
+    return call(coarse_kernel, 1, 6, f32(96, 8, 128), scratch)(meta, *arrays)
 
 
 def begins(meta, tiles, flow):
@@ -396,9 +448,13 @@
     windows, flow = cut(here, initial_state, guessed_ends[0], velocity[0])
     cur = lax.all_to_all(windows.reshape(intervals, 40, 128), "tm", 0, 0)
     cur = cur.reshape(intervals * 5, 8, 128)
-    mate = lax.ppermute(cur, "gy", mates)
-    other = lax.ppermute(cur, "gy", others)
-    tiles = cycle(slab, mate, cur, other)
+    both, one, two = sort(cur)
+    other_one = lax.ppermute(one, "gy", others)
+    other_two = lax.ppermute(two, "gy", others)
+    mate = lax.ppermute(both, "gy", mates)
+    vv0, src0, ends, begin = fine(0, slab, one, mate, other_one)
+    vv1, src1 = fine(1, slab, two, mate, other_two)
+    tiles = coarse(slab, ends, vv0, src0, begin, vv1, src1)
     tiles = lax.all_to_all(tiles.reshape(intervals, 24, 128), "tm", 0, 0)
     tiles = tiles.reshape(intervals * 3, 8, 128)
     mid, mate, other = begins(slab, tiles, flow)

time: 86.6 us -> 87.7 us (1.013); the launches traced: 86.3 us -> 86.4 us
  starting transfers between devices: 17.6 us -> 20.2 us
  waiting for transfers between devices: 7.46 us -> 5.1 us
  blocking collectives: 46.5 us -> 45.3 us
  Pallas kernels: 13.9 us -> 15 us
    ppermute x2 -> x3, waiting for transfers between devices: 6.25 us -> 3.89 us  [the longest x1 2.74 us: per_device(): other_two = lax.ppermute(two, 'gy', others)]
    ppermute x2 -> x3, starting transfers between devices: 8.25 us -> 10.2 us  [the longest x1 4.37 us: per_device(): mate = lax.ppermute(both, 'gy', mates)]
    all_to_all x1, blocking collectives: 17.3 us -> 16.1 us  [per_device(): tiles = lax.all_to_all(tiles.reshape(intervals, 24, 128), 'tm', 0, 0)]
    pallas_call x1 -> x4, Pallas kernels: 7.92 us -> 8.96 us  [the longest x2 4.98 us: fine(): return call(kernel, 1, 3, tuple(outs), scratch)(meta, own, mate, other)]
  transfers between devices with their start and end apart: 4 -> 5, of which waited for: 2 -> 3; matrix products, arithmetic and copies ran while one was open for 0% -> 0% of each run, Pallas kernels for 1% -> 4%
where the time goes in v4:
time: 87.7 us; the launch traced here: 86.4 us
  blocking collectives  45.3 us (52%)
  starting transfers between devices  20.2 us (23%)
  Pallas kernels  15 us (17%)
  waiting for transfers between devices  5.1 us (6%)
    all_to_all x1, blocking collectives, per_device(): cur = lax.all_to_all(windows.reshape(intervals, 40, 128), 'tm', 0, 0)  29.2 us
    all_to_all x1, blocking collectives, per_device(): tiles = lax.all_to_all(tiles.reshape(intervals, 24, 128), 'tm', 0, 0)  16.1 us
    ppermute x1, starting transfers between devices, per_device(): other = lax.ppermute(other, 'gy', others)  8.14 us
    pallas_call x2, Pallas kernels, fine(): return call(kernel, 1, 3, tuple(outs), scratch)(meta, own, mate, other)  4.98 us
    ppermute x1, starting transfers between devices, per_device(): mate = lax.ppermute(both, 'gy', mates)  4.37 us
    ppermute x1, starting transfers between devices, per_device(): other_two = lax.ppermute(two, 'gy', others)  3.9 us
    pallas_call x1, Pallas kernels, coarse(): return call(coarse_kernel, 1, 6, f32(96, 8, 128), scratch)(meta, *arrays)  3.85 us
    ppermute x1, waiting for transfers between devices, per_device(): other_two = lax.ppermute(two, 'gy', others)  2.74 us
  transfers between devices with their start and end apart: 5, of which 3 were waited for; matrix products, arithmetic and copies ran while one was open for 0% of the time, Pallas kernels for 4%

profile of v4, /device:TPU:1, one launch (start us, length us, event | category | flops | bytes accessed | tf_op | source)
XLA Modules:
  0.0 86.4 jit_solution(2308254612608271070)
XLA Ops:
  0.6 2.4 %shard_map.50 = (f32[160,8,128]{2,1,0:T(8,128)}, f32[32,8,128]{2,1,0:T(8,128)}) custom-call(s32[1]{0:T(128)} %bitcast.1.meta, f32[3,16,1024]{2,1,0:T(8,128)} %init_hbm.1, f32[3,16,1024]{2,1,0:T(8,128)} %bitcast.15, f32[2,16,1024]{2,1,0:T(8,128)} %bitcast.18), custom_call_target="tpu_custom_call" | custom-call | tf_op jit(solution)/shard_map/pallas_call | solution.py:391
  3.0 29.2 %all_to_all.10 = f32[32,40,128]{2,1,0:T(8,128)S(1)} all-to-all(f32[32,40,128]{2,1,0:T(8,128)} %bitcast.14), channel_id=1, replica_groups=mesh['tm'=32,'gy'=16] {'tm'}, dimensions={0} | all-to-all | bytes 1310720 | tf_op jit(solution)/shard_map/all_to_all | solution.py:449
  32.2 0.1 shard_map.51
  32.4 4.4 %collective-permute-start = (f32[160,8,128]{2,1,0:T(8,128)S(1)}, f32[160,8,128]{2,1,0:T(8,128)S(1)}, u32[]{:S(2)}, u32[]{:S(2)}) collective-permute-start(f32[160,8,128]{2,1,0:T(8,128)S(1)} %get-tuple-element.18), channel_id=1, source_target_pairs={{0,1},{1,0},{2,3},{3,2},{4,5},{5,4},{6,7},{7,6},{8,9},{9,8},{10,11... | collective-permute-start | bytes 1966088 | tf_op jit(solution)/shard_map/ppermute | solution.py:454
  36.7 3.9 %collective-permute-start.2 = (f32[80,8,128]{2,1,0:T(8,128)S(1)}, f32[80,8,128]{2,1,0:T(8,128)S(1)}, u32[]{:S(2)}, u32[]{:S(2)}) collective-permute-start(f32[80,8,128]{2,1,0:T(8,128)S(1)} %get-tuple-element.23.own), channel_id=1, source_target_pairs={{1,2},{2,1},{3,4},{4,3},{5,6},{6,5},{7,8},{8,7},{9,10},{10,9},{11,... | collective-permute-start | bytes 983048 | tf_op jit(solution)/shard_map/ppermute | solution.py:453
  40.6 1.9 %collective-permute-start.1 = (f32[80,8,128]{2,1,0:T(8,128)S(1)}, f32[80,8,128]{2,1,0:T(8,128)S(1)}, u32[]{:S(2)}, u32[]{:S(2)}) collective-permute-start(f32[80,8,128]{2,1,0:T(8,128)S(1)} %get-tuple-element.17.own), channel_id=1, source_target_pairs={{1,2},{2,1},{3,4},{4,3},{5,6},{6,5},{7,8},{8,7},{9,10},{10,9},{11,... | collective-permute-start | bytes 983048 | tf_op jit(solution)/shard_map/ppermute | solution.py:452
  42.6 0.1 pad_add_fusion.meta
  42.7 2.7 %collective-permute-done.2.other = f32[80,8,128]{2,1,0:T(8,128)S(1)} collective-permute-done((f32[80,8,128]{2,1,0:T(8,128)S(1)}, f32[80,8,128]{2,1,0:T(8,128)S(1)}, u32[]{:S(2)}, u32[]{:S(2)}) %collective-permute-start.2) | collective-permute-done | bytes 327712 | tf_op jit(solution)/shard_map/ppermute | solution.py:453
  45.4 0.0 collective-permute-done.mate
  45.4 2.5 %shard_map.53 = (f32[6,24,8,128]{3,2,1,0:T(8,128)S(1)}, f32[6,24,8,128]{3,2,1,0:T(8,128)S(1)}) custom-call(s32[2]{0:T(128)S(1)} %pad_add_fusion.meta, f32[80,8,128]{2,1,0:T(8,128)S(1)} %get-tuple-element.23.own, f32[160,8,128]{2,1,0:T(8,128)S(1)} %collective-permute-done.mate, f32[80,8,128]{2,1,0:T(8,128)S(1)} %collective-permute-done.2.other), custom_call_target="tpu_custom_call" | custom-call | tf_op jit(solution)/shard_map/pallas_call | solution.py:407
  47.9 1.2 %collective-permute-done.1.other = f32[80,8,128]{2,1,0:T(8,128)S(1)} collective-permute-done((f32[80,8,128]{2,1,0:T(8,128)S(1)}, f32[80,8,128]{2,1,0:T(8,128)S(1)}, u32[]{:S(2)}, u32[]{:S(2)}) %collective-permute-start.1) | collective-permute-done | bytes 327712 | tf_op jit(solution)/shard_map/ppermute | solution.py:452
  49.0 2.5 %shard_map.52 = (f32[4,24,8,128]{3,2,1,0:T(8,128)S(1)}, f32[6,24,8,128]{3,2,1,0:T(8,128)S(1)}, f32[6,25,8,128]{3,2,1,0:T(8,128)S(1)}, f32[3,25,8,128]{3,2,1,0:T(8,128)S(1)}) custom-call(s32[2]{0:T(128)S(1)} %pad_add_fusion.meta, f32[80,8,128]{2,1,0:T(8,128)S(1)} %get-tuple-element.17.own, f32[160,8,128]{2,1,0:T(8,128)S(1)} %collective-permute-done.mate, ...), custom_call_target="tpu_custom_call" | custom-call | tf_op jit(solution)/shard_map/pallas_call | solution.py:407
  51.5 3.9 %shard_map.54 = f32[96,8,128]{2,1,0:T(8,128)S(1)} custom-call(s32[2]{0:T(128)S(1)} %pad_add_fusion.meta, f32[6,25,8,128]{3,2,1,0:T(8,128)S(1)} %get-tuple-element.19.ends, f32[4,24,8,128]{3,2,1,0:T(8,128)S(1)} %get-tuple-element.20.vv0, f32[6,24,8,128]{3,2,1,0:T(8,128)S(1)} %get-tuple-element.21.src0, f32[3,25,8,128]{3,2,1,0:T(8,128)S(1)} %get-tuple-element.22.begin, ...), custom_call_target="tpu_custom_call" | custom-call | tf_op jit(solution)/shard_map/pallas_call | solution.py:422
  55.4 0.0 copy-start
  55.4 16.1 %all_to_all.11 = f32[32,24,128]{2,1,0:T(8,128)S(1)} all-to-all(f32[32,24,128]{2,1,0:T(8,128)S(1)} %bitcast.13), channel_id=1, replica_groups=mesh['tm'=32,'gy'=16] {'tm'}, dimensions={0} | all-to-all | bytes 786432 | tf_op jit(solution)/shard_map/all_to_all | solution.py:458
  71.5 0.0 copy-done
  71.5 0.8 shard_map.56
  72.3 1.9 %collective-permute-start.3 = (f32[20,8,128]{2,1,0:T(8,128)S(1)}, f32[20,8,128]{2,1,0:T(8,128)S(1)}, u32[]{:S(2)}, u32[]{:S(2)}) collective-permute-start(f32[20,8,128]{2,1,0:T(8,128)S(1)} %get-tuple-element.28), channel_id=1, source_target_pairs={{0,1},{1,0},{2,3},{3,2},{4,5},{5,4},{6,7},{7,6},{8,9},{9,8},{10,11... | collective-permute-start | bytes 245768 | tf_op jit(solution)/shard_map/ppermute | solution.py:461
  74.2 8.1 %collective-permute-start.4 = (f32[20,8,128]{2,1,0:T(8,128)S(1)}, f32[20,8,128]{2,1,0:T(8,128)S(1)}, u32[]{:S(2)}, u32[]{:S(2)}) collective-permute-start(f32[20,8,128]{2,1,0:T(8,128)S(1)} %get-tuple-element.29), channel_id=1, source_target_pairs={{1,2},{2,1},{3,4},{4,3},{5,6},{6,5},{7,8},{8,7},{9,10},{10,9},{11,... | collective-permute-start | bytes 245768 | tf_op jit(solution)/shard_map/ppermute | solution.py:462
  82.4 0.9 %shard_map.55 = f32[3,16,1024]{2,1,0:T(8,128)} custom-call(f32[96,8,128]{2,1,0:T(8,128)S(1)} %bitcast.11), custom_call_target="tpu_custom_call" | custom-call | tf_op jit(solution)/shard_map/pallas_call | solution.py:431
  83.3 0.0 collective-permute-done.3.mate
  83.3 1.2 %collective-permute-done.4.other = f32[20,8,128]{2,1,0:T(8,128)S(1)} collective-permute-done((f32[20,8,128]{2,1,0:T(8,128)S(1)}, f32[20,8,128]{2,1,0:T(8,128)S(1)}, u32[]{:S(2)}, u32[]{:S(2)}) %collective-permute-start.4) | collective-permute-done | bytes 81952 | tf_op jit(solution)/shard_map/ppermute | solution.py:462
  84.5 1.9 %shard_map.57 = f32[3,16,1024]{2,1,0:T(8,128)} custom-call(s32[2]{0:T(128)S(1)} %pad_add_fusion.meta, f32[48,8,128]{2,1,0:T(8,128)S(1)} %get-tuple-element.27.mid, f32[32,8,128]{2,1,0:T(8,128)S(1)} %copy-done, f32[20,8,128]{2,1,0:T(8,128)S(1)} %collective-permute-done.3.mate, f32[20,8,128]{2,1,0:T(8,128)S(1)} %collective-permute-done.4.other), custom_call_target="tpu_custom_call" | custom-call | tf_op jit(solution)/shard_map/pallas_call | solution.py:437
Async XLA Ops:
  32.4 13.0 %collective-permute-start = (f32[160,8,128]{2,1,0:T(8,128)S(1)}, f32[160,8,128]{2,1,0:T(8,128)S(1)}, u32[]{:S(2)}, u32[]{:S(2)}) collective-permute-start(f32[160,8,128]{2,1,0:T(8,128)S(1)} %get-tuple-element.18), channel_id=1, source_target_pairs={{0,1},{1,0},{2,3},{3,2},{4,5},{5,4},{6,7},{7,6},{8,9},{9,8},{10,11... | collective-permute-start | bytes 1966088 | tf_op jit(solution)/shard_map/ppermute | solution.py:454
  36.7 8.6 %collective-permute-start.2 = (f32[80,8,128]{2,1,0:T(8,128)S(1)}, f32[80,8,128]{2,1,0:T(8,128)S(1)}, u32[]{:S(2)}, u32[]{:S(2)}) collective-permute-start(f32[80,8,128]{2,1,0:T(8,128)S(1)} %get-tuple-element.23.own), channel_id=1, source_target_pairs={{1,2},{2,1},{3,4},{4,3},{5,6},{6,5},{7,8},{8,7},{9,10},{10,9},{11,... | collective-permute-start | bytes 983048 | tf_op jit(solution)/shard_map/ppermute | solution.py:453
  40.6 8.4 %collective-permute-start.1 = (f32[80,8,128]{2,1,0:T(8,128)S(1)}, f32[80,8,128]{2,1,0:T(8,128)S(1)}, u32[]{:S(2)}, u32[]{:S(2)}) collective-permute-start(f32[80,8,128]{2,1,0:T(8,128)S(1)} %get-tuple-element.17.own), channel_id=1, source_target_pairs={{1,2},{2,1},{3,4},{4,3},{5,6},{6,5},{7,8},{8,7},{9,10},{10,9},{11,... | collective-permute-start | bytes 983048 | tf_op jit(solution)/shard_map/ppermute | solution.py:452
  55.4 16.1 %copy-start = (f32[32,8,128]{2,1,0:T(8,128)S(1)}, f32[32,8,128]{2,1,0:T(8,128)}, u32[]{:S(2)}) copy-start(f32[32,8,128]{2,1,0:T(8,128)} %get-tuple-element.26.flow) | copy-start | bytes 393220
  72.3 11.0 %collective-permute-start.3 = (f32[20,8,128]{2,1,0:T(8,128)S(1)}, f32[20,8,128]{2,1,0:T(8,128)S(1)}, u32[]{:S(2)}, u32[]{:S(2)}) collective-permute-start(f32[20,8,128]{2,1,0:T(8,128)S(1)} %get-tuple-element.28), channel_id=1, source_target_pairs={{0,1},{1,0},{2,3},{3,2},{4,5},{5,4},{6,7},{7,6},{8,9},{9,8},{10,11... | collective-permute-start | bytes 245768 | tf_op jit(solution)/shard_map/ppermute | solution.py:461
  74.2 10.3 %collective-permute-start.4 = (f32[20,8,128]{2,1,0:T(8,128)S(1)}, f32[20,8,128]{2,1,0:T(8,128)S(1)}, u32[]{:S(2)}, u32[]{:S(2)}) collective-permute-start(f32[20,8,128]{2,1,0:T(8,128)S(1)} %get-tuple-element.29), channel_id=1, source_target_pairs={{1,2},{2,1},{3,4},{4,3},{5,6},{6,5},{7,8},{8,7},{9,10},{10,9},{11,... | collective-permute-start | bytes 245768 | tf_op jit(solution)/shard_map/ppermute | solution.py:462

commit v5 on v3

--- a/solution.py
+++ b/solution.py
@@ -86,7 +86,7 @@
                 flow[c * ROWS + y0 + y] = value
 
 
-def cycle_kernel(meta, mate, cur, other, out, ua, ub, vv, src, gg, ff, init, xa, xb, yy, cc):
+def cycle_kernel(meta, mate, cur, other, flow, xa, cc, yy, to_mate, to_other, ua, ub, vv, src, gg, ff, init, xb):
     lane, sub = lanes(), sublanes()
     low = lane < HALF
     sign = jnp.where(low, 1.0, -1.0)
@@ -223,6 +223,27 @@
     step(cc, 0, 1, 15, plus(cc, 1, 3))
     step(cc, 3, 2, 16, plus(cc, 2, 6))
 
+    group = lane // TILE
+    for k, (buf, base) in enumerate([(xa, 0), (cc, 0), (cc, 3), (cc, 6)]):
+        for q in range(FINE):
+            sides = []
+            for r, at in ((23 - FINE - q, HALF + HALO), (16 + q, HALO)):
+                parts = [pltpu.roll(buf[base + c, r], (TILE * c - at) % 128, 1) for c in range(3)]
+                sides.append(jnp.where(group == 0, parts[0], jnp.where(group == 1, parts[1], parts[2])))
+            up, down = sides
+            to_mate[k * FINE + q] = jnp.where(even, up, down)
+            to_other[k * FINE + q] = jnp.where(even, down, up)
+    for c in range(2):
+        for q in range(FINE):
+            down, up = flow[c * ROWS + q], flow[(c + 1) * ROWS - FINE + q]
+            to_mate[(GROUP + c) * FINE + q] = jnp.where(even, up, down)
+            to_other[(GROUP + c) * FINE + q] = jnp.where(even, down, up)
+
+
+def pack_kernel(xa, cc, yy, out):
+    lane = lanes()
+    low = lane < HALF
+
     def compact(buf, base, c, y):
         m = jnp.where(low, buf[base + c, y + 16], buf[base + c, 23 - y])
         return jnp.where(lane < TILE, pltpu.roll(m, 128 - HALO, 1), pltpu.roll(m, 128 - HALO - TILE, 1))
@@ -238,56 +259,59 @@
             before = own
 
 
-def gathered(tiles, c, b, part):
+def edge_kernel(meta, tiles, mate, other, out):
+    even = meta[0] % 2 == 0
+    for i in range(GROUP * GROUPS):
+        for c in range(3):
+            out[4 * i + c] = tiles[3 * i + c]
+    for k in range(GROUP):
+        below, above = [], []
+        for q in range(FINE):
+            m, o = mate[k * FINE + q], other[k * FINE + q]
+            below.append(jnp.where(even, o, m))
+            above.append(jnp.where(even, m, o))
+        for j, value in enumerate(swap8(below + above)):
+            out[4 * (4 * j + k) + 3] = value
+
+
+def gathered(tiles, block, b, part):
     group = lanes() // TILE
     value = None
     for q in range(4):
         shift = (TILE * (q - part)) % 128
-        x = tiles[(4 * b + q) * 3 + c]
+        x = tiles[(4 * b + q) * 4 + block]
         x = pltpu.roll(x, shift, 1) if shift else x
         value = x if value is None else jnp.where(group == q, x, value)
     return value
 
 
-def begin_kernel(meta, tiles, flow, begin, mate, other):
-    even = meta[0] % 2 == 0
-    for c in range(5):
-        if c < 3:
-            rows = []
-            for part in (2, 3):
-                rows += swap8([gathered(tiles, c, b, part) for b in range(8)])
-            for y in range(ROWS):
-                begin[c * ROWS + y] = rows[y]
-        else:
-            rows = [flow[(c - 3) * ROWS + y] for y in range(ROWS)]
-        for y in range(FINE):
-            down, up = rows[y], rows[ROWS - FINE + y]
-            mate[c * FINE + y] = jnp.where(even, up, down)
-            other[c * FINE + y] = jnp.where(even, down, up)
-
-
-def own_kernel(tiles, own):
+def relax_kernel(meta, tiles, flow, mate, other, own_hbm, out_hbm, own, out, wa, wb, vv, sems):
     for c in range(3):
         for b in range(8):
             at = slice(128 * b, 128 * b + 128)
             own[c, 0:8, at] = gathered(tiles, c, b, 0)
             own[c, 8:16, at] = gathered(tiles, c, b, 1)
-
-
-def relax_kernel(meta, mid, flow, mate, other, out, wa, wb, vv):
+    first = pltpu.make_async_copy(own, own_hbm, sems.at[0])
+    first.start()
+
     lane = lanes()
     tall = ROWS + 2 * FINE
     kappa = time_step * kappa_coupling
     even = meta[0] % 2 == 0
-    for a in range(5):
-        src, buf, at = (mid, wa, a) if a < 3 else (flow, vv, a - 3)
-        scale = 1.0 if a < 3 else time_step
+    for c in range(3):
+        edges = swap8([gathered(tiles, 3, b, c) for b in range(8)])
+        rows = edges[:FINE]
+        for part in (2, 3):
+            rows += swap8([gathered(tiles, c, b, part) for b in range(8)])
+        for r, value in enumerate(rows + edges[FINE:]):
+            wa[c * tall + r] = value
+    for c in range(2):
         for r in range(FINE):
-            m, o = mate[a * FINE + r], other[a * FINE + r]
-            buf[at * tall + r] = scale * jnp.where(even, o, m)
-            buf[at * tall + FINE + ROWS + r] = scale * jnp.where(even, m, o)
+            m, o = mate[(GROUP + c) * FINE + r], other[(GROUP + c) * FINE + r]
+            vv[c * tall + r] = time_step * jnp.where(even, o, m)
+            vv[c * tall + FINE + ROWS + r] = time_step * jnp.where(even, m, o)
         for r in range(ROWS):
-            buf[at * tall + FINE + r] = scale * src[at * ROWS + r]
+            vv[c * tall + FINE + r] = time_step * flow[c * ROWS + r]
 
     bottom, top = meta[0] == 0, meta[0] == meta[1] - 1
     def sweep(section, buf, to):
@@ -323,6 +347,10 @@
     for section in range(FINE):
         buf, to = (wa, wb) if section % 2 == 0 else (wb, wa)
         sweep(section, buf, to)
+    second = pltpu.make_async_copy(out, out_hbm, sems.at[1])
+    second.start()
+    first.wait()
+    second.wait()
 
 
 def f32(*shape):
@@ -333,13 +361,13 @@
     return pltpu.VMEM(shape, jnp.float32)
 
 
-def call(kernel, n_scalars, n_arrays, outs, scratch=(), space=VMEM, mib=24):
+def call(kernel, n_scalars, n_arrays, outs, scratch=(), space=VMEM, to=VMEM, mib=24):
     many = isinstance(outs, tuple)
     return pl.pallas_call(
         kernel,
         out_shape=outs,
         in_specs=[SMEM] * n_scalars + [space] * n_arrays,
-        out_specs=(VMEM,) * len(outs) if many else VMEM,
+        out_specs=(to,) * len(outs) if many else to,
         scratch_shapes=list(scratch),
         compiler_params=pltpu.CompilerParams(vmem_limit_bytes=mib * 1024 * 1024),
     )
@@ -349,11 +377,13 @@
     state, flow = buffer(3, ROWS, 1024), buffer(2, ROWS, 1024)
     scratch = [state, state, flow, pltpu.SemaphoreType.DMA((3,))]
     outs = (f32(160, 8, 128), f32(2 * ROWS, 8, 128))
-    return call(cut_kernel, 1, 3, outs, scratch, HBM, 60)(meta, init, ends, vel)
-
-
-def cycle(meta, mate, cur, other):
+    return call(cut_kernel, 1, 3, outs, scratch, HBM, VMEM, 60)(meta, init, ends, vel)
+
+
+def cycle(meta, mate, cur, other, flow):
     tall = BAND + 1
+    edge = f32((GROUP + 2) * FINE, 8, 128)
+    outs = (f32(3, tall, 8, 128), f32(9, tall, 8, 128), f32(3, BAND, 8, 128), edge, edge)
     scratch = [
         buffer(12, tall, 8, 128),
         buffer(12, tall, 8, 128),
@@ -363,26 +393,30 @@
         buffer(3, BAND, 8, 128),
         buffer(3, tall, 8, 128),
         buffer(3, tall, 8, 128),
-        buffer(3, tall, 8, 128),
-        buffer(3, BAND, 8, 128),
-        buffer(9, tall, 8, 128),
     ]
-    return call(cycle_kernel, 1, 3, f32(96, 8, 128), scratch)(meta, mate, cur, other)
-
-
-def begins(meta, tiles, flow):
-    halo = f32(5 * FINE, 8, 128)
-    return call(begin_kernel, 1, 2, (f32(3 * ROWS, 8, 128), halo, halo))(meta, tiles, flow)
-
-
-def owns(tiles):
-    return call(own_kernel, 0, 1, f32(3, ROWS, 1024))(tiles)
-
-
-def relax(meta, mid, flow, mate, other):
+    return call(cycle_kernel, 1, 4, outs, scratch)(meta, mate, cur, other, flow)
+
+
+def pack(xa, cc, yy):
+    return call(pack_kernel, 0, 3, f32(96, 8, 128))(xa, cc, yy)
+
+
+def edge(meta, tiles, mate, other):
+    return call(edge_kernel, 1, 3, f32(128, 8, 128))(meta, tiles, mate, other)
+
+
+def relax(meta, tiles, flow, mate, other):
     tall = ROWS + 2 * FINE
-    scratch = [buffer(3 * tall, 8, 128), buffer(3 * tall, 8, 128), buffer(2 * tall, 8, 128)]
-    return call(relax_kernel, 1, 4, f32(3, ROWS, 1024), scratch)(meta, mid, flow, mate, other)
+    whole = f32(3, ROWS, 1024)
+    scratch = [
+        buffer(3, ROWS, 1024),
+        buffer(3, ROWS, 1024),
+        buffer(3 * tall, 8, 128),
+        buffer(3 * tall, 8, 128),
+        buffer(2 * tall, 8, 128),
+        pltpu.SemaphoreType.DMA((2,)),
+    ]
+    return call(relax_kernel, 1, 4, (whole, whole), scratch, VMEM, HBM)(meta, tiles, flow, mate, other)
 
 
 def per_device(initial_state, guessed_ends, velocity):
@@ -398,14 +432,13 @@
     cur = cur.reshape(intervals * 5, 8, 128)
     mate = lax.ppermute(cur, "gy", mates)
     other = lax.ppermute(cur, "gy", others)
-    tiles = cycle(slab, mate, cur, other)
-    tiles = lax.all_to_all(tiles.reshape(intervals, 24, 128), "tm", 0, 0)
-    tiles = tiles.reshape(intervals * 3, 8, 128)
-    mid, mate, other = begins(slab, tiles, flow)
-    mate = lax.ppermute(mate, "gy", mates)
-    other = lax.ppermute(other, "gy", others)
-    own = owns(tiles)
-    relaxed = relax(slab, mid, flow, mate, other)
+    xa, cc, yy, to_mate, to_other = cycle(slab, mate, cur, other, flow)
+    mate = lax.ppermute(to_mate, "gy", mates)
+    other = lax.ppermute(to_other, "gy", others)
+    tiles = pack(xa, cc, yy)
+    tiles = edge(slab, tiles, mate, other)
+    tiles = lax.all_to_all(tiles.reshape(intervals, 32, 128), "tm", 0, 0)
+    own, relaxed = relax(slab, tiles.reshape(intervals * 4, 8, 128), flow, mate, other)
     return own[None], relaxed[None]
 
 

time: 86.6 us -> 89.1 us (1.029)
  the two profiles are of different devices: /device:TPU:1 before, /device:TPU:195 now
where the time goes in v5:
time: 89.1 us; the launch traced here: 88.7 us
  blocking collectives  50.4 us (57%)
  starting transfers between devices  16.3 us (18%)
  Pallas kernels  13.4 us (15%)
  waiting for transfers between devices  7.88 us (9%)
    all_to_all x1, blocking collectives, per_device(): cur = lax.all_to_all(windows.reshape(intervals, 40, 128), 'tm', 0, 0)  28.2 us
    all_to_all x1, blocking collectives, per_device(): tiles = lax.all_to_all(tiles.reshape(intervals, 32, 128), 'tm', 0, 0)  22.2 us
    ppermute x1, starting transfers between devices, per_device(): other = lax.ppermute(cur, 'gy', others)  7.6 us
    pallas_call x1, Pallas kernels, cycle(): return call(cycle_kernel, 1, 4, outs, scratch)(meta, mate, cur, other, flow)  7.46 us
    ppermute x1, waiting for transfers between devices, per_device(): other = lax.ppermute(cur, 'gy', others)  6.25 us
    ppermute x1, starting transfers between devices, per_device(): other = lax.ppermute(to_other, 'gy', others)  4.85 us
    pallas_call x1, Pallas kernels, cut(): call(cut_kernel, 1, 3, outs, scratch, HBM, VMEM, 60)(meta, init, ends, vel)  2.37 us
    pallas_call x1, Pallas kernels, relax(): call(relax_kernel, 1, 4, (whole, whole), scratch, VMEM, HBM)  2.33 us
  transfers between devices with their start and end apart: 4, of which 2 were waited for; matrix products, arithmetic and copies ran while one was open for 0% of the time, Pallas kernels for 1%

profile of v5, /device:TPU:195, one launch (start us, length us, event | category | flops | bytes accessed | tf_op | source)
XLA Modules:
  0.0 88.7 jit_solution(3799985439148058779)
XLA Ops:
  0.6 2.4 %shard_map.50 = (f32[160,8,128]{2,1,0:T(8,128)}, f32[32,8,128]{2,1,0:T(8,128)}) custom-call(s32[1]{0:T(128)} %bitcast.1.meta, f32[3,16,1024]{2,1,0:T(8,128)} %init_hbm.1, f32[3,16,1024]{2,1,0:T(8,128)} %bitcast.16, f32[2,16,1024]{2,1,0:T(8,128)} %bitcast.17), custom_call_target="tpu_custom_call" | custom-call | tf_op jit(solution)/shard_map/pallas_call | solution.py:380
  3.0 0.0 copy-start
  3.0 28.2 %all_to_all.10 = f32[32,40,128]{2,1,0:T(8,128)S(1)} all-to-all(f32[32,40,128]{2,1,0:T(8,128)} %bitcast.15), channel_id=1, replica_groups=mesh['tm'=32,'gy'=16] {'tm'}, dimensions={0} | all-to-all | bytes 1310720 | tf_op jit(solution)/shard_map/all_to_all | solution.py:431
  31.2 7.6 %collective-permute-start.1 = (f32[160,8,128]{2,1,0:T(8,128)S(1)}, f32[160,8,128]{2,1,0:T(8,128)S(1)}, u32[]{:S(2)}, u32[]{:S(2)}) collective-permute-start(f32[160,8,128]{2,1,0:T(8,128)S(1)} %bitcast.10), channel_id=1, source_target_pairs={{1,2},{2,1},{3,4},{4,3},{5,6},{6,5},{7,8},{8,7},{9,10},{10,9},{11,... | collective-permute-start | bytes 1966088 | tf_op jit(solution)/shard_map/ppermute | solution.py:434
  38.8 1.9 %collective-permute-start = (f32[160,8,128]{2,1,0:T(8,128)S(1)}, f32[160,8,128]{2,1,0:T(8,128)S(1)}, u32[]{:S(2)}, u32[]{:S(2)}) collective-permute-start(f32[160,8,128]{2,1,0:T(8,128)S(1)} %bitcast.11), channel_id=1, source_target_pairs={{0,1},{1,0},{2,3},{3,2},{4,5},{5,4},{6,7},{7,6},{8,9},{9,8},{10,11... | collective-permute-start | bytes 1966088 | tf_op jit(solution)/shard_map/ppermute | solution.py:433
  40.8 0.1 pad_add_fusion.meta
  40.8 6.2 %collective-permute-done.1.other = f32[160,8,128]{2,1,0:T(8,128)S(1)} collective-permute-done((f32[160,8,128]{2,1,0:T(8,128)S(1)}, f32[160,8,128]{2,1,0:T(8,128)S(1)}, u32[]{:S(2)}, u32[]{:S(2)}) %collective-permute-start.1) | collective-permute-done | bytes 655392 | tf_op jit(solution)/shard_map/ppermute | solution.py:434
  47.1 0.0 collective-permute-done.mate
  47.1 0.0 copy-done
  47.1 7.5 %shard_map.51 = (f32[3,25,8,128]{3,2,1,0:T(8,128)S(1)}, f32[9,25,8,128]{3,2,1,0:T(8,128)S(1)}, f32[3,24,8,128]{3,2,1,0:T(8,128)S(1)}, f32[24,8,128]{2,1,0:T(8,128)S(1)}, f32[24,8,128]{2,1,0:T(8,128)S(1)}) custom-call(s32[2]{0:T(128)S(1)} %pad_add_fusion.meta, f32[160,8,128]{2,1,0:T(8,128)S(1)} %collective-permute-done.mate, f32[160,8,128]{2,1,0:T(8,128)S(1)} %bitcast.12, ...), custom_call_target="tpu_custom_call" | custom-call | tf_op jit(solution)/shard_map/pallas_call | solution.py:397
  54.5 1.9 %collective-permute-start.2 = (f32[24,8,128]{2,1,0:T(8,128)S(1)}, f32[24,8,128]{2,1,0:T(8,128)S(1)}, u32[]{:S(2)}, u32[]{:S(2)}) collective-permute-start(f32[24,8,128]{2,1,0:T(8,128)S(1)} %get-tuple-element.16), channel_id=1, source_target_pairs={{0,1},{1,0},{2,3},{3,2},{4,5},{5,4},{6,7},{7,6},{8,9},{9,8},{10,11... | collective-permute-start | bytes 294920 | tf_op jit(solution)/shard_map/ppermute | solution.py:436
  56.5 4.9 %collective-permute-start.3 = (f32[24,8,128]{2,1,0:T(8,128)S(1)}, f32[24,8,128]{2,1,0:T(8,128)S(1)}, u32[]{:S(2)}, u32[]{:S(2)}) collective-permute-start(f32[24,8,128]{2,1,0:T(8,128)S(1)} %get-tuple-element.17), channel_id=1, source_target_pairs={{1,2},{2,1},{3,4},{4,3},{5,6},{6,5},{7,8},{8,7},{9,10},{10,9},{11,... | collective-permute-start | bytes 294920 | tf_op jit(solution)/shard_map/ppermute | solution.py:437
  61.3 0.6 shard_map.52.tiles
  62.0 0.0 collective-permute-done.2.mate
  62.0 1.6 %collective-permute-done.3.other = f32[24,8,128]{2,1,0:T(8,128)S(1)} collective-permute-done((f32[24,8,128]{2,1,0:T(8,128)S(1)}, f32[24,8,128]{2,1,0:T(8,128)S(1)}, u32[]{:S(2)}, u32[]{:S(2)}) %collective-permute-start.3) | collective-permute-done | bytes 98336 | tf_op jit(solution)/shard_map/ppermute | solution.py:437
  63.6 0.6 shard_map.53
  64.2 22.2 %all_to_all.11 = f32[32,32,128]{2,1,0:T(8,128)S(1)} all-to-all(f32[32,32,128]{2,1,0:T(8,128)S(1)} %bitcast.14), channel_id=1, replica_groups=mesh['tm'=32,'gy'=16] {'tm'}, dimensions={0} | all-to-all | bytes 1048576 | tf_op jit(solution)/shard_map/all_to_all | solution.py:440
  86.4 2.3 %shard_map.54 = (f32[3,16,1024]{2,1,0:T(8,128)}, f32[3,16,1024]{2,1,0:T(8,128)}) custom-call(s32[2]{0:T(128)S(1)} %pad_add_fusion.meta, f32[128,8,128]{2,1,0:T(8,128)S(1)} %bitcast.13, f32[32,8,128]{2,1,0:T(8,128)S(1)} %copy-done, f32[24,8,128]{2,1,0:T(8,128)S(1)} %collective-permute-done.2.mate, f32[24,8,128]{2,1,0:T(8,128)S(1)} %collective-permute-done.3.other), custom_call_target="tpu_custom_call" | custom-call | tf_op jit(solution)/shard_map/pallas_call | solution.py:419
Async XLA Ops:
  3.0 44.1 %copy-start = (f32[32,8,128]{2,1,0:T(8,128)S(1)}, f32[32,8,128]{2,1,0:T(8,128)}, u32[]{:S(2)}) copy-start(f32[32,8,128]{2,1,0:T(8,128)} %get-tuple-element.12.flow) | copy-start | bytes 393220
  31.2 15.9 %collective-permute-start.1 = (f32[160,8,128]{2,1,0:T(8,128)S(1)}, f32[160,8,128]{2,1,0:T(8,128)S(1)}, u32[]{:S(2)}, u32[]{:S(2)}) collective-permute-start(f32[160,8,128]{2,1,0:T(8,128)S(1)} %bitcast.10), channel_id=1, source_target_pairs={{1,2},{2,1},{3,4},{4,3},{5,6},{6,5},{7,8},{8,7},{9,10},{10,9},{11,... | collective-permute-start | bytes 1966088 | tf_op jit(solution)/shard_map/ppermute | solution.py:434
  38.8 8.3 %collective-permute-start = (f32[160,8,128]{2,1,0:T(8,128)S(1)}, f32[160,8,128]{2,1,0:T(8,128)S(1)}, u32[]{:S(2)}, u32[]{:S(2)}) collective-permute-start(f32[160,8,128]{2,1,0:T(8,128)S(1)} %bitcast.11), channel_id=1, source_target_pairs={{0,1},{1,0},{2,3},{3,2},{4,5},{5,4},{6,7},{7,6},{8,9},{9,8},{10,11... | collective-permute-start | bytes 1966088 | tf_op jit(solution)/shard_map/ppermute | solution.py:433
  54.5 7.4 %collective-permute-start.2 = (f32[24,8,128]{2,1,0:T(8,128)S(1)}, f32[24,8,128]{2,1,0:T(8,128)S(1)}, u32[]{:S(2)}, u32[]{:S(2)}) collective-permute-start(f32[24,8,128]{2,1,0:T(8,128)S(1)} %get-tuple-element.16), channel_id=1, source_target_pairs={{0,1},{1,0},{2,3},{3,2},{4,5},{5,4},{6,7},{7,6},{8,9},{9,8},{10,11... | collective-permute-start | bytes 294920 | tf_op jit(solution)/shard_map/ppermute | solution.py:436
  56.5 7.1 %collective-permute-start.3 = (f32[24,8,128]{2,1,0:T(8,128)S(1)}, f32[24,8,128]{2,1,0:T(8,128)S(1)}, u32[]{:S(2)}, u32[]{:S(2)}) collective-permute-start(f32[24,8,128]{2,1,0:T(8,128)S(1)} %get-tuple-element.17), channel_id=1, source_target_pairs={{1,2},{2,1},{3,4},{4,3},{5,6},{6,5},{7,8},{8,7},{9,10},{10,9},{11,... | collective-permute-start | bytes 294920 | tf_op jit(solution)/shard_map/ppermute | solution.py:437

commit v6 on v4

--- a/solution.py
+++ b/solution.py
@@ -88,7 +88,7 @@
                 flow[c * ROWS + y0 + y] = value
 
 
-def sort_kernel(cur, both, one, two):
+def sort_kernel(cur, one, two):
     for k in range(GROUP):
         for a in range(5):
             values = swap8([cur[(4 * j + k) * 5 + a] for j in range(8)])
@@ -100,7 +100,6 @@
             half = one if to < 2 else two
             for y in range(8):
                 half[(to % 2 * 5 + a) * 8 + y] = values[y]
-                both[(to * 5 + a) * 8 + y] = values[y]
 
 
 def masks(meta):
@@ -161,7 +160,7 @@
         for a in range(5):
             at = (k * 5 + a) * 8
             mine = [own[at + y] for y in range(8)]
-            m = [mate[pair * 80 + at + y] for y in range(8)]
+            m = [mate[at + y] for y in range(8)]
             o = [other[at + y] for y in range(8)]
             before = [jnp.where(even, x, y) for x, y in zip(o, m)]
             after = [jnp.where(even, y, x) for x, y in zip(o, m)]
@@ -392,7 +391,7 @@
 
 
 def sort(cur):
-    return call(sort_kernel, 0, 1, (f32(160, 8, 128), f32(80, 8, 128), f32(80, 8, 128)))(cur)
+    return call(sort_kernel, 0, 1, (f32(80, 8, 128), f32(80, 8, 128)))(cur)
 
 
 def fine(pair, meta, own, mate, other):
@@ -448,12 +447,13 @@
     windows, flow = cut(here, initial_state, guessed_ends[0], velocity[0])
     cur = lax.all_to_all(windows.reshape(intervals, 40, 128), "tm", 0, 0)
     cur = cur.reshape(intervals * 5, 8, 128)
-    both, one, two = sort(cur)
+    one, two = sort(cur)
+    mate_two = lax.ppermute(two, "gy", mates)
+    mate_one = lax.ppermute(one, "gy", mates)
+    other_two = lax.ppermute(two, "gy", others)
     other_one = lax.ppermute(one, "gy", others)
-    other_two = lax.ppermute(two, "gy", others)
-    mate = lax.ppermute(both, "gy", mates)
-    vv0, src0, ends, begin = fine(0, slab, one, mate, other_one)
-    vv1, src1 = fine(1, slab, two, mate, other_two)
+    vv0, src0, ends, begin = fine(0, slab, one, mate_one, other_one)
+    vv1, src1 = fine(1, slab, two, mate_two, other_two)
     tiles = coarse(slab, ends, vv0, src0, begin, vv1, src1)
     tiles = lax.all_to_all(tiles.reshape(intervals, 24, 128), "tm", 0, 0)
     tiles = tiles.reshape(intervals * 3, 8, 128)

time: 87.7 us -> 89.2 us (1.017)
  waiting for transfers between devices: 5.1 us -> 1.45 us
  blocking collectives: 45.3 us -> 47.9 us
  starting transfers between devices: 20.2 us -> 22.6 us
    ppermute x1, starting transfers between devices: 8.14 us -> 3.9 us  [per_device(): other = lax.ppermute(other, 'gy', others)]
    ppermute x1, waiting for transfers between devices: 2.74 us -> 0.01 us  [per_device(): other_two = lax.ppermute(two, 'gy', others)]
    all_to_all x1, blocking collectives: 16.1 us -> 18.7 us  [per_device(): tiles = lax.all_to_all(tiles.reshape(intervals, 24, 128), 'tm', 0, 0)]
    ppermute x1, starting transfers between devices: 1.92 us -> 4.38 us  [per_device(): other_one = lax.ppermute(one, 'gy', others)]
    ppermute x1, starting transfers between devices: 3.9 us -> 6.34 us  [per_device(): other_two = lax.ppermute(two, 'gy', others)]
    ppermute x1, starting transfers between devices: 1.92 us -> 4.13 us  [per_device(): mate = lax.ppermute(mate, 'gy', mates)]
    ppermute x1, waiting for transfers between devices: 1.15 us -> 0.23 us  [per_device(): other_one = lax.ppermute(one, 'gy', others)]
    ppermute x1 -> x2, starting transfers between devices: 4.37 us -> 3.84 us  [the longest x1 1.92 us: per_device(): mate_two = lax.ppermute(two, 'gy', mates)]
  transfers between devices with their start and end apart: 5 -> 6, of which waited for: 3 -> 2; matrix products, arithmetic and copies ran while one was open for 0% -> 0% of each run, Pallas kernels for 4% -> 4%
where the time goes in v6:
time: 89.2 us; the launch traced here: 87.8 us
  blocking collectives  47.9 us (54%)
  starting transfers between devices  22.6 us (25%)
  Pallas kernels  14.9 us (17%)
  waiting for transfers between devices  1.45 us (2%)
    all_to_all x1, blocking collectives, per_device(): cur = lax.all_to_all(windows.reshape(intervals, 40, 128), 'tm', 0, 0)  29.2 us
    all_to_all x1, blocking collectives, per_device(): tiles = lax.all_to_all(tiles.reshape(intervals, 24, 128), 'tm', 0, 0)  18.7 us
    ppermute x1, starting transfers between devices, per_device(): other_two = lax.ppermute(two, 'gy', others)  6.34 us
    pallas_call x2, Pallas kernels, fine(): return call(kernel, 1, 3, tuple(outs), scratch)(meta, own, mate, other)  4.98 us
    ppermute x1, starting transfers between devices, per_device(): other_one = lax.ppermute(one, 'gy', others)  4.38 us
    ppermute x1, starting transfers between devices, per_device(): mate = lax.ppermute(mate, 'gy', mates)  4.13 us
    ppermute x1, starting transfers between devices, per_device(): other = lax.ppermute(other, 'gy', others)  3.9 us
    pallas_call x1, Pallas kernels, coarse(): return call(coarse_kernel, 1, 6, f32(96, 8, 128), scratch)(meta, *arrays)  3.85 us
  transfers between devices with their start and end apart: 6, of which 2 were waited for; matrix products, arithmetic and copies ran while one was open for 0% of the time, Pallas kernels for 4%

profile of v6, /device:TPU:1, one launch (start us, length us, event | category | flops | bytes accessed | tf_op | source)
XLA Modules:
  0.0 87.8 jit_solution(612863407212082935)
XLA Ops:
  0.6 2.4 %shard_map.50 = (f32[160,8,128]{2,1,0:T(8,128)}, f32[32,8,128]{2,1,0:T(8,128)}) custom-call(s32[1]{0:T(128)} %bitcast.1.meta, f32[3,16,1024]{2,1,0:T(8,128)} %init_hbm.1, f32[3,16,1024]{2,1,0:T(8,128)} %bitcast.15, f32[2,16,1024]{2,1,0:T(8,128)} %bitcast.18), custom_call_target="tpu_custom_call" | custom-call | tf_op jit(solution)/shard_map/pallas_call | solution.py:390
  3.0 29.2 %all_to_all.10 = f32[32,40,128]{2,1,0:T(8,128)S(1)} all-to-all(f32[32,40,128]{2,1,0:T(8,128)} %bitcast.14), channel_id=1, replica_groups=mesh['tm'=32,'gy'=16] {'tm'}, dimensions={0} | all-to-all | bytes 1310720 | tf_op jit(solution)/shard_map/all_to_all | solution.py:448
  32.2 0.1 shard_map.51
  32.4 6.3 %collective-permute-start.3 = (f32[80,8,128]{2,1,0:T(8,128)S(1)}, f32[80,8,128]{2,1,0:T(8,128)S(1)}, u32[]{:S(2)}, u32[]{:S(2)}) collective-permute-start(f32[80,8,128]{2,1,0:T(8,128)S(1)} %get-tuple-element.21.own), channel_id=1, source_target_pairs={{1,2},{2,1},{3,4},{4,3},{5,6},{6,5},{7,8},{8,7},{9,10},{10,9},{11,... | collective-permute-start | bytes 983048 | tf_op jit(solution)/shard_map/ppermute | solution.py:453
  38.7 1.9 %collective-permute-start.2 = (f32[80,8,128]{2,1,0:T(8,128)S(1)}, f32[80,8,128]{2,1,0:T(8,128)S(1)}, u32[]{:S(2)}, u32[]{:S(2)}) collective-permute-start(f32[80,8,128]{2,1,0:T(8,128)S(1)} %get-tuple-element.21.own), channel_id=1, source_target_pairs={{0,1},{1,0},{2,3},{3,2},{4,5},{5,4},{6,7},{7,6},{8,9},{9,8},{10,11... | collective-permute-start | bytes 983048 | tf_op jit(solution)/shard_map/ppermute | solution.py:451
  40.6 4.4 %collective-permute-start.1 = (f32[80,8,128]{2,1,0:T(8,128)S(1)}, f32[80,8,128]{2,1,0:T(8,128)S(1)}, u32[]{:S(2)}, u32[]{:S(2)}) collective-permute-start(f32[80,8,128]{2,1,0:T(8,128)S(1)} %get-tuple-element.16.own), channel_id=1, source_target_pairs={{1,2},{2,1},{3,4},{4,3},{5,6},{6,5},{7,8},{8,7},{9,10},{10,9},{11,... | collective-permute-start | bytes 983048 | tf_op jit(solution)/shard_map/ppermute | solution.py:454
  45.0 1.9 %collective-permute-start = (f32[80,8,128]{2,1,0:T(8,128)S(1)}, f32[80,8,128]{2,1,0:T(8,128)S(1)}, u32[]{:S(2)}, u32[]{:S(2)}) collective-permute-start(f32[80,8,128]{2,1,0:T(8,128)S(1)} %get-tuple-element.16.own), channel_id=1, source_target_pairs={{0,1},{1,0},{2,3},{3,2},{4,5},{5,4},{6,7},{7,6},{8,9},{9,8},{10,11... | collective-permute-start | bytes 983048 | tf_op jit(solution)/shard_map/ppermute | solution.py:452
  47.0 0.1 pad_add_fusion.meta
  47.0 0.0 collective-permute-done.3.other
  47.0 0.0 collective-permute-done.2.mate
  47.0 2.5 %shard_map.53 = (f32[6,24,8,128]{3,2,1,0:T(8,128)S(1)}, f32[6,24,8,128]{3,2,1,0:T(8,128)S(1)}) custom-call(s32[2]{0:T(128)S(1)} %pad_add_fusion.meta, f32[80,8,128]{2,1,0:T(8,128)S(1)} %get-tuple-element.21.own, f32[80,8,128]{2,1,0:T(8,128)S(1)} %collective-permute-done.2.mate, f32[80,8,128]{2,1,0:T(8,128)S(1)} %collective-permute-done.3.other), custom_call_target="tpu_custom_call" | custom-call | tf_op jit(solution)/shard_map/pallas_call | solution.py:406
  49.5 0.2 collective-permute-done.1.other
  49.8 0.0 collective-permute-done.mate
  49.8 2.5 %shard_map.52 = (f32[4,24,8,128]{3,2,1,0:T(8,128)S(1)}, f32[6,24,8,128]{3,2,1,0:T(8,128)S(1)}, f32[6,25,8,128]{3,2,1,0:T(8,128)S(1)}, f32[3,25,8,128]{3,2,1,0:T(8,128)S(1)}) custom-call(s32[2]{0:T(128)S(1)} %pad_add_fusion.meta, f32[80,8,128]{2,1,0:T(8,128)S(1)} %get-tuple-element.16.own, f32[80,8,128]{2,1,0:T(8,128)S(1)} %collective-permute-done.mate, ...), custom_call_target="tpu_custom_call" | custom-call | tf_op jit(solution)/shard_map/pallas_call | solution.py:406
  52.3 3.9 %shard_map.54 = f32[96,8,128]{2,1,0:T(8,128)S(1)} custom-call(s32[2]{0:T(128)S(1)} %pad_add_fusion.meta, f32[6,25,8,128]{3,2,1,0:T(8,128)S(1)} %get-tuple-element.17.ends, f32[4,24,8,128]{3,2,1,0:T(8,128)S(1)} %get-tuple-element.18.vv0, f32[6,24,8,128]{3,2,1,0:T(8,128)S(1)} %get-tuple-element.19.src0, f32[3,25,8,128]{3,2,1,0:T(8,128)S(1)} %get-tuple-element.20.begin, ...), custom_call_target="tpu_custom_call" | custom-call | tf_op jit(solution)/shard_map/pallas_call | solution.py:421
  56.1 0.0 copy-start
  56.2 18.7 %all_to_all.11 = f32[32,24,128]{2,1,0:T(8,128)S(1)} all-to-all(f32[32,24,128]{2,1,0:T(8,128)S(1)} %bitcast.13), channel_id=1, replica_groups=mesh['tm'=32,'gy'=16] {'tm'}, dimensions={0} | all-to-all | bytes 786432 | tf_op jit(solution)/shard_map/all_to_all | solution.py:458
  74.9 0.0 copy-done
  74.9 0.8 shard_map.56
  75.7 4.1 %collective-permute-start.4 = (f32[20,8,128]{2,1,0:T(8,128)S(1)}, f32[20,8,128]{2,1,0:T(8,128)S(1)}, u32[]{:S(2)}, u32[]{:S(2)}) collective-permute-start(f32[20,8,128]{2,1,0:T(8,128)S(1)} %get-tuple-element.26), channel_id=1, source_target_pairs={{0,1},{1,0},{2,3},{3,2},{4,5},{5,4},{6,7},{7,6},{8,9},{9,8},{10,11... | collective-permute-start | bytes 245768 | tf_op jit(solution)/shard_map/ppermute | solution.py:461
  79.8 3.9 %collective-permute-start.5 = (f32[20,8,128]{2,1,0:T(8,128)S(1)}, f32[20,8,128]{2,1,0:T(8,128)S(1)}, u32[]{:S(2)}, u32[]{:S(2)}) collective-permute-start(f32[20,8,128]{2,1,0:T(8,128)S(1)} %get-tuple-element.27), channel_id=1, source_target_pairs={{1,2},{2,1},{3,4},{4,3},{5,6},{6,5},{7,8},{8,7},{9,10},{10,9},{11,... | collective-permute-start | bytes 245768 | tf_op jit(solution)/shard_map/ppermute | solution.py:462
  83.7 0.9 %shard_map.55 = f32[3,16,1024]{2,1,0:T(8,128)} custom-call(f32[96,8,128]{2,1,0:T(8,128)S(1)} %bitcast.11), custom_call_target="tpu_custom_call" | custom-call | tf_op jit(solution)/shard_map/pallas_call | solution.py:430
  84.6 0.0 collective-permute-done.4.mate
  84.6 1.2 %collective-permute-done.5.other = f32[20,8,128]{2,1,0:T(8,128)S(1)} collective-permute-done((f32[20,8,128]{2,1,0:T(8,128)S(1)}, f32[20,8,128]{2,1,0:T(8,128)S(1)}, u32[]{:S(2)}, u32[]{:S(2)}) %collective-permute-start.5) | collective-permute-done | bytes 81952 | tf_op jit(solution)/shard_map/ppermute | solution.py:462
  85.8 1.9 %shard_map.57 = f32[3,16,1024]{2,1,0:T(8,128)} custom-call(s32[2]{0:T(128)S(1)} %pad_add_fusion.meta, f32[48,8,128]{2,1,0:T(8,128)S(1)} %get-tuple-element.25.mid, f32[32,8,128]{2,1,0:T(8,128)S(1)} %copy-done, f32[20,8,128]{2,1,0:T(8,128)S(1)} %collective-permute-done.4.mate, f32[20,8,128]{2,1,0:T(8,128)S(1)} %collective-permute-done.5.other), custom_call_target="tpu_custom_call" | custom-call | tf_op jit(solution)/shard_map/pallas_call | solution.py:436
Async XLA Ops:
  32.4 14.7 %collective-permute-start.3 = (f32[80,8,128]{2,1,0:T(8,128)S(1)}, f32[80,8,128]{2,1,0:T(8,128)S(1)}, u32[]{:S(2)}, u32[]{:S(2)}) collective-permute-start(f32[80,8,128]{2,1,0:T(8,128)S(1)} %get-tuple-element.21.own), channel_id=1, source_target_pairs={{1,2},{2,1},{3,4},{4,3},{5,6},{6,5},{7,8},{8,7},{9,10},{10,9},{11,... | collective-permute-start | bytes 983048 | tf_op jit(solution)/shard_map/ppermute | solution.py:453
  38.7 8.3 %collective-permute-start.2 = (f32[80,8,128]{2,1,0:T(8,128)S(1)}, f32[80,8,128]{2,1,0:T(8,128)S(1)}, u32[]{:S(2)}, u32[]{:S(2)}) collective-permute-start(f32[80,8,128]{2,1,0:T(8,128)S(1)} %get-tuple-element.21.own), channel_id=1, source_target_pairs={{0,1},{1,0},{2,3},{3,2},{4,5},{5,4},{6,7},{7,6},{8,9},{9,8},{10,11... | collective-permute-start | bytes 983048 | tf_op jit(solution)/shard_map/ppermute | solution.py:451
  40.6 9.1 %collective-permute-start.1 = (f32[80,8,128]{2,1,0:T(8,128)S(1)}, f32[80,8,128]{2,1,0:T(8,128)S(1)}, u32[]{:S(2)}, u32[]{:S(2)}) collective-permute-start(f32[80,8,128]{2,1,0:T(8,128)S(1)} %get-tuple-element.16.own), channel_id=1, source_target_pairs={{1,2},{2,1},{3,4},{4,3},{5,6},{6,5},{7,8},{8,7},{9,10},{10,9},{11,... | collective-permute-start | bytes 983048 | tf_op jit(solution)/shard_map/ppermute | solution.py:454
  45.0 4.7 %collective-permute-start = (f32[80,8,128]{2,1,0:T(8,128)S(1)}, f32[80,8,128]{2,1,0:T(8,128)S(1)}, u32[]{:S(2)}, u32[]{:S(2)}) collective-permute-start(f32[80,8,128]{2,1,0:T(8,128)S(1)} %get-tuple-element.16.own), channel_id=1, source_target_pairs={{0,1},{1,0},{2,3},{3,2},{4,5},{5,4},{6,7},{7,6},{8,9},{9,8},{10,11... | collective-permute-start | bytes 983048 | tf_op jit(solution)/shard_map/ppermute | solution.py:452
  56.1 18.7 %copy-start = (f32[32,8,128]{2,1,0:T(8,128)S(1)}, f32[32,8,128]{2,1,0:T(8,128)}, u32[]{:S(2)}) copy-start(f32[32,8,128]{2,1,0:T(8,128)} %get-tuple-element.24.flow) | copy-start | bytes 393220
  75.7 8.9 %collective-permute-start.4 = (f32[20,8,128]{2,1,0:T(8,128)S(1)}, f32[20,8,128]{2,1,0:T(8,128)S(1)}, u32[]{:S(2)}, u32[]{:S(2)}) collective-permute-start(f32[20,8,128]{2,1,0:T(8,128)S(1)} %get-tuple-element.26), channel_id=1, source_target_pairs={{0,1},{1,0},{2,3},{3,2},{4,5},{5,4},{6,7},{7,6},{8,9},{9,8},{10,11... | collective-permute-start | bytes 245768 | tf_op jit(solution)/shard_map/ppermute | solution.py:461
  79.8 6.0 %collective-permute-start.5 = (f32[20,8,128]{2,1,0:T(8,128)S(1)}, f32[20,8,128]{2,1,0:T(8,128)S(1)}, u32[]{:S(2)}, u32[]{:S(2)}) collective-permute-start(f32[20,8,128]{2,1,0:T(8,128)S(1)} %get-tuple-element.27), channel_id=1, source_target_pairs={{1,2},{2,1},{3,4},{4,3},{5,6},{6,5},{7,8},{8,7},{9,10},{10,9},{11,... | collective-permute-start | bytes 245768 | tf_op jit(solution)/shard_map/ppermute | solution.py:462

commit v7 on v3

--- a/solution.py
+++ b/solution.py
@@ -86,13 +86,55 @@
                 flow[c * ROWS + y0 + y] = value
 
 
-def cycle_kernel(meta, mate, cur, other, out, ua, ub, vv, src, gg, ff, init, xa, xb, yy, cc):
+def fold(own, out, parity):
+    sub, near = sublanes(), lanes() // HALF == parity
+    for m in range(10):
+        tails = []
+        for h in range(2):
+            at = (2 * m + h) * 8
+            x = [jnp.where(parity == 0, own[at + z], own[at + 7 - z]) for z in range(8)]
+            for z in range(5):
+                value = x[z]
+                if 0 < z < 4:
+                    both = jnp.where(sub <= 7 - z, value, pltpu.roll(x[8 - z], 8 - z, 0))
+                    value = jnp.where(near, value, both)
+                out[13 * m + 5 * h + z] = value
+            tails.append(x[5:])
+        for z in range(3):
+            out[13 * m + 10 + z] = jnp.where(near, tails[0][z], pltpu.roll(tails[1][z], HALF, 1))
+
+
+def unfold(folded, at):
+    x = [folded[13 * (at // 2) + 5 * (at % 2) + z] for z in range(5)]
+    tail = [folded[13 * (at // 2) + 10 + z] for z in range(3)]
+    near = x + ([pltpu.roll(t, HALF, 1) for t in tail] if at % 2 else tail)
+    far = x + [pltpu.roll(x[8 - z], 8 - z, 0) for z in range(5, 8)]
+    return near, far
+
+
+def sort_kernel(meta, cur, own, to_other, to_mate):
+    for k in range(GROUP):
+        for a in range(5):
+            values = swap8([cur[(4 * j + k) * 5 + a] for j in range(8)])
+            to = k
+            if a < 3:
+                to = (k + 1) % GROUP
+                if to == 0:
+                    values = [pltpu.roll(value, 1, 0) for value in values]
+            for y in range(8):
+                own[(to * 5 + a) * 8 + y] = values[y]
+    parity = meta[0] % 2
+    fold(own, to_other, parity)
+    fold(own, to_mate, 1 - parity)
+
+
+def cycle_kernel(meta, other, cur, mate, out, ua, ub, vv, src, gg, ff, init, xa, xb, yy, cc):
     lane, sub = lanes(), sublanes()
     low = lane < HALF
     sign = jnp.where(low, 1.0, -1.0)
     kappa = time_step * kappa_coupling
     swing = kappa * sign
-    even = meta[0] % 2 == 0
+    here = lane // HALF == meta[0] % 2
     outside = jnp.where(low, meta[0], meta[1] - 1 - meta[0]) == 0
 
     def step(buf, base, k, start, emit, scale=1.0):
@@ -128,15 +170,15 @@
 
     for k in range(GROUP):
         for a in range(5):
-            at = [(4 * j + k) * 5 + a for j in range(8)]
-            own = swap8([cur[i] for i in at])
-            before = swap8([jnp.where(even, other[i], mate[i]) for i in at])
-            after = swap8([jnp.where(even, mate[i], other[i]) for i in at])
+            at = k * 5 + a
+            mine = [cur[at * 8 + y] for y in range(8)]
+            near, far = unfold(other, at)
+            mate_near, mate_far = unfold(mate, at)
             for y in range(8):
                 rows = (
-                    (y, jnp.where(low, before[y], after[7 - y])),
-                    (y + 8, pltpu.roll(jnp.where(low, after[7 - y], before[y]), HALF, 1)),
-                    (y + 16, jnp.where(low, own[y], own[7 - y])),
+                    (y, jnp.where(here, far[7 - y], mate_far[7 - y])),
+                    (y + 8, pltpu.roll(jnp.where(here, mate_near[7 - y], near[7 - y]), HALF, 1)),
+                    (y + 16, jnp.where(low, mine[y], mine[7 - y])),
                 )
                 for r, value in rows:
                     if a == 3:
@@ -147,14 +189,12 @@
                         vv[2 * k + 1, r] = (time_step * sign) * value
                         if k == GROUP - 1:
                             vv[2 * GROUP + 1, r] = (coarsest * sign) * value
-                    elif k == GROUP - 1:
-                        value = pltpu.roll(value, 1, 0)
-                        put(ua, a, r, value)
-                        put(xa, a, r, value)
-                        xb[a, r] = value
-                        init[a, r] = value
                     else:
-                        put(ua, 3 * (k + 1) + a, r, value)
+                        put(ua, 3 * k + a, r, value)
+                        if k == 0:
+                            put(xa, a, r, value)
+                            xb[a, r] = value
+                            init[a, r] = value
 
     def keep_g(r, u, s):
         for c in range(3):
@@ -352,6 +392,10 @@
     return call(cut_kernel, 1, 3, outs, scratch, HBM, 60)(meta, init, ends, vel)
 
 
+def sort(meta, cur):
+    return call(sort_kernel, 1, 1, (f32(160, 8, 128), f32(130, 8, 128), f32(130, 8, 128)))(meta, cur)
+
+
 def cycle(meta, mate, cur, other):
     tall = BAND + 1
     scratch = [
@@ -367,7 +411,7 @@
         buffer(3, BAND, 8, 128),
         buffer(9, tall, 8, 128),
     ]
-    return call(cycle_kernel, 1, 3, f32(96, 8, 128), scratch)(meta, mate, cur, other)
+    return call(cycle_kernel, 1, 3, f32(96, 8, 128), scratch)(meta, other, cur, mate)
 
 
 def begins(meta, tiles, flow):
@@ -396,8 +440,9 @@
     windows, flow = cut(here, initial_state, guessed_ends[0], velocity[0])
     cur = lax.all_to_all(windows.reshape(intervals, 40, 128), "tm", 0, 0)
     cur = cur.reshape(intervals * 5, 8, 128)
-    mate = lax.ppermute(cur, "gy", mates)
-    other = lax.ppermute(cur, "gy", others)
+    cur, to_other, to_mate = sort(slab, cur)
+    other = lax.ppermute(to_other, "gy", others)
+    mate = lax.ppermute(to_mate, "gy", mates)
     tiles = cycle(slab, mate, cur, other)
     tiles = lax.all_to_all(tiles.reshape(intervals, 24, 128), "tm", 0, 0)
     tiles = tiles.reshape(intervals * 3, 8, 128)

time: 86.6 us -> 86.2 us (level)
  blocking collectives: 46.5 us -> 17.9 us
  waiting for transfers between devices: 7.46 us -> 24.8 us
  starting transfers between devices: 17.6 us -> 27.5 us
  Pallas kernels: 13.9 us -> 14.8 us
    all_to_all x1 -> x0, blocking collectives: 29.2 us -> none  [per_device(): cur = lax.all_to_all(windows.reshape(intervals, 40, 128), 'tm', 0, 0)]
    all_to_all x0 -> x1, waiting for transfers between devices: none -> 18.6 us  [per_device(): cur = lax.all_to_all(windows.reshape(intervals, 40, 128), 'tm', 0, 0)]
    all_to_all x0 -> x1, starting transfers between devices: none -> 10.5 us  [per_device(): cur = lax.all_to_all(windows.reshape(intervals, 40, 128), 'tm', 0, 0)]
    ppermute x2, waiting for transfers between devices: 6.25 us -> 5.01 us  [the longest x1 5.01 us: per_device(): other = lax.ppermute(to_other, 'gy', others)]
    pallas_call x1 -> x2, Pallas kernels: 7.92 us -> 8.81 us  [the longest x1 8.03 us: cycle(): call(cycle_kernel, 1, 3, f32(96, 8, 128), scratch)(meta, other, cur, mate)]
  transfers between devices with their start and end apart: 4 -> 5, of which waited for: 2 -> 3; matrix products, arithmetic and copies ran while one was open for 0% -> 0% of each run, Pallas kernels for 1% -> 1%
where the time goes in v7:
time: 86.2 us; the launch traced here: 85.9 us
  starting transfers between devices  27.5 us (32%)
  waiting for transfers between devices  24.8 us (29%)
  blocking collectives  17.9 us (21%)
  Pallas kernels  14.8 us (17%)
    all_to_all x1, waiting for transfers between devices, per_device(): cur = lax.all_to_all(windows.reshape(intervals, 40, 128), 'tm', 0, 0)  18.6 us
    all_to_all x1, blocking collectives, per_device(): tiles = lax.all_to_all(tiles.reshape(intervals, 24, 128), 'tm', 0, 0)  17.9 us
    all_to_all x1, starting transfers between devices, per_device(): cur = lax.all_to_all(windows.reshape(intervals, 40, 128), 'tm', 0, 0)  10.5 us
    pallas_call x1, Pallas kernels, cycle(): call(cycle_kernel, 1, 3, f32(96, 8, 128), scratch)(meta, other, cur, mate)  8.03 us
    ppermute x1, starting transfers between devices, per_device(): other = lax.ppermute(other, 'gy', others)  6.84 us
    ppermute x1, starting transfers between devices, per_device(): other = lax.ppermute(to_other, 'gy', others)  6.34 us
    ppermute x1, waiting for transfers between devices, per_device(): other = lax.ppermute(to_other, 'gy', others)  5.01 us
    pallas_call x1, Pallas kernels, cut(): return call(cut_kernel, 1, 3, outs, scratch, HBM, 60)(meta, init, ends, vel)  2.37 us
  transfers between devices with their start and end apart: 5, of which 3 were waited for; matrix products, arithmetic and copies ran while one was open for 0% of the time, Pallas kernels for 1%

profile of v7, /device:TPU:1, one launch (start us, length us, event | category | flops | bytes accessed | tf_op | source)
XLA Modules:
  0.0 85.9 jit_solution(11051067761075634284)
XLA Ops:
  0.6 2.4 %shard_map.50 = (f32[160,8,128]{2,1,0:T(8,128)}, f32[32,8,128]{2,1,0:T(8,128)}) custom-call(s32[1]{0:T(128)} %bitcast.1.meta, f32[3,16,1024]{2,1,0:T(8,128)} %init_hbm.1, f32[3,16,1024]{2,1,0:T(8,128)} %bitcast.15, f32[2,16,1024]{2,1,0:T(8,128)} %bitcast.18), custom_call_target="tpu_custom_call" | custom-call | tf_op jit(solution)/shard_map/pallas_call | solution.py:392
  3.0 10.5 %all-to-all-start = ((f32[32,40,128]{2,1,0:T(8,128)}), f32[32,40,128]{2,1,0:T(8,128)S(1)}, u32[]{:S(2)}, u32[]{:S(2)}) async-start(f32[32,40,128]{2,1,0:T(8,128)} %bitcast.14), calls=%async_computation | async-start | bytes 1310720 | tf_op jit(solution)/shard_map/all_to_all | solution.py:441
  13.5 0.1 pad_add_fusion.meta
  13.6 18.6 %all-to-all-done = f32[32,40,128]{2,1,0:T(8,128)S(1)} async-done(((f32[32,40,128]{2,1,0:T(8,128)}), f32[32,40,128]{2,1,0:T(8,128)S(1)}, u32[]{:S(2)}, u32[]{:S(2)}) %all-to-all-start) | async-done | bytes 655392 | tf_op jit(solution)/shard_map/all_to_all | solution.py:441
  32.2 0.8 shard_map.51
  33.0 6.3 %collective-permute-start = (f32[130,8,128]{2,1,0:T(8,128)S(1)}, f32[130,8,128]{2,1,0:T(8,128)S(1)}, u32[]{:S(2)}, u32[]{:S(2)}) collective-permute-start(f32[130,8,128]{2,1,0:T(8,128)S(1)} %get-tuple-element.11), channel_id=1, source_target_pairs={{1,2},{2,1},{3,4},{4,3},{5,6},{6,5},{7,8},{8,7},{9,10},{10,9},{11,... | collective-permute-start | bytes 1597448 | tf_op jit(solution)/shard_map/ppermute | solution.py:444
  39.4 1.9 %collective-permute-start.1 = (f32[130,8,128]{2,1,0:T(8,128)S(1)}, f32[130,8,128]{2,1,0:T(8,128)S(1)}, u32[]{:S(2)}, u32[]{:S(2)}) collective-permute-start(f32[130,8,128]{2,1,0:T(8,128)S(1)} %get-tuple-element.13), channel_id=1, source_target_pairs={{0,1},{1,0},{2,3},{3,2},{4,5},{5,4},{6,7},{7,6},{8,9},{9,8},{10,11... | collective-permute-start | bytes 1597448 | tf_op jit(solution)/shard_map/ppermute | solution.py:445
  41.3 5.0 %collective-permute-done.other = f32[130,8,128]{2,1,0:T(8,128)S(1)} collective-permute-done((f32[130,8,128]{2,1,0:T(8,128)S(1)}, f32[130,8,128]{2,1,0:T(8,128)S(1)}, u32[]{:S(2)}, u32[]{:S(2)}) %collective-permute-start) | collective-permute-done | bytes 532512 | tf_op jit(solution)/shard_map/ppermute | solution.py:444
  46.3 0.0 collective-permute-done.1.mate
  46.3 8.0 %shard_map.52 = f32[96,8,128]{2,1,0:T(8,128)S(1)} custom-call(s32[2]{0:T(128)S(1)} %pad_add_fusion.meta, f32[130,8,128]{2,1,0:T(8,128)S(1)} %collective-permute-done.other, f32[160,8,128]{2,1,0:T(8,128)S(1)} %get-tuple-element.12.cur, f32[130,8,128]{2,1,0:T(8,128)S(1)} %collective-permute-done.1.mate), custom_call_target="tpu_custom_call" | custom-call | tf_op jit(solution)/shard_map/pallas_call | solution.py:414
  54.3 0.0 copy-start
  54.4 17.9 %all_to_all.10 = f32[32,24,128]{2,1,0:T(8,128)S(1)} all-to-all(f32[32,24,128]{2,1,0:T(8,128)S(1)} %bitcast.13), channel_id=1, replica_groups=mesh['tm'=32,'gy'=16] {'tm'}, dimensions={0} | all-to-all | bytes 786432 | tf_op jit(solution)/shard_map/all_to_all | solution.py:447
  72.3 0.0 copy-done
  72.3 0.8 shard_map.54
  73.1 1.9 %collective-permute-start.2 = (f32[20,8,128]{2,1,0:T(8,128)S(1)}, f32[20,8,128]{2,1,0:T(8,128)S(1)}, u32[]{:S(2)}, u32[]{:S(2)}) collective-permute-start(f32[20,8,128]{2,1,0:T(8,128)S(1)} %get-tuple-element.16), channel_id=1, source_target_pairs={{0,1},{1,0},{2,3},{3,2},{4,5},{5,4},{6,7},{7,6},{8,9},{9,8},{10,11... | collective-permute-start | bytes 245768 | tf_op jit(solution)/shard_map/ppermute | solution.py:450
  75.0 6.8 %collective-permute-start.3 = (f32[20,8,128]{2,1,0:T(8,128)S(1)}, f32[20,8,128]{2,1,0:T(8,128)S(1)}, u32[]{:S(2)}, u32[]{:S(2)}) collective-permute-start(f32[20,8,128]{2,1,0:T(8,128)S(1)} %get-tuple-element.17), channel_id=1, source_target_pairs={{1,2},{2,1},{3,4},{4,3},{5,6},{6,5},{7,8},{8,7},{9,10},{10,9},{11,... | collective-permute-start | bytes 245768 | tf_op jit(solution)/shard_map/ppermute | solution.py:451
  81.8 0.9 %shard_map.53 = f32[3,16,1024]{2,1,0:T(8,128)} custom-call(f32[96,8,128]{2,1,0:T(8,128)S(1)} %bitcast.11), custom_call_target="tpu_custom_call" | custom-call | tf_op jit(solution)/shard_map/pallas_call | solution.py:423
  82.7 0.0 collective-permute-done.2.mate
  82.7 1.2 %collective-permute-done.3.other = f32[20,8,128]{2,1,0:T(8,128)S(1)} collective-permute-done((f32[20,8,128]{2,1,0:T(8,128)S(1)}, f32[20,8,128]{2,1,0:T(8,128)S(1)}, u32[]{:S(2)}, u32[]{:S(2)}) %collective-permute-start.3) | collective-permute-done | bytes 81952 | tf_op jit(solution)/shard_map/ppermute | solution.py:451
  84.0 1.9 %shard_map.55 = f32[3,16,1024]{2,1,0:T(8,128)} custom-call(s32[2]{0:T(128)S(1)} %pad_add_fusion.meta, f32[48,8,128]{2,1,0:T(8,128)S(1)} %get-tuple-element.15.mid, f32[32,8,128]{2,1,0:T(8,128)S(1)} %copy-done, f32[20,8,128]{2,1,0:T(8,128)S(1)} %collective-permute-done.2.mate, f32[20,8,128]{2,1,0:T(8,128)S(1)} %collective-permute-done.3.other), custom_call_target="tpu_custom_call" | custom-call | tf_op jit(solution)/shard_map/pallas_call | solution.py:429
Async XLA Ops:
  3.0 29.2 %all-to-all-start = ((f32[32,40,128]{2,1,0:T(8,128)}), f32[32,40,128]{2,1,0:T(8,128)S(1)}, u32[]{:S(2)}, u32[]{:S(2)}) async-start(f32[32,40,128]{2,1,0:T(8,128)} %bitcast.14), calls=%async_computation | async-start | bytes 1310720 | tf_op jit(solution)/shard_map/all_to_all | solution.py:441
  33.0 13.3 %collective-permute-start = (f32[130,8,128]{2,1,0:T(8,128)S(1)}, f32[130,8,128]{2,1,0:T(8,128)S(1)}, u32[]{:S(2)}, u32[]{:S(2)}) collective-permute-start(f32[130,8,128]{2,1,0:T(8,128)S(1)} %get-tuple-element.11), channel_id=1, source_target_pairs={{1,2},{2,1},{3,4},{4,3},{5,6},{6,5},{7,8},{8,7},{9,10},{10,9},{11,... | collective-permute-start | bytes 1597448 | tf_op jit(solution)/shard_map/ppermute | solution.py:444
  39.4 6.9 %collective-permute-start.1 = (f32[130,8,128]{2,1,0:T(8,128)S(1)}, f32[130,8,128]{2,1,0:T(8,128)S(1)}, u32[]{:S(2)}, u32[]{:S(2)}) collective-permute-start(f32[130,8,128]{2,1,0:T(8,128)S(1)} %get-tuple-element.13), channel_id=1, source_target_pairs={{0,1},{1,0},{2,3},{3,2},{4,5},{5,4},{6,7},{7,6},{8,9},{9,8},{10,11... | collective-permute-start | bytes 1597448 | tf_op jit(solution)/shard_map/ppermute | solution.py:445
  54.3 18.0 %copy-start = (f32[32,8,128]{2,1,0:T(8,128)S(1)}, f32[32,8,128]{2,1,0:T(8,128)}, u32[]{:S(2)}) copy-start(f32[32,8,128]{2,1,0:T(8,128)} %get-tuple-element.14.flow) | copy-start | bytes 393220
  73.1 9.7 %collective-permute-start.2 = (f32[20,8,128]{2,1,0:T(8,128)S(1)}, f32[20,8,128]{2,1,0:T(8,128)S(1)}, u32[]{:S(2)}, u32[]{:S(2)}) collective-permute-start(f32[20,8,128]{2,1,0:T(8,128)S(1)} %get-tuple-element.16), channel_id=1, source_target_pairs={{0,1},{1,0},{2,3},{3,2},{4,5},{5,4},{6,7},{7,6},{8,9},{9,8},{10,11... | collective-permute-start | bytes 245768 | tf_op jit(solution)/shard_map/ppermute | solution.py:450
  75.0 9.0 %collective-permute-start.3 = (f32[20,8,128]{2,1,0:T(8,128)S(1)}, f32[20,8,128]{2,1,0:T(8,128)S(1)}, u32[]{:S(2)}, u32[]{:S(2)}) collective-permute-start(f32[20,8,128]{2,1,0:T(8,128)S(1)} %get-tuple-element.17), channel_id=1, source_target_pairs={{1,2},{2,1},{3,4},{4,3},{5,6},{6,5},{7,8},{8,7},{9,10},{10,9},{11,... | collective-permute-start | bytes 245768 | tf_op jit(solution)/shard_map/ppermute | solution.py:451

commit v8 on v7

--- a/solution.py
+++ b/solution.py
@@ -21,7 +21,14 @@
 
 VMEM = pl.BlockSpec(memory_space=pltpu.VMEM)
 HBM = pl.BlockSpec(memory_space=pltpu.HBM)
-SMEM = pl.BlockSpec(memory_space=pltpu.SMEM)
+
+
+def slab():
+    return lax.axis_index("gy")
+
+
+def slabs():
+    return lax.axis_size("gy")
 
 
 def lanes():
@@ -56,7 +63,7 @@
     return out
 
 
-def cut_kernel(meta, init_hbm, ends_hbm, vel_hbm, out, flow, init, ends, vel, sems):
+def cut_kernel(init_hbm, ends_hbm, vel_hbm, out, flow, init, ends, vel, sems):
     copies = [
         pltpu.make_async_copy(far, near, sems.at[i])
         for i, (far, near) in enumerate(((init_hbm, init), (ends_hbm, ends), (vel_hbm, vel)))
@@ -65,7 +72,7 @@
         copy.start()
     for copy in copies:
         copy.wait()
-    last = meta[0] == GROUP * GROUPS - 1
+    last = lax.axis_index("tm") == GROUP * GROUPS - 1
     low = lanes() < HALF
     for a in range(5):
         if a < 3:
@@ -112,7 +119,7 @@
     return near, far
 
 
-def sort_kernel(meta, cur, own, to_other, to_mate):
+def sort_kernel(cur, own, to_other, to_mate):
     for k in range(GROUP):
         for a in range(5):
             values = swap8([cur[(4 * j + k) * 5 + a] for j in range(8)])
@@ -123,22 +130,22 @@
                     values = [pltpu.roll(value, 1, 0) for value in values]
             for y in range(8):
                 own[(to * 5 + a) * 8 + y] = values[y]
-    parity = meta[0] % 2
+    parity = slab() % 2
     fold(own, to_other, parity)
     fold(own, to_mate, 1 - parity)
 
 
-def cycle_kernel(meta, other, cur, mate, out, ua, ub, vv, src, gg, ff, init, xa, xb, yy, cc):
+def cycle_kernel(other, cur, mate, out, ua, ub, vv, src, gg, ff, init, xa, xb, yy, cc):
     lane, sub = lanes(), sublanes()
     low = lane < HALF
     sign = jnp.where(low, 1.0, -1.0)
     kappa = time_step * kappa_coupling
     swing = kappa * sign
-    here = lane // HALF == meta[0] % 2
-    outside = jnp.where(low, meta[0], meta[1] - 1 - meta[0]) == 0
+    here = lane // HALF == slab() % 2
+    outside = jnp.where(low, slab(), slabs() - 1 - slab()) == 0
 
     def step(buf, base, k, start, emit, scale=1.0):
-        pl.when(meta[1] > 0)(lambda: sweep(buf, base, k, start, emit, scale))
+        pl.when(slab() >= 0)(lambda: sweep(buf, base, k, start, emit, scale))
 
     def sweep(buf, base, k, start, emit, scale):
         rows, climbs = {}, {}
@@ -289,8 +296,8 @@
     return value
 
 
-def begin_kernel(meta, tiles, flow, begin, mate, other):
-    even = meta[0] % 2 == 0
+def begin_kernel(tiles, flow, begin, mate, other):
+    even = slab() % 2 == 0
     for c in range(5):
         if c < 3:
             rows = []
@@ -314,11 +321,11 @@
             own[c, 8:16, at] = gathered(tiles, c, b, 1)
 
 
-def relax_kernel(meta, mid, flow, mate, other, out, wa, wb, vv):
+def relax_kernel(mid, flow, mate, other, out, wa, wb, vv):
     lane = lanes()
     tall = ROWS + 2 * FINE
     kappa = time_step * kappa_coupling
-    even = meta[0] % 2 == 0
+    even = slab() % 2 == 0
     for a in range(5):
         src, buf, at = (mid, wa, a) if a < 3 else (flow, vv, a - 3)
         scale = 1.0 if a < 3 else time_step
@@ -329,7 +336,7 @@
         for r in range(ROWS):
             buf[at * tall + FINE + r] = scale * src[at * ROWS + r]
 
-    bottom, top = meta[0] == 0, meta[0] == meta[1] - 1
+    bottom, top = slab() == 0, slab() == slabs() - 1
     def sweep(section, buf, to):
         rows = {r: [buf[c * tall + r] for c in range(3)] for r in range(section, tall - section)}
         climbs = {r: [x - y for x, y in zip(rows[r + 1], rows[r])] for r in range(section, tall - section - 1)}
@@ -373,30 +380,30 @@
     return pltpu.VMEM(shape, jnp.float32)
 
 
-def call(kernel, n_scalars, n_arrays, outs, scratch=(), space=VMEM, mib=24):
+def call(kernel, n_arrays, outs, scratch=(), space=VMEM, mib=24):
     many = isinstance(outs, tuple)
     return pl.pallas_call(
         kernel,
         out_shape=outs,
-        in_specs=[SMEM] * n_scalars + [space] * n_arrays,
+        in_specs=[space] * n_arrays,
         out_specs=(VMEM,) * len(outs) if many else VMEM,
         scratch_shapes=list(scratch),
         compiler_params=pltpu.CompilerParams(vmem_limit_bytes=mib * 1024 * 1024),
     )
 
 
-def cut(meta, init, ends, vel):
+def cut(init, ends, vel):
     state, flow = buffer(3, ROWS, 1024), buffer(2, ROWS, 1024)
     scratch = [state, state, flow, pltpu.SemaphoreType.DMA((3,))]
     outs = (f32(160, 8, 128), f32(2 * ROWS, 8, 128))
-    return call(cut_kernel, 1, 3, outs, scratch, HBM, 60)(meta, init, ends, vel)
-
-
-def sort(meta, cur):
-    return call(sort_kernel, 1, 1, (f32(160, 8, 128), f32(130, 8, 128), f32(130, 8, 128)))(meta, cur)
-
-
-def cycle(meta, mate, cur, other):
+    return call(cut_kernel, 3, outs, scratch, HBM, 60)(init, ends, vel)
+
+
+def sort(cur):
+    return call(sort_kernel, 1, (f32(160, 8, 128), f32(130, 8, 128), f32(130, 8, 128)))(cur)
+
+
+def cycle(mate, cur, other):
     tall = BAND + 1
     scratch = [
         buffer(12, tall, 8, 128),
@@ -411,22 +418,22 @@
         buffer(3, BAND, 8, 128),
         buffer(9, tall, 8, 128),
     ]
-    return call(cycle_kernel, 1, 3, f32(96, 8, 128), scratch)(meta, other, cur, mate)
-
-
-def begins(meta, tiles, flow):
+    return call(cycle_kernel, 3, f32(96, 8, 128), scratch)(other, cur, mate)
+
+
+def begins(tiles, flow):
     halo = f32(5 * FINE, 8, 128)
-    return call(begin_kernel, 1, 2, (f32(3 * ROWS, 8, 128), halo, halo))(meta, tiles, flow)
+    return call(begin_kernel, 2, (f32(3 * ROWS, 8, 128), halo, halo))(tiles, flow)
 
 
 def owns(tiles):
-    return call(own_kernel, 0, 1, f32(3, ROWS, 1024))(tiles)
-
-
-def relax(meta, mid, flow, mate, other):
+    return call(own_kernel, 1, f32(3, ROWS, 1024))(tiles)
+
+
+def relax(mid, flow, mate, other):
     tall = ROWS + 2 * FINE
     scratch = [buffer(3 * tall, 8, 128), buffer(3 * tall, 8, 128), buffer(2 * tall, 8, 128)]
-    return call(relax_kernel, 1, 4, f32(3, ROWS, 1024), scratch)(meta, mid, flow, mate, other)
+    return call(relax_kernel, 4, f32(3, ROWS, 1024), scratch)(mid, flow, mate, other)
 
 
 def per_device(initial_state, guessed_ends, velocity):
@@ -434,23 +441,21 @@
     mates = [(i, i ^ 1) for i in range(slabs)]
     others = [(i, i + 1 if i % 2 else i - 1) for i in range(1, slabs - 1)]
     intervals = lax.axis_size("tm")
-    here = lax.axis_index("tm").astype(jnp.int32).reshape(1)
-    slab = jnp.stack([lax.axis_index("gy").astype(jnp.int32), jnp.int32(slabs)])
-
-    windows, flow = cut(here, initial_state, guessed_ends[0], velocity[0])
+
+    windows, flow = cut(initial_state, guessed_ends[0], velocity[0])
     cur = lax.all_to_all(windows.reshape(intervals, 40, 128), "tm", 0, 0)
     cur = cur.reshape(intervals * 5, 8, 128)
-    cur, to_other, to_mate = sort(slab, cur)
+    cur, to_other, to_mate = sort(cur)
     other = lax.ppermute(to_other, "gy", others)
     mate = lax.ppermute(to_mate, "gy", mates)
-    tiles = cycle(slab, mate, cur, other)
+    tiles = cycle(mate, cur, other)
     tiles = lax.all_to_all(tiles.reshape(intervals, 24, 128), "tm", 0, 0)
     tiles = tiles.reshape(intervals * 3, 8, 128)
-    mid, mate, other = begins(slab, tiles, flow)
+    mid, mate, other = begins(tiles, flow)
     mate = lax.ppermute(mate, "gy", mates)
     other = lax.ppermute(other, "gy", others)
     own = owns(tiles)
-    relaxed = relax(slab, mid, flow, mate, other)
+    relaxed = relax(mid, flow, mate, other)
     return own[None], relaxed[None]
 
 

time: 86.2 us -> 83.8 us (0.972)
  blocking collectives: 17.9 us -> 47.1 us
  waiting for transfers between devices: 24.8 us -> 6.23 us
  starting transfers between devices: 27.5 us -> 17 us
  Pallas kernels: 14.8 us -> 12.3 us
    all_to_all x0 -> x1, blocking collectives: none -> 29.2 us  [per_device(): cur = lax.all_to_all(windows.reshape(intervals, 40, 128), 'tm', 0, 0)]
    all_to_all x1 -> x0, waiting for transfers between devices: 18.6 us -> none  [per_device(): cur = lax.all_to_all(windows.reshape(intervals, 40, 128), 'tm', 0, 0)]
    all_to_all x1 -> x0, starting transfers between devices: 10.5 us -> none  [per_device(): cur = lax.all_to_all(windows.reshape(intervals, 40, 128), 'tm', 0, 0)]
    pallas_call x6, Pallas kernels: 14.8 us -> 12.3 us  [the longest x1 7.18 us: cycle(): return call(cycle_kernel, 3, f32(96, 8, 128), scratch)(other, cur, mate)]
  transfers between devices with their start and end apart: 5 -> 4, of which waited for: 3 -> 2; matrix products, arithmetic and copies ran while one was open for 0% -> 0% of each run, Pallas kernels for 1% -> 1%
where the time goes in v8:
time: 83.8 us; the launch traced here: 83.4 us
  blocking collectives  47.1 us (56%)
  starting transfers between devices  17 us (20%)
  Pallas kernels  12.3 us (15%)
  waiting for transfers between devices  6.23 us (7%)
    all_to_all x1, blocking collectives, per_device(): cur = lax.all_to_all(windows.reshape(intervals, 40, 128), 'tm', 0, 0)  29.2 us
    all_to_all x1, blocking collectives, per_device(): tiles = lax.all_to_all(tiles.reshape(intervals, 24, 128), 'tm', 0, 0)  17.9 us
    pallas_call x1, Pallas kernels, cycle(): return call(cycle_kernel, 3, f32(96, 8, 128), scratch)(other, cur, mate)  7.18 us
    ppermute x1, starting transfers between devices, per_device(): other = lax.ppermute(other, 'gy', others)  6.84 us
    ppermute x1, starting transfers between devices, per_device(): other = lax.ppermute(to_other, 'gy', others)  6.34 us
    ppermute x1, waiting for transfers between devices, per_device(): other = lax.ppermute(to_other, 'gy', others)  5.01 us
    pallas_call x1, Pallas kernels, cut(): return call(cut_kernel, 3, outs, scratch, HBM, 60)(init, ends, vel)  2.37 us
    ppermute x1, starting transfers between devices, per_device(): mate = lax.ppermute(to_mate, 'gy', mates)  1.92 us
  transfers between devices with their start and end apart: 4, of which 2 were waited for; matrix products, arithmetic and copies ran while one was open for 0% of the time, Pallas kernels for 1%

profile of v8, /device:TPU:1, one launch (start us, length us, event | category | flops | bytes accessed | tf_op | source)
XLA Modules:
  0.0 83.4 jit_solution(17433012257162189376)
XLA Ops:
  0.6 2.4 %shard_map.50 = (f32[160,8,128]{2,1,0:T(8,128)}, f32[32,8,128]{2,1,0:T(8,128)}) custom-call(f32[3,16,1024]{2,1,0:T(8,128)} %init_hbm.1, f32[3,16,1024]{2,1,0:T(8,128)} %bitcast.13, f32[2,16,1024]{2,1,0:T(8,128)} %bitcast.16), custom_call_target="tpu_custom_call" | custom-call | tf_op jit(solution)/shard_map/pallas_call | solution.py:399
  3.0 29.2 %all_to_all.10 = f32[32,40,128]{2,1,0:T(8,128)S(1)} all-to-all(f32[32,40,128]{2,1,0:T(8,128)} %bitcast.12), channel_id=1, replica_groups=mesh['tm'=32,'gy'=16] {'tm'}, dimensions={0} | all-to-all | bytes 1310720 | tf_op jit(solution)/shard_map/all_to_all | solution.py:446
  32.2 0.2 shard_map.51
  32.5 6.3 %collective-permute-start = (f32[130,8,128]{2,1,0:T(8,128)S(1)}, f32[130,8,128]{2,1,0:T(8,128)S(1)}, u32[]{:S(2)}, u32[]{:S(2)}) collective-permute-start(f32[130,8,128]{2,1,0:T(8,128)S(1)} %get-tuple-element.11), channel_id=1, source_target_pairs={{1,2},{2,1},{3,4},{4,3},{5,6},{6,5},{7,8},{8,7},{9,10},{10,9},{11,... | collective-permute-start | bytes 1597448 | tf_op jit(solution)/shard_map/ppermute | solution.py:449
  38.8 1.9 %collective-permute-start.1 = (f32[130,8,128]{2,1,0:T(8,128)S(1)}, f32[130,8,128]{2,1,0:T(8,128)S(1)}, u32[]{:S(2)}, u32[]{:S(2)}) collective-permute-start(f32[130,8,128]{2,1,0:T(8,128)S(1)} %get-tuple-element.13), channel_id=1, source_target_pairs={{0,1},{1,0},{2,3},{3,2},{4,5},{5,4},{6,7},{7,6},{8,9},{9,8},{10,11... | collective-permute-start | bytes 1597448 | tf_op jit(solution)/shard_map/ppermute | solution.py:450
  40.7 5.0 %collective-permute-done.other = f32[130,8,128]{2,1,0:T(8,128)S(1)} collective-permute-done((f32[130,8,128]{2,1,0:T(8,128)S(1)}, f32[130,8,128]{2,1,0:T(8,128)S(1)}, u32[]{:S(2)}, u32[]{:S(2)}) %collective-permute-start) | collective-permute-done | bytes 532512 | tf_op jit(solution)/shard_map/ppermute | solution.py:449
  45.8 0.0 collective-permute-done.1.mate
  45.8 7.2 %shard_map.52 = f32[96,8,128]{2,1,0:T(8,128)S(1)} custom-call(f32[130,8,128]{2,1,0:T(8,128)S(1)} %collective-permute-done.other, f32[160,8,128]{2,1,0:T(8,128)S(1)} %get-tuple-element.12.cur, f32[130,8,128]{2,1,0:T(8,128)S(1)} %collective-permute-done.1.mate), custom_call_target="tpu_custom_call" | custom-call | tf_op jit(solution)/shard_map/pallas_call | solution.py:421
  52.9 0.0 copy-start
  53.0 17.9 %all_to_all.11 = f32[32,24,128]{2,1,0:T(8,128)S(1)} all-to-all(f32[32,24,128]{2,1,0:T(8,128)S(1)} %bitcast.11), channel_id=1, replica_groups=mesh['tm'=32,'gy'=16] {'tm'}, dimensions={0} | all-to-all | bytes 786432 | tf_op jit(solution)/shard_map/all_to_all | solution.py:452
  70.9 0.0 copy-done
  70.9 0.2 shard_map.54
  71.1 1.9 %collective-permute-start.2 = (f32[20,8,128]{2,1,0:T(8,128)S(1)}, f32[20,8,128]{2,1,0:T(8,128)S(1)}, u32[]{:S(2)}, u32[]{:S(2)}) collective-permute-start(f32[20,8,128]{2,1,0:T(8,128)S(1)} %get-tuple-element.16), channel_id=1, source_target_pairs={{0,1},{1,0},{2,3},{3,2},{4,5},{5,4},{6,7},{7,6},{8,9},{9,8},{10,11... | collective-permute-start | bytes 245768 | tf_op jit(solution)/shard_map/ppermute | solution.py:455
  73.1 6.8 %collective-permute-start.3 = (f32[20,8,128]{2,1,0:T(8,128)S(1)}, f32[20,8,128]{2,1,0:T(8,128)S(1)}, u32[]{:S(2)}, u32[]{:S(2)}) collective-permute-start(f32[20,8,128]{2,1,0:T(8,128)S(1)} %get-tuple-element.17), channel_id=1, source_target_pairs={{1,2},{2,1},{3,4},{4,3},{5,6},{6,5},{7,8},{8,7},{9,10},{10,9},{11,... | collective-permute-start | bytes 245768 | tf_op jit(solution)/shard_map/ppermute | solution.py:456
  79.9 0.9 %shard_map.53 = f32[3,16,1024]{2,1,0:T(8,128)} custom-call(f32[96,8,128]{2,1,0:T(8,128)S(1)} %bitcast.9), custom_call_target="tpu_custom_call" | custom-call | tf_op jit(solution)/shard_map/pallas_call | solution.py:430
  80.8 0.0 collective-permute-done.2.mate
  80.8 1.2 %collective-permute-done.3.other = f32[20,8,128]{2,1,0:T(8,128)S(1)} collective-permute-done((f32[20,8,128]{2,1,0:T(8,128)S(1)}, f32[20,8,128]{2,1,0:T(8,128)S(1)}, u32[]{:S(2)}, u32[]{:S(2)}) %collective-permute-start.3) | collective-permute-done | bytes 81952 | tf_op jit(solution)/shard_map/ppermute | solution.py:456
  82.0 1.4 %shard_map.55 = f32[3,16,1024]{2,1,0:T(8,128)} custom-call(f32[48,8,128]{2,1,0:T(8,128)S(1)} %get-tuple-element.15.mid, f32[32,8,128]{2,1,0:T(8,128)S(1)} %copy-done, f32[20,8,128]{2,1,0:T(8,128)S(1)} %collective-permute-done.2.mate, f32[20,8,128]{2,1,0:T(8,128)S(1)} %collective-permute-done.3.other), custom_call_target="tpu_custom_call" | custom-call | tf_op jit(solution)/shard_map/pallas_call | solution.py:436
Async XLA Ops:
  32.5 13.3 %collective-permute-start = (f32[130,8,128]{2,1,0:T(8,128)S(1)}, f32[130,8,128]{2,1,0:T(8,128)S(1)}, u32[]{:S(2)}, u32[]{:S(2)}) collective-permute-start(f32[130,8,128]{2,1,0:T(8,128)S(1)} %get-tuple-element.11), channel_id=1, source_target_pairs={{1,2},{2,1},{3,4},{4,3},{5,6},{6,5},{7,8},{8,7},{9,10},{10,9},{11,... | collective-permute-start | bytes 1597448 | tf_op jit(solution)/shard_map/ppermute | solution.py:449
  38.8 6.9 %collective-permute-start.1 = (f32[130,8,128]{2,1,0:T(8,128)S(1)}, f32[130,8,128]{2,1,0:T(8,128)S(1)}, u32[]{:S(2)}, u32[]{:S(2)}) collective-permute-start(f32[130,8,128]{2,1,0:T(8,128)S(1)} %get-tuple-element.13), channel_id=1, source_target_pairs={{0,1},{1,0},{2,3},{3,2},{4,5},{5,4},{6,7},{7,6},{8,9},{9,8},{10,11... | collective-permute-start | bytes 1597448 | tf_op jit(solution)/shard_map/ppermute | solution.py:450
  52.9 18.0 %copy-start = (f32[32,8,128]{2,1,0:T(8,128)S(1)}, f32[32,8,128]{2,1,0:T(8,128)}, u32[]{:S(2)}) copy-start(f32[32,8,128]{2,1,0:T(8,128)} %get-tuple-element.14.flow) | copy-start | bytes 393220
  71.1 9.7 %collective-permute-start.2 = (f32[20,8,128]{2,1,0:T(8,128)S(1)}, f32[20,8,128]{2,1,0:T(8,128)S(1)}, u32[]{:S(2)}, u32[]{:S(2)}) collective-permute-start(f32[20,8,128]{2,1,0:T(8,128)S(1)} %get-tuple-element.16), channel_id=1, source_target_pairs={{0,1},{1,0},{2,3},{3,2},{4,5},{5,4},{6,7},{7,6},{8,9},{9,8},{10,11... | collective-permute-start | bytes 245768 | tf_op jit(solution)/shard_map/ppermute | solution.py:455
  73.1 9.0 %collective-permute-start.3 = (f32[20,8,128]{2,1,0:T(8,128)S(1)}, f32[20,8,128]{2,1,0:T(8,128)S(1)}, u32[]{:S(2)}, u32[]{:S(2)}) collective-permute-start(f32[20,8,128]{2,1,0:T(8,128)S(1)} %get-tuple-element.17), channel_id=1, source_target_pairs={{1,2},{2,1},{3,4},{4,3},{5,6},{6,5},{7,8},{8,7},{9,10},{10,9},{11,... | collective-permute-start | bytes 245768 | tf_op jit(solution)/shard_map/ppermute | solution.py:456

commit v9 on v8

--- a/solution.py
+++ b/solution.py
@@ -135,19 +135,33 @@
     fold(own, to_mate, 1 - parity)
 
 
-def cycle_kernel(other, cur, mate, out, ua, ub, vv, src, gg, ff, init, xa, xb, yy, cc):
-    lane, sub = lanes(), sublanes()
-    low = lane < HALF
+class Rows:
+    def __init__(self, lower, upper, edge):
+        self.lower, self.upper, self.edge = lower, upper, edge
+
+    def __getitem__(self, at):
+        i, r = at
+        return self.upper[i, r - HALO] if r >= self.edge else self.lower[i, r]
+
+    def __setitem__(self, at, value):
+        i, r = at
+        if r >= self.edge:
+            self.upper[i, r - HALO] = value
+        else:
+            self.lower[i, r] = value
+
+
+def tools():
+    low = lanes() < HALF
     sign = jnp.where(low, 1.0, -1.0)
     kappa = time_step * kappa_coupling
     swing = kappa * sign
-    here = lane // HALF == slab() % 2
     outside = jnp.where(low, slab(), slabs() - 1 - slab()) == 0
 
-    def step(buf, base, k, start, emit, scale=1.0):
-        pl.when(slab() >= 0)(lambda: sweep(buf, base, k, start, emit, scale))
-
-    def sweep(buf, base, k, start, emit, scale):
+    def step(*arguments):
+        pl.when(slab() * slab() >= slab())(lambda: sweep(*arguments))
+
+    def sweep(buf, base, flow, at, start, stop, emit, scale=1.0):
         rows, climbs = {}, {}
 
         def row(r):
@@ -160,12 +174,12 @@
                 climbs[r] = [x - y for x, y in zip(row(r + 1), row(r))]
             return climbs[r]
 
-        for r in range(start, BAND):
+        for r in range(start, stop):
             u = row(r)
             west = [x - pltpu.roll(x, 1, 1) for x in u]
             east = [pltpu.roll(x, 127, 1) - x for x in u]
-            across = vv[2 * k, r] + (scale * kappa) * u[0]
-            along = vv[2 * k + 1, r] + (scale * swing) * u[1]
+            across = flow[at, r] + (scale * kappa) * u[0]
+            along = flow[at + 1, r] + (scale * swing) * u[1]
             emit(r, u, slope(west, east, climb(r - 1), climb(r), across, along, scale))
 
     def put(buf, at, r, value):
@@ -175,68 +189,92 @@
         if r == BAND - 1:
             buf[at, BAND] = pltpu.roll(value, HALF, 1)
 
+    return low, sign, step, put
+
+
+def keep_flow(vv, k, a, r, value, sign):
+    way = 1.0 if a == 3 else sign
+    vv[2 * k + a - 3, r] = (time_step * way) * value
+    if k == GROUP - 1:
+        vv[2 * GROUP + a - 3, r] = (coarsest * way) * value
+
+
+def fine_steps(states, vv, src_in, src, step, put, spans):
+    def member(k, carry):
+        base = 3 * k
+
+        def opening(r, u, s):
+            for c in range(3):
+                put(states[1], base + c, r, u[c] + s[c])
+                src_in[base + c, r] = u[c] + float(FINE) * s[c]
+
+        def onward(buf):
+            def emit(r, u, s):
+                for c in range(3):
+                    put(buf, base + c, r, u[c] + s[c])
+
+            return emit
+
+        def closing(r, u, s):
+            for c in range(3):
+                end = u[c] + s[c]
+                put(states[4], base + c, r, end)
+                src[base + c, r] = end - src_in[base + c, r]
+
+        emits = (opening, onward(states[2]), onward(states[3]), closing)
+        for i, (emit, span) in enumerate(zip(emits, spans)):
+            step(states[i], base, vv, 2 * k, *span, emit)
+        return carry
+
+    lax.fori_loop(0, GROUP, member, 0)
+
+
+def early_kernel(cur, e0, e1, e2, e3, e4, vv, src):
+    low, sign, step, put = tools()
+    states = [Rows(None, x, 0) for x in (e0, e1, e2, e3, e4)]
+    vv, src = Rows(None, vv, 0), Rows(None, src, 0)
     for k in range(GROUP):
         for a in range(5):
-            at = k * 5 + a
-            mine = [cur[at * 8 + y] for y in range(8)]
-            near, far = unfold(other, at)
-            mate_near, mate_far = unfold(mate, at)
+            mine = [cur[(k * 5 + a) * 8 + y] for y in range(8)]
+            for y in range(8):
+                value = jnp.where(low, mine[y], mine[7 - y])
+                if a < 3:
+                    put(states[0], 3 * k + a, HALO + y, value)
+                else:
+                    keep_flow(vv, k, a, HALO + y, value, sign)
+    fine_steps(states, vv, src, src, step, put, [(HALO + d, BAND) for d in range(1, 5)])
+
+
+def cycle_kernel(other, mate, e0, e1, e2, e3, e4, ev, es, out, u0, u1, u2, u3, u4, lv, ls, gg, ff, ca, cb, xa, xb, yy, cc):
+    low, sign, step, put = tools()
+    lane, sub = lanes(), sublanes()
+    here = lane // HALF == slab() % 2
+    states = [Rows(u, e, HALO + d) for d, (u, e) in enumerate(zip((u0, u1, u2, u3, u4), (e0, e1, e2, e3, e4)))]
+    vv = Rows(lv, ev, HALO)
+    begin, ends, src = states[0], states[4], Rows(ls, es, HALO + 4)
+
+    for k in range(GROUP):
+        for a in range(5):
+            near, far = unfold(other, k * 5 + a)
+            mate_near, mate_far = unfold(mate, k * 5 + a)
             for y in range(8):
                 rows = (
                     (y, jnp.where(here, far[7 - y], mate_far[7 - y])),
                     (y + 8, pltpu.roll(jnp.where(here, mate_near[7 - y], near[7 - y]), HALF, 1)),
-                    (y + 16, jnp.where(low, mine[y], mine[7 - y])),
                 )
                 for r, value in rows:
-                    if a == 3:
-                        vv[2 * k, r] = time_step * value
-                        if k == GROUP - 1:
-                            vv[2 * GROUP, r] = coarsest * value
-                    elif a == 4:
-                        vv[2 * k + 1, r] = (time_step * sign) * value
-                        if k == GROUP - 1:
-                            vv[2 * GROUP + 1, r] = (coarsest * sign) * value
+                    if a < 3:
+                        put(begin, 3 * k + a, r, value)
                     else:
-                        put(ua, 3 * k + a, r, value)
-                        if k == 0:
-                            put(xa, a, r, value)
-                            xb[a, r] = value
-                            init[a, r] = value
+                        keep_flow(vv, k, a, r, value, sign)
+
+    fine_steps(states, vv, Rows(ls, es, HALO + 1), src, step, put, [(d, HALO + d) for d in range(1, 5)])
 
     def keep_g(r, u, s):
         for c in range(3):
             gg[c, r] = u[c] + s[c]
 
-    step(ua, 0, GROUP, 7, keep_g, float(FINE * GROUP))
-
-    def fine(k, carry):
-        base = 3 * k
-
-        def opening(r, u, s):
-            for c in range(3):
-                put(ub, base + c, r, u[c] + s[c])
-                src[base + c, r] = u[c] + float(FINE) * s[c]
-
-        def onward(buf):
-            def emit(r, u, s):
-                for c in range(3):
-                    put(buf, base + c, r, u[c] + s[c])
-
-            return emit
-
-        def closing(r, u, s):
-            for c in range(3):
-                end = u[c] + s[c]
-                put(ua, base + c, r, end)
-                src[base + c, r] = end - src[base + c, r]
-
-        step(ua, base, k, 1, opening)
-        step(ub, base, k, 2, onward(ua))
-        step(ua, base, k, 3, onward(ub))
-        step(ub, base, k, 4, closing)
-        return carry
-
-    lax.fori_loop(0, GROUP, fine, 0)
+    step(begin, 0, vv, 2 * GROUP, 7, BAND, keep_g, float(FINE * GROUP))
 
     def plus(buf, k, base):
         def emit(r, u, s):
@@ -245,30 +283,32 @@
 
         return emit
 
-    step(ua, 0, 1, 5, plus(ub, 1, 0))
-    step(ub, 0, 2, 6, plus(ua, 2, 0))
+    step(ends, 0, vv, 2, 5, BAND, plus(cb, 1, 0))
+    step(cb, 0, vv, 4, 6, BAND, plus(ca, 2, 0))
 
     def forcing(r, u, s):
         for c in range(3):
             ff[c, r] = u[c] + float(FINE) * s[c] + src[3 * (GROUP - 1) + c, r] - gg[c, r]
 
-    step(ua, 0, GROUP - 1, 7, forcing)
-
+    step(ca, 0, vv, 2 * (GROUP - 1), 7, BAND, forcing)
+
+    for c in range(3):
+        xb[c, 6] = begin[c, 6]
     for t in range(GROUPS):
-        buf, to = (xa, xb) if t % 2 == 0 else (xb, xa)
+        buf, to = (xa if t else begin, xb) if t % 2 == 0 else (xb, xa)
 
         def settle(r, u, s):
             for c in range(3):
                 y = u[c] + s[c] + ff[c, r]
                 if t == GROUPS - 1 and r >= HALO:
                     yy[c, r] = y
-                put(to, c, r, jnp.where(sub == 0, init[c, r], pltpu.roll(y, 1, 0)))
-
-        step(buf, 0, GROUP, max(7, 6 + t), settle, float(FINE * GROUP))
-
-    step(xa, 0, 0, 14, plus(cc, 0, 0))
-    step(cc, 0, 1, 15, plus(cc, 1, 3))
-    step(cc, 3, 2, 16, plus(cc, 2, 6))
+                put(to, c, r, jnp.where(sub == 0, begin[c, r], pltpu.roll(y, 1, 0)))
+
+        step(buf, 0, vv, 2 * GROUP, max(7, 6 + t), BAND, settle, float(FINE * GROUP))
+
+    step(xa, 0, vv, 0, 14, BAND, plus(cc, 0, 0))
+    step(cc, 0, vv, 2, 15, BAND, plus(cc, 1, 3))
+    step(cc, 3, vv, 4, 16, BAND, plus(cc, 2, 6))
 
     def compact(buf, base, c, y):
         m = jnp.where(low, buf[base + c, y + 16], buf[base + c, 23 - y])
@@ -403,22 +443,27 @@
     return call(sort_kernel, 1, (f32(160, 8, 128), f32(130, 8, 128), f32(130, 8, 128)))(cur)
 
 
-def cycle(mate, cur, other):
+def early(cur):
+    top, flat = f32(12, 9, 8, 128), f32(12, 8, 8, 128)
+    return call(early_kernel, 1, (top, top, top, top, top, f32(10, 8, 8, 128), flat))(cur)
+
+
+def cycle(other, mate, *upper):
     tall = BAND + 1
-    scratch = [
-        buffer(12, tall, 8, 128),
-        buffer(12, tall, 8, 128),
-        buffer(10, BAND, 8, 128),
-        buffer(12, BAND, 8, 128),
+    scratch = [buffer(12, HALO + d, 8, 128) for d in range(5)]
+    scratch += [
+        buffer(10, HALO, 8, 128),
+        buffer(12, HALO + 4, 8, 128),
         buffer(3, BAND, 8, 128),
         buffer(3, BAND, 8, 128),
+        buffer(3, tall, 8, 128),
         buffer(3, tall, 8, 128),
         buffer(3, tall, 8, 128),
         buffer(3, tall, 8, 128),
         buffer(3, BAND, 8, 128),
         buffer(9, tall, 8, 128),
     ]
-    return call(cycle_kernel, 3, f32(96, 8, 128), scratch)(other, cur, mate)
+    return call(cycle_kernel, 9, f32(96, 8, 128), scratch)(other, mate, *upper)
 
 
 def begins(tiles, flow):
@@ -448,7 +493,7 @@
     cur, to_other, to_mate = sort(cur)
     other = lax.ppermute(to_other, "gy", others)
     mate = lax.ppermute(to_mate, "gy", mates)
-    tiles = cycle(mate, cur, other)
+    tiles = cycle(other, mate, *early(cur))
     tiles = lax.all_to_all(tiles.reshape(intervals, 24, 128), "tm", 0, 0)
     tiles = tiles.reshape(intervals * 3, 8, 128)
     mid, mate, other = begins(tiles, flow)

time: 83.8 us -> 82.3 us (0.982)
  waiting for transfers between devices: 6.23 us -> 4.54 us
    ppermute x1, waiting for transfers between devices: 5.01 us -> 3.32 us  [per_device(): other = lax.ppermute(to_other, 'gy', others)]
    pallas_call x1 -> x2, Pallas kernels: 7.18 us -> 7.43 us  [the longest x1 5.74 us: cycle(): return call(cycle_kernel, 9, f32(96, 8, 128), scratch)(other, mate, *upper)]
  transfers between devices with their start and end apart: 4 -> 4, of which waited for: 2 -> 2; matrix products, arithmetic and copies ran while one was open for 0% -> 0% of each run, Pallas kernels for 1% -> 3%
where the time goes in v9:
time: 82.3 us; the launch traced here: 82 us
  blocking collectives  47.4 us (58%)
  starting transfers between devices  16.8 us (20%)
  Pallas kernels  12.6 us (15%)
  waiting for transfers between devices  4.54 us (6%)
    all_to_all x1, blocking collectives, per_device(): cur = lax.all_to_all(windows.reshape(intervals, 40, 128), 'tm', 0, 0)  29.2 us
    all_to_all x1, blocking collectives, per_device(): tiles = lax.all_to_all(tiles.reshape(intervals, 24, 128), 'tm', 0, 0)  18.2 us
    ppermute x1, starting transfers between devices, per_device(): other = lax.ppermute(other, 'gy', others)  6.61 us
    ppermute x1, starting transfers between devices, per_device(): other = lax.ppermute(to_other, 'gy', others)  6.34 us
    pallas_call x1, Pallas kernels, cycle(): return call(cycle_kernel, 9, f32(96, 8, 128), scratch)(other, mate, *upper)  5.74 us
    ppermute x1, waiting for transfers between devices, per_device(): other = lax.ppermute(to_other, 'gy', others)  3.32 us
    pallas_call x1, Pallas kernels, cut(): return call(cut_kernel, 3, outs, scratch, HBM, 60)(init, ends, vel)  2.38 us
    ppermute x1, starting transfers between devices, per_device(): mate = lax.ppermute(to_mate, 'gy', mates)  1.92 us
  transfers between devices with their start and end apart: 4, of which 2 were waited for; matrix products, arithmetic and copies ran while one was open for 0% of the time, Pallas kernels for 3%

profile of v9, /device:TPU:1, one launch (start us, length us, event | category | flops | bytes accessed | tf_op | source)
XLA Modules:
  0.0 82.0 jit_solution(11153736481219252842)
XLA Ops:
  0.6 2.4 %shard_map.50 = (f32[160,8,128]{2,1,0:T(8,128)}, f32[32,8,128]{2,1,0:T(8,128)}) custom-call(f32[3,16,1024]{2,1,0:T(8,128)} %init_hbm.1, f32[3,16,1024]{2,1,0:T(8,128)} %bitcast.13, f32[2,16,1024]{2,1,0:T(8,128)} %bitcast.16), custom_call_target="tpu_custom_call" | custom-call | tf_op jit(solution)/shard_map/pallas_call | solution.py:439
  3.0 29.2 %all_to_all.10 = f32[32,40,128]{2,1,0:T(8,128)S(1)} all-to-all(f32[32,40,128]{2,1,0:T(8,128)} %bitcast.12), channel_id=1, replica_groups=mesh['tm'=32,'gy'=16] {'tm'}, dimensions={0} | all-to-all | bytes 1310720 | tf_op jit(solution)/shard_map/all_to_all | solution.py:491
  32.2 0.2 shard_map.51
  32.5 6.3 %collective-permute-start = (f32[130,8,128]{2,1,0:T(8,128)S(1)}, f32[130,8,128]{2,1,0:T(8,128)S(1)}, u32[]{:S(2)}, u32[]{:S(2)}) collective-permute-start(f32[130,8,128]{2,1,0:T(8,128)S(1)} %get-tuple-element.18), channel_id=1, source_target_pairs={{1,2},{2,1},{3,4},{4,3},{5,6},{6,5},{7,8},{8,7},{9,10},{10,9},{11,... | collective-permute-start | bytes 1597448 | tf_op jit(solution)/shard_map/ppermute | solution.py:494
  38.8 1.9 %collective-permute-start.1 = (f32[130,8,128]{2,1,0:T(8,128)S(1)}, f32[130,8,128]{2,1,0:T(8,128)S(1)}, u32[]{:S(2)}, u32[]{:S(2)}) collective-permute-start(f32[130,8,128]{2,1,0:T(8,128)S(1)} %get-tuple-element.19), channel_id=1, source_target_pairs={{0,1},{1,0},{2,3},{3,2},{4,5},{5,4},{6,7},{7,6},{8,9},{9,8},{10,11... | collective-permute-start | bytes 1597448 | tf_op jit(solution)/shard_map/ppermute | solution.py:495
  40.7 1.7 %shard_map.52 = (f32[12,9,8,128]{3,2,1,0:T(8,128)S(1)}, f32[12,9,8,128]{3,2,1,0:T(8,128)S(1)}, f32[12,9,8,128]{3,2,1,0:T(8,128)S(1)}, f32[12,9,8,128]{3,2,1,0:T(...) custom-call(f32[160,8,128]{2,1,0:T(8,128)S(1)} %get-tuple-element.20.cur), custom_call_target="tpu_custom_call" | custom-call | tf_op jit(solution)/shard_map/pallas_call | solution.py:448
  42.4 3.3 %collective-permute-done.other = f32[130,8,128]{2,1,0:T(8,128)S(1)} collective-permute-done((f32[130,8,128]{2,1,0:T(8,128)S(1)}, f32[130,8,128]{2,1,0:T(8,128)S(1)}, u32[]{:S(2)}, u32[]{:S(2)}) %collective-permute-start) | collective-permute-done | bytes 532512 | tf_op jit(solution)/shard_map/ppermute | solution.py:494
  45.8 0.0 collective-permute-done.1.mate
  45.8 5.7 %shard_map.53 = f32[96,8,128]{2,1,0:T(8,128)S(1)} custom-call(f32[130,8,128]{2,1,0:T(8,128)S(1)} %collective-permute-done.other, f32[130,8,128]{2,1,0:T(8,128)S(1)} %collective-permute-done.1.mate, f32[12,9,8,128]{3,2,1,0:T(8,128)S(1)} %get-tuple-element.21.e0, f32[12,9,8,128]{3,2,1,0:T(8,128)S(1)} %get-tuple-element.22.e1, ...), custom_call_target="tpu_custom_call" | custom-call | tf_op jit(solution)/shard_map/pallas_call | solution.py:466
  51.5 0.0 copy-start
  51.5 18.2 %all_to_all.11 = f32[32,24,128]{2,1,0:T(8,128)S(1)} all-to-all(f32[32,24,128]{2,1,0:T(8,128)S(1)} %bitcast.11), channel_id=1, replica_groups=mesh['tm'=32,'gy'=16] {'tm'}, dimensions={0} | all-to-all | bytes 786432 | tf_op jit(solution)/shard_map/all_to_all | solution.py:497
  69.7 0.0 copy-done
  69.7 0.2 shard_map.55
  69.9 1.9 %collective-permute-start.2 = (f32[20,8,128]{2,1,0:T(8,128)S(1)}, f32[20,8,128]{2,1,0:T(8,128)S(1)}, u32[]{:S(2)}, u32[]{:S(2)}) collective-permute-start(f32[20,8,128]{2,1,0:T(8,128)S(1)} %get-tuple-element.30), channel_id=1, source_target_pairs={{0,1},{1,0},{2,3},{3,2},{4,5},{5,4},{6,7},{7,6},{8,9},{9,8},{10,11... | collective-permute-start | bytes 245768 | tf_op jit(solution)/shard_map/ppermute | solution.py:500
  71.9 6.6 %collective-permute-start.3 = (f32[20,8,128]{2,1,0:T(8,128)S(1)}, f32[20,8,128]{2,1,0:T(8,128)S(1)}, u32[]{:S(2)}, u32[]{:S(2)}) collective-permute-start(f32[20,8,128]{2,1,0:T(8,128)S(1)} %get-tuple-element.31), channel_id=1, source_target_pairs={{1,2},{2,1},{3,4},{4,3},{5,6},{6,5},{7,8},{8,7},{9,10},{10,9},{11,... | collective-permute-start | bytes 245768 | tf_op jit(solution)/shard_map/ppermute | solution.py:501
  78.5 0.9 %shard_map.54 = f32[3,16,1024]{2,1,0:T(8,128)} custom-call(f32[96,8,128]{2,1,0:T(8,128)S(1)} %bitcast.9), custom_call_target="tpu_custom_call" | custom-call | tf_op jit(solution)/shard_map/pallas_call | solution.py:475
  79.4 0.0 collective-permute-done.2.mate
  79.4 1.2 %collective-permute-done.3.other = f32[20,8,128]{2,1,0:T(8,128)S(1)} collective-permute-done((f32[20,8,128]{2,1,0:T(8,128)S(1)}, f32[20,8,128]{2,1,0:T(8,128)S(1)}, u32[]{:S(2)}, u32[]{:S(2)}) %collective-permute-start.3) | collective-permute-done | bytes 81952 | tf_op jit(solution)/shard_map/ppermute | solution.py:501
  80.6 1.4 %shard_map.56 = f32[3,16,1024]{2,1,0:T(8,128)} custom-call(f32[48,8,128]{2,1,0:T(8,128)S(1)} %get-tuple-element.29.mid, f32[32,8,128]{2,1,0:T(8,128)S(1)} %copy-done, f32[20,8,128]{2,1,0:T(8,128)S(1)} %collective-permute-done.2.mate, f32[20,8,128]{2,1,0:T(8,128)S(1)} %collective-permute-done.3.other), custom_call_target="tpu_custom_call" | custom-call | tf_op jit(solution)/shard_map/pallas_call | solution.py:481
Async XLA Ops:
  32.5 13.3 %collective-permute-start = (f32[130,8,128]{2,1,0:T(8,128)S(1)}, f32[130,8,128]{2,1,0:T(8,128)S(1)}, u32[]{:S(2)}, u32[]{:S(2)}) collective-permute-start(f32[130,8,128]{2,1,0:T(8,128)S(1)} %get-tuple-element.18), channel_id=1, source_target_pairs={{1,2},{2,1},{3,4},{4,3},{5,6},{6,5},{7,8},{8,7},{9,10},{10,9},{11,... | collective-permute-start | bytes 1597448 | tf_op jit(solution)/shard_map/ppermute | solution.py:494
  38.8 6.9 %collective-permute-start.1 = (f32[130,8,128]{2,1,0:T(8,128)S(1)}, f32[130,8,128]{2,1,0:T(8,128)S(1)}, u32[]{:S(2)}, u32[]{:S(2)}) collective-permute-start(f32[130,8,128]{2,1,0:T(8,128)S(1)} %get-tuple-element.19), channel_id=1, source_target_pairs={{0,1},{1,0},{2,3},{3,2},{4,5},{5,4},{6,7},{7,6},{8,9},{9,8},{10,11... | collective-permute-start | bytes 1597448 | tf_op jit(solution)/shard_map/ppermute | solution.py:495
  51.5 18.2 %copy-start = (f32[32,8,128]{2,1,0:T(8,128)S(1)}, f32[32,8,128]{2,1,0:T(8,128)}, u32[]{:S(2)}) copy-start(f32[32,8,128]{2,1,0:T(8,128)} %get-tuple-element.28.flow) | copy-start | bytes 393220
  69.9 9.4 %collective-permute-start.2 = (f32[20,8,128]{2,1,0:T(8,128)S(1)}, f32[20,8,128]{2,1,0:T(8,128)S(1)}, u32[]{:S(2)}, u32[]{:S(2)}) collective-permute-start(f32[20,8,128]{2,1,0:T(8,128)S(1)} %get-tuple-element.30), channel_id=1, source_target_pairs={{0,1},{1,0},{2,3},{3,2},{4,5},{5,4},{6,7},{7,6},{8,9},{9,8},{10,11... | collective-permute-start | bytes 245768 | tf_op jit(solution)/shard_map/ppermute | solution.py:500
  71.9 8.7 %collective-permute-start.3 = (f32[20,8,128]{2,1,0:T(8,128)S(1)}, f32[20,8,128]{2,1,0:T(8,128)S(1)}, u32[]{:S(2)}, u32[]{:S(2)}) collective-permute-start(f32[20,8,128]{2,1,0:T(8,128)S(1)} %get-tuple-element.31), channel_id=1, source_target_pairs={{1,2},{2,1},{3,4},{4,3},{5,6},{6,5},{7,8},{8,7},{9,10},{10,9},{11,... | collective-permute-start | bytes 245768 | tf_op jit(solution)/shard_map/ppermute | solution.py:501

commit v10 on v9

--- a/solution.py
+++ b/solution.py
@@ -63,18 +63,21 @@
     return out
 
 
-def cut_kernel(init_hbm, ends_hbm, vel_hbm, out, flow, init, ends, vel, sems):
-    copies = [
-        pltpu.make_async_copy(far, near, sems.at[i])
-        for i, (far, near) in enumerate(((init_hbm, init), (ends_hbm, ends), (vel_hbm, vel)))
-    ]
-    for copy in copies:
+def cut_kernel(init_hbm, ends_hbm, vel_hbm, out_hbm, flow_hbm, init, ends, vel, out, flow, arrive, leave):
+    def fetch(far, near, i, at):
+        copy = pltpu.make_async_copy(far.at[i], near.at[i], arrive.at[at])
         copy.start()
-    for copy in copies:
-        copy.wait()
+        return copy
+
+    coming = {3 + c: [fetch(vel_hbm, vel, c, c)] for c in range(2)}
+    for c in range(3):
+        coming[c] = [fetch(ends_hbm, ends, c, 2 + c), fetch(init_hbm, init, c, 5 + c)]
+    going = []
     last = lax.axis_index("tm") == GROUP * GROUPS - 1
     low = lanes() < HALF
-    for a in range(5):
+    for a in (3, 4, 0, 1, 2):
+        for copy in coming[a]:
+            copy.wait()
         if a < 3:
             top = jnp.where(last, init[a, 0:8, :], ends[a, 0:8, :])
             bottom = jnp.where(last, init[a, 8:16, :], ends[a, 8:16, :])
@@ -85,12 +88,22 @@
             lower = pltpu.roll(bottom, (HALO + HALF - TILE * q) % 1024, 1)
             for b in range(8):
                 at = slice(128 * b, 128 * b + 128)
-                out[(4 * b + q) * 5 + a] = jnp.where(low, upper[:, at], lower[:, at])
-    for c in range(2):
+                out[a, 4 * b + q] = jnp.where(low, upper[:, at], lower[:, at])
+        copy = pltpu.make_async_copy(out.at[a], out_hbm.at[:, a], leave.at[a])
+        copy.start()
+        going.append(copy)
+        if a < 3:
+            continue
         for y0 in (0, 8):
-            blocks = [vel[c, y0 : y0 + 8, 128 * b : 128 * b + 128] for b in range(8)]
+            blocks = [vel[a - 3, y0 : y0 + 8, 128 * b : 128 * b + 128] for b in range(8)]
             for y, value in enumerate(swap8(blocks)):
-                flow[c * ROWS + y0 + y] = value
+                flow[(a - 3) * ROWS + y0 + y] = value
+        if a == 4:
+            copy = pltpu.make_async_copy(flow, flow_hbm, leave.at[5])
+            copy.start()
+            going.append(copy)
+    for copy in going:
+        copy.wait()
 
 
 def fold(own, out, parity):
@@ -420,13 +433,13 @@
     return pltpu.VMEM(shape, jnp.float32)
 
 
-def call(kernel, n_arrays, outs, scratch=(), space=VMEM, mib=24):
+def call(kernel, n_arrays, outs, scratch=(), space=VMEM, to=VMEM, mib=24):
     many = isinstance(outs, tuple)
     return pl.pallas_call(
         kernel,
         out_shape=outs,
         in_specs=[space] * n_arrays,
-        out_specs=(VMEM,) * len(outs) if many else VMEM,
+        out_specs=(to,) * len(outs) if many else to,
         scratch_shapes=list(scratch),
         compiler_params=pltpu.CompilerParams(vmem_limit_bytes=mib * 1024 * 1024),
     )
@@ -434,9 +447,10 @@
 
 def cut(init, ends, vel):
     state, flow = buffer(3, ROWS, 1024), buffer(2, ROWS, 1024)
-    scratch = [state, state, flow, pltpu.SemaphoreType.DMA((3,))]
-    outs = (f32(160, 8, 128), f32(2 * ROWS, 8, 128))
-    return call(cut_kernel, 3, outs, scratch, HBM, 60)(init, ends, vel)
+    scratch = [state, state, flow, buffer(5, 32, 8, 128), buffer(2 * ROWS, 8, 128)]
+    scratch += [pltpu.SemaphoreType.DMA((8,)), pltpu.SemaphoreType.DMA((6,))]
+    outs = (f32(32, 5, 8, 128), f32(2 * ROWS, 8, 128))
+    return call(cut_kernel, 3, outs, scratch, HBM, HBM, 60)(init, ends, vel)
 
 
 def sort(cur):

time: 82.3 us -> 82.3 us (level)
  no operation moved by 1% of the time
where the time goes in v10:
time: 82.3 us; the launch traced here: 82 us
  blocking collectives  47.4 us (58%)
  starting transfers between devices  16.8 us (20%)
  Pallas kernels  12.5 us (15%)
  waiting for transfers between devices  4.54 us (6%)
    all_to_all x1, blocking collectives, per_device(): cur = lax.all_to_all(windows.reshape(intervals, 40, 128), 'tm', 0, 0)  29.2 us
    all_to_all x1, blocking collectives, per_device(): tiles = lax.all_to_all(tiles.reshape(intervals, 24, 128), 'tm', 0, 0)  18.2 us
    ppermute x1, starting transfers between devices, per_device(): other = lax.ppermute(other, 'gy', others)  6.61 us
    ppermute x1, starting transfers between devices, per_device(): other = lax.ppermute(to_other, 'gy', others)  6.34 us
    pallas_call x1, Pallas kernels, cycle(): return call(cycle_kernel, 9, f32(96, 8, 128), scratch)(other, mate, *upper)  5.74 us
    ppermute x1, waiting for transfers between devices, per_device(): other = lax.ppermute(to_other, 'gy', others)  3.32 us
    pallas_call x1, Pallas kernels, cut(): return call(cut_kernel, 3, outs, scratch, HBM, HBM, 60)(init, ends, vel)  2.35 us
    ppermute x1, starting transfers between devices, per_device(): mate = lax.ppermute(to_mate, 'gy', mates)  1.92 us
  transfers between devices with their start and end apart: 4, of which 2 were waited for; matrix products, arithmetic and copies ran while one was open for 0% of the time, Pallas kernels for 3%

profile of v10, /device:TPU:1, one launch (start us, length us, event | category | flops | bytes accessed | tf_op | source)
XLA Modules:
  0.0 82.0 jit_solution(3292710393564052851)
XLA Ops:
  0.6 2.4 %shard_map.50 = (f32[32,5,8,128]{3,2,1,0:T(8,128)}, f32[32,8,128]{2,1,0:T(8,128)}) custom-call(f32[3,16,1024]{2,1,0:T(8,128)} %init_hbm.1, f32[3,16,1024]{2,1,0:T(8,128)} %bitcast.13, f32[2,16,1024]{2,1,0:T(8,128)} %bitcast.16), custom_call_target="tpu_custom_call" | custom-call | tf_op jit(solution)/shard_map/pallas_call | solution.py:453
  3.0 29.2 %all_to_all.10 = f32[32,40,128]{2,1,0:T(8,128)S(1)} all-to-all(f32[32,40,128]{2,1,0:T(8,128)} %bitcast.12), channel_id=1, replica_groups=mesh['tm'=32,'gy'=16] {'tm'}, dimensions={0} | all-to-all | bytes 1310720 | tf_op jit(solution)/shard_map/all_to_all | solution.py:505
  32.2 0.2 shard_map.51
  32.4 6.3 %collective-permute-start = (f32[130,8,128]{2,1,0:T(8,128)S(1)}, f32[130,8,128]{2,1,0:T(8,128)S(1)}, u32[]{:S(2)}, u32[]{:S(2)}) collective-permute-start(f32[130,8,128]{2,1,0:T(8,128)S(1)} %get-tuple-element.18), channel_id=1, source_target_pairs={{1,2},{2,1},{3,4},{4,3},{5,6},{6,5},{7,8},{8,7},{9,10},{10,9},{11,... | collective-permute-start | bytes 1597448 | tf_op jit(solution)/shard_map/ppermute | solution.py:508
  38.8 1.9 %collective-permute-start.1 = (f32[130,8,128]{2,1,0:T(8,128)S(1)}, f32[130,8,128]{2,1,0:T(8,128)S(1)}, u32[]{:S(2)}, u32[]{:S(2)}) collective-permute-start(f32[130,8,128]{2,1,0:T(8,128)S(1)} %get-tuple-element.19), channel_id=1, source_target_pairs={{0,1},{1,0},{2,3},{3,2},{4,5},{5,4},{6,7},{7,6},{8,9},{9,8},{10,11... | collective-permute-start | bytes 1597448 | tf_op jit(solution)/shard_map/ppermute | solution.py:509
  40.7 1.7 %shard_map.52 = (f32[12,9,8,128]{3,2,1,0:T(8,128)S(1)}, f32[12,9,8,128]{3,2,1,0:T(8,128)S(1)}, f32[12,9,8,128]{3,2,1,0:T(8,128)S(1)}, f32[12,9,8,128]{3,2,1,0:T(...) custom-call(f32[160,8,128]{2,1,0:T(8,128)S(1)} %get-tuple-element.20.cur), custom_call_target="tpu_custom_call" | custom-call | tf_op jit(solution)/shard_map/pallas_call | solution.py:462
  42.4 3.3 %collective-permute-done.other = f32[130,8,128]{2,1,0:T(8,128)S(1)} collective-permute-done((f32[130,8,128]{2,1,0:T(8,128)S(1)}, f32[130,8,128]{2,1,0:T(8,128)S(1)}, u32[]{:S(2)}, u32[]{:S(2)}) %collective-permute-start) | collective-permute-done | bytes 532512 | tf_op jit(solution)/shard_map/ppermute | solution.py:508
  45.7 0.0 collective-permute-done.1.mate
  45.7 5.7 %shard_map.53 = f32[96,8,128]{2,1,0:T(8,128)S(1)} custom-call(f32[130,8,128]{2,1,0:T(8,128)S(1)} %collective-permute-done.other, f32[130,8,128]{2,1,0:T(8,128)S(1)} %collective-permute-done.1.mate, f32[12,9,8,128]{3,2,1,0:T(8,128)S(1)} %get-tuple-element.21.e0, f32[12,9,8,128]{3,2,1,0:T(8,128)S(1)} %get-tuple-element.22.e1, ...), custom_call_target="tpu_custom_call" | custom-call | tf_op jit(solution)/shard_map/pallas_call | solution.py:480
  51.5 0.0 copy-start
  51.5 18.2 %all_to_all.11 = f32[32,24,128]{2,1,0:T(8,128)S(1)} all-to-all(f32[32,24,128]{2,1,0:T(8,128)S(1)} %bitcast.11), channel_id=1, replica_groups=mesh['tm'=32,'gy'=16] {'tm'}, dimensions={0} | all-to-all | bytes 786432 | tf_op jit(solution)/shard_map/all_to_all | solution.py:511
  69.7 0.0 copy-done
  69.7 0.2 shard_map.55
  69.9 1.9 %collective-permute-start.2 = (f32[20,8,128]{2,1,0:T(8,128)S(1)}, f32[20,8,128]{2,1,0:T(8,128)S(1)}, u32[]{:S(2)}, u32[]{:S(2)}) collective-permute-start(f32[20,8,128]{2,1,0:T(8,128)S(1)} %get-tuple-element.30), channel_id=1, source_target_pairs={{0,1},{1,0},{2,3},{3,2},{4,5},{5,4},{6,7},{7,6},{8,9},{9,8},{10,11... | collective-permute-start | bytes 245768 | tf_op jit(solution)/shard_map/ppermute | solution.py:514
  71.8 6.6 %collective-permute-start.3 = (f32[20,8,128]{2,1,0:T(8,128)S(1)}, f32[20,8,128]{2,1,0:T(8,128)S(1)}, u32[]{:S(2)}, u32[]{:S(2)}) collective-permute-start(f32[20,8,128]{2,1,0:T(8,128)S(1)} %get-tuple-element.31), channel_id=1, source_target_pairs={{1,2},{2,1},{3,4},{4,3},{5,6},{6,5},{7,8},{8,7},{9,10},{10,9},{11,... | collective-permute-start | bytes 245768 | tf_op jit(solution)/shard_map/ppermute | solution.py:515
  78.4 0.9 %shard_map.54 = f32[3,16,1024]{2,1,0:T(8,128)} custom-call(f32[96,8,128]{2,1,0:T(8,128)S(1)} %bitcast.9), custom_call_target="tpu_custom_call" | custom-call | tf_op jit(solution)/shard_map/pallas_call | solution.py:489
  79.3 0.0 collective-permute-done.2.mate
  79.3 1.2 %collective-permute-done.3.other = f32[20,8,128]{2,1,0:T(8,128)S(1)} collective-permute-done((f32[20,8,128]{2,1,0:T(8,128)S(1)}, f32[20,8,128]{2,1,0:T(8,128)S(1)}, u32[]{:S(2)}, u32[]{:S(2)}) %collective-permute-start.3) | collective-permute-done | bytes 81952 | tf_op jit(solution)/shard_map/ppermute | solution.py:515
  80.6 1.4 %shard_map.56 = f32[3,16,1024]{2,1,0:T(8,128)} custom-call(f32[48,8,128]{2,1,0:T(8,128)S(1)} %get-tuple-element.29.mid, f32[32,8,128]{2,1,0:T(8,128)S(1)} %copy-done, f32[20,8,128]{2,1,0:T(8,128)S(1)} %collective-permute-done.2.mate, f32[20,8,128]{2,1,0:T(8,128)S(1)} %collective-permute-done.3.other), custom_call_target="tpu_custom_call" | custom-call | tf_op jit(solution)/shard_map/pallas_call | solution.py:495
Async XLA Ops:
  32.4 13.3 %collective-permute-start = (f32[130,8,128]{2,1,0:T(8,128)S(1)}, f32[130,8,128]{2,1,0:T(8,128)S(1)}, u32[]{:S(2)}, u32[]{:S(2)}) collective-permute-start(f32[130,8,128]{2,1,0:T(8,128)S(1)} %get-tuple-element.18), channel_id=1, source_target_pairs={{1,2},{2,1},{3,4},{4,3},{5,6},{6,5},{7,8},{8,7},{9,10},{10,9},{11,... | collective-permute-start | bytes 1597448 | tf_op jit(solution)/shard_map/ppermute | solution.py:508
  38.8 6.9 %collective-permute-start.1 = (f32[130,8,128]{2,1,0:T(8,128)S(1)}, f32[130,8,128]{2,1,0:T(8,128)S(1)}, u32[]{:S(2)}, u32[]{:S(2)}) collective-permute-start(f32[130,8,128]{2,1,0:T(8,128)S(1)} %get-tuple-element.19), channel_id=1, source_target_pairs={{0,1},{1,0},{2,3},{3,2},{4,5},{5,4},{6,7},{7,6},{8,9},{9,8},{10,11... | collective-permute-start | bytes 1597448 | tf_op jit(solution)/shard_map/ppermute | solution.py:509
  51.5 18.2 %copy-start = (f32[32,8,128]{2,1,0:T(8,128)S(1)}, f32[32,8,128]{2,1,0:T(8,128)}, u32[]{:S(2)}) copy-start(f32[32,8,128]{2,1,0:T(8,128)} %get-tuple-element.28.flow) | copy-start | bytes 393220
  69.9 9.4 %collective-permute-start.2 = (f32[20,8,128]{2,1,0:T(8,128)S(1)}, f32[20,8,128]{2,1,0:T(8,128)S(1)}, u32[]{:S(2)}, u32[]{:S(2)}) collective-permute-start(f32[20,8,128]{2,1,0:T(8,128)S(1)} %get-tuple-element.30), channel_id=1, source_target_pairs={{0,1},{1,0},{2,3},{3,2},{4,5},{5,4},{6,7},{7,6},{8,9},{9,8},{10,11... | collective-permute-start | bytes 245768 | tf_op jit(solution)/shard_map/ppermute | solution.py:514
  71.8 8.7 %collective-permute-start.3 = (f32[20,8,128]{2,1,0:T(8,128)S(1)}, f32[20,8,128]{2,1,0:T(8,128)S(1)}, u32[]{:S(2)}, u32[]{:S(2)}) collective-permute-start(f32[20,8,128]{2,1,0:T(8,128)S(1)} %get-tuple-element.31), channel_id=1, source_target_pairs={{1,2},{2,1},{3,4},{4,3},{5,6},{6,5},{7,8},{8,7},{9,10},{10,9},{11,... | collective-permute-start | bytes 245768 | tf_op jit(solution)/shard_map/ppermute | solution.py:515

commit v11 on v10

--- a/solution.py
+++ b/solution.py
@@ -374,7 +374,7 @@
             own[c, 8:16, at] = gathered(tiles, c, b, 1)
 
 
-def relax_kernel(mid, flow, mate, other, out, wa, wb, vv):
+def relax_kernel(mid, flow, other, mate, out, wa, wb, vv):
     lane = lanes()
     tall = ROWS + 2 * FINE
     kappa = time_step * kappa_coupling
@@ -489,10 +489,10 @@
     return call(own_kernel, 1, f32(3, ROWS, 1024))(tiles)
 
 
-def relax(mid, flow, mate, other):
+def relax(mid, flow, other, mate):
     tall = ROWS + 2 * FINE
     scratch = [buffer(3 * tall, 8, 128), buffer(3 * tall, 8, 128), buffer(2 * tall, 8, 128)]
-    return call(relax_kernel, 4, f32(3, ROWS, 1024), scratch)(mid, flow, mate, other)
+    return call(relax_kernel, 4, f32(3, ROWS, 1024), scratch)(mid, flow, other, mate)
 
 
 def per_device(initial_state, guessed_ends, velocity):
@@ -514,7 +514,7 @@
     mate = lax.ppermute(mate, "gy", mates)
     other = lax.ppermute(other, "gy", others)
     own = owns(tiles)
-    relaxed = relax(mid, flow, mate, other)
+    relaxed = relax(mid, flow, other, mate)
     return own[None], relaxed[None]
 
 

time: 82.3 us -> 81.5 us (level)
  waiting for transfers between devices: 4.54 us -> 3.67 us
    ppermute x1, waiting for transfers between devices: 1.21 us -> 0.01 us  [per_device(): other = lax.ppermute(other, 'gy', others)]
where the time goes in v11:
time: 81.5 us; the launch traced here: 81.1 us
  blocking collectives  47.4 us (58%)
  starting transfers between devices  16.8 us (21%)
  Pallas kernels  12.5 us (15%)
  waiting for transfers between devices  3.67 us (5%)
    all_to_all x1, blocking collectives, per_device(): cur = lax.all_to_all(windows.reshape(intervals, 40, 128), 'tm', 0, 0)  29.2 us
    all_to_all x1, blocking collectives, per_device(): tiles = lax.all_to_all(tiles.reshape(intervals, 24, 128), 'tm', 0, 0)  18.2 us
    ppermute x1, starting transfers between devices, per_device(): other = lax.ppermute(other, 'gy', others)  6.61 us
    ppermute x1, starting transfers between devices, per_device(): other = lax.ppermute(to_other, 'gy', others)  6.34 us
    pallas_call x1, Pallas kernels, cycle(): return call(cycle_kernel, 9, f32(96, 8, 128), scratch)(other, mate, *upper)  5.74 us
    ppermute x1, waiting for transfers between devices, per_device(): other = lax.ppermute(to_other, 'gy', others)  3.32 us
    pallas_call x1, Pallas kernels, cut(): return call(cut_kernel, 3, outs, scratch, HBM, HBM, 60)(init, ends, vel)  2.35 us
    ppermute x1, starting transfers between devices, per_device(): mate = lax.ppermute(to_mate, 'gy', mates)  1.92 us
  transfers between devices with their start and end apart: 4, of which 2 were waited for; matrix products, arithmetic and copies ran while one was open for 0% of the time, Pallas kernels for 3%

profile of v11, /device:TPU:1, one launch (start us, length us, event | category | flops | bytes accessed | tf_op | source)
XLA Modules:
  0.0 81.1 jit_solution(15530652792805175281)
XLA Ops:
  0.6 2.4 %shard_map.50 = (f32[32,5,8,128]{3,2,1,0:T(8,128)}, f32[32,8,128]{2,1,0:T(8,128)}) custom-call(f32[3,16,1024]{2,1,0:T(8,128)} %init_hbm.1, f32[3,16,1024]{2,1,0:T(8,128)} %bitcast.13, f32[2,16,1024]{2,1,0:T(8,128)} %bitcast.16), custom_call_target="tpu_custom_call" | custom-call | tf_op jit(solution)/shard_map/pallas_call | solution.py:453
  3.0 29.2 %all_to_all.10 = f32[32,40,128]{2,1,0:T(8,128)S(1)} all-to-all(f32[32,40,128]{2,1,0:T(8,128)} %bitcast.12), channel_id=1, replica_groups=mesh['tm'=32,'gy'=16] {'tm'}, dimensions={0} | all-to-all | bytes 1310720 | tf_op jit(solution)/shard_map/all_to_all | solution.py:505
  32.2 0.2 shard_map.51
  32.4 6.3 %collective-permute-start = (f32[130,8,128]{2,1,0:T(8,128)S(1)}, f32[130,8,128]{2,1,0:T(8,128)S(1)}, u32[]{:S(2)}, u32[]{:S(2)}) collective-permute-start(f32[130,8,128]{2,1,0:T(8,128)S(1)} %get-tuple-element.18), channel_id=1, source_target_pairs={{1,2},{2,1},{3,4},{4,3},{5,6},{6,5},{7,8},{8,7},{9,10},{10,9},{11,... | collective-permute-start | bytes 1597448 | tf_op jit(solution)/shard_map/ppermute | solution.py:508
  38.8 1.9 %collective-permute-start.1 = (f32[130,8,128]{2,1,0:T(8,128)S(1)}, f32[130,8,128]{2,1,0:T(8,128)S(1)}, u32[]{:S(2)}, u32[]{:S(2)}) collective-permute-start(f32[130,8,128]{2,1,0:T(8,128)S(1)} %get-tuple-element.19), channel_id=1, source_target_pairs={{0,1},{1,0},{2,3},{3,2},{4,5},{5,4},{6,7},{7,6},{8,9},{9,8},{10,11... | collective-permute-start | bytes 1597448 | tf_op jit(solution)/shard_map/ppermute | solution.py:509
  40.7 1.7 %shard_map.52 = (f32[12,9,8,128]{3,2,1,0:T(8,128)S(1)}, f32[12,9,8,128]{3,2,1,0:T(8,128)S(1)}, f32[12,9,8,128]{3,2,1,0:T(8,128)S(1)}, f32[12,9,8,128]{3,2,1,0:T(...) custom-call(f32[160,8,128]{2,1,0:T(8,128)S(1)} %get-tuple-element.20.cur), custom_call_target="tpu_custom_call" | custom-call | tf_op jit(solution)/shard_map/pallas_call | solution.py:462
  42.4 3.3 %collective-permute-done.other = f32[130,8,128]{2,1,0:T(8,128)S(1)} collective-permute-done((f32[130,8,128]{2,1,0:T(8,128)S(1)}, f32[130,8,128]{2,1,0:T(8,128)S(1)}, u32[]{:S(2)}, u32[]{:S(2)}) %collective-permute-start) | collective-permute-done | bytes 532512 | tf_op jit(solution)/shard_map/ppermute | solution.py:508
  45.7 0.0 collective-permute-done.1.mate
  45.7 5.7 %shard_map.53 = f32[96,8,128]{2,1,0:T(8,128)S(1)} custom-call(f32[130,8,128]{2,1,0:T(8,128)S(1)} %collective-permute-done.other, f32[130,8,128]{2,1,0:T(8,128)S(1)} %collective-permute-done.1.mate, f32[12,9,8,128]{3,2,1,0:T(8,128)S(1)} %get-tuple-element.21.e0, f32[12,9,8,128]{3,2,1,0:T(8,128)S(1)} %get-tuple-element.22.e1, ...), custom_call_target="tpu_custom_call" | custom-call | tf_op jit(solution)/shard_map/pallas_call | solution.py:480
  51.5 0.0 copy-start
  51.5 18.2 %all_to_all.11 = f32[32,24,128]{2,1,0:T(8,128)S(1)} all-to-all(f32[32,24,128]{2,1,0:T(8,128)S(1)} %bitcast.11), channel_id=1, replica_groups=mesh['tm'=32,'gy'=16] {'tm'}, dimensions={0} | all-to-all | bytes 786432 | tf_op jit(solution)/shard_map/all_to_all | solution.py:511
  69.7 0.0 copy-done
  69.7 0.2 shard_map.55
  69.9 6.6 %collective-permute-start.2 = (f32[20,8,128]{2,1,0:T(8,128)S(1)}, f32[20,8,128]{2,1,0:T(8,128)S(1)}, u32[]{:S(2)}, u32[]{:S(2)}) collective-permute-start(f32[20,8,128]{2,1,0:T(8,128)S(1)} %get-tuple-element.30), channel_id=1, source_target_pairs={{1,2},{2,1},{3,4},{4,3},{5,6},{6,5},{7,8},{8,7},{9,10},{10,9},{11,... | collective-permute-start | bytes 245768 | tf_op jit(solution)/shard_map/ppermute | solution.py:515
  76.5 1.9 %collective-permute-start.3 = (f32[20,8,128]{2,1,0:T(8,128)S(1)}, f32[20,8,128]{2,1,0:T(8,128)S(1)}, u32[]{:S(2)}, u32[]{:S(2)}) collective-permute-start(f32[20,8,128]{2,1,0:T(8,128)S(1)} %get-tuple-element.31), channel_id=1, source_target_pairs={{0,1},{1,0},{2,3},{3,2},{4,5},{5,4},{6,7},{7,6},{8,9},{9,8},{10,11... | collective-permute-start | bytes 245768 | tf_op jit(solution)/shard_map/ppermute | solution.py:514
  78.4 0.9 %shard_map.54 = f32[3,16,1024]{2,1,0:T(8,128)} custom-call(f32[96,8,128]{2,1,0:T(8,128)S(1)} %bitcast.9), custom_call_target="tpu_custom_call" | custom-call | tf_op jit(solution)/shard_map/pallas_call | solution.py:489
  79.3 0.0 collective-permute-done.2.other
  79.3 0.3 collective-permute-done.3.mate
  79.7 1.4 %shard_map.56 = f32[3,16,1024]{2,1,0:T(8,128)} custom-call(f32[48,8,128]{2,1,0:T(8,128)S(1)} %get-tuple-element.29.mid, f32[32,8,128]{2,1,0:T(8,128)S(1)} %copy-done, f32[20,8,128]{2,1,0:T(8,128)S(1)} %collective-permute-done.2.other, f32[20,8,128]{2,1,0:T(8,128)S(1)} %collective-permute-done.3.mate), custom_call_target="tpu_custom_call" | custom-call | tf_op jit(solution)/shard_map/pallas_call | solution.py:495
Async XLA Ops:
  32.4 13.3 %collective-permute-start = (f32[130,8,128]{2,1,0:T(8,128)S(1)}, f32[130,8,128]{2,1,0:T(8,128)S(1)}, u32[]{:S(2)}, u32[]{:S(2)}) collective-permute-start(f32[130,8,128]{2,1,0:T(8,128)S(1)} %get-tuple-element.18), channel_id=1, source_target_pairs={{1,2},{2,1},{3,4},{4,3},{5,6},{6,5},{7,8},{8,7},{9,10},{10,9},{11,... | collective-permute-start | bytes 1597448 | tf_op jit(solution)/shard_map/ppermute | solution.py:508
  38.8 6.9 %collective-permute-start.1 = (f32[130,8,128]{2,1,0:T(8,128)S(1)}, f32[130,8,128]{2,1,0:T(8,128)S(1)}, u32[]{:S(2)}, u32[]{:S(2)}) collective-permute-start(f32[130,8,128]{2,1,0:T(8,128)S(1)} %get-tuple-element.19), channel_id=1, source_target_pairs={{0,1},{1,0},{2,3},{3,2},{4,5},{5,4},{6,7},{7,6},{8,9},{9,8},{10,11... | collective-permute-start | bytes 1597448 | tf_op jit(solution)/shard_map/ppermute | solution.py:509
  51.5 18.2 %copy-start = (f32[32,8,128]{2,1,0:T(8,128)S(1)}, f32[32,8,128]{2,1,0:T(8,128)}, u32[]{:S(2)}) copy-start(f32[32,8,128]{2,1,0:T(8,128)} %get-tuple-element.28.flow) | copy-start | bytes 393220
  69.9 9.4 %collective-permute-start.2 = (f32[20,8,128]{2,1,0:T(8,128)S(1)}, f32[20,8,128]{2,1,0:T(8,128)S(1)}, u32[]{:S(2)}, u32[]{:S(2)}) collective-permute-start(f32[20,8,128]{2,1,0:T(8,128)S(1)} %get-tuple-element.30), channel_id=1, source_target_pairs={{1,2},{2,1},{3,4},{4,3},{5,6},{6,5},{7,8},{8,7},{9,10},{10,9},{11,... | collective-permute-start | bytes 245768 | tf_op jit(solution)/shard_map/ppermute | solution.py:515
  76.5 3.2 %collective-permute-start.3 = (f32[20,8,128]{2,1,0:T(8,128)S(1)}, f32[20,8,128]{2,1,0:T(8,128)S(1)}, u32[]{:S(2)}, u32[]{:S(2)}) collective-permute-start(f32[20,8,128]{2,1,0:T(8,128)S(1)} %get-tuple-element.31), channel_id=1, source_target_pairs={{0,1},{1,0},{2,3},{3,2},{4,5},{5,4},{6,7},{7,6},{8,9},{9,8},{10,11... | collective-permute-start | bytes 245768 | tf_op jit(solution)/shard_map/ppermute | solution.py:514

commit v12 on v11

--- a/solution.py
+++ b/solution.py
@@ -374,7 +374,7 @@
             own[c, 8:16, at] = gathered(tiles, c, b, 1)
 
 
-def relax_kernel(mid, flow, other, mate, out, wa, wb, vv):
+def relax_kernel(mid, flow, other, mate, out, wa, wb, vv, near, leave):
     lane = lanes()
     tall = ROWS + 2 * FINE
     kappa = time_step * kappa_coupling
@@ -415,10 +415,16 @@
                 if section < FINE - 1:
                     to[c * tall + r] = new[c]
         if section == FINE - 1:
+            going = []
             for y0 in (0, 8):
+                at = pl.ds(y0, 8)
                 for c in range(3):
                     for b, value in enumerate(swap8([ends[y0 + y][c] for y in range(8)])):
-                        out[c, y0 : y0 + 8, 128 * b : 128 * b + 128] = value
+                        near[c, at, 128 * b : 128 * b + 128] = value
+                going.append(pltpu.make_async_copy(near.at[:, at], out.at[:, at], leave.at[y0 // 8]))
+                going[-1].start()
+            for copy in going:
+                copy.wait()
 
     for section in range(FINE):
         buf, to = (wa, wb) if section % 2 == 0 else (wb, wa)
@@ -492,7 +498,8 @@
 def relax(mid, flow, other, mate):
     tall = ROWS + 2 * FINE
     scratch = [buffer(3 * tall, 8, 128), buffer(3 * tall, 8, 128), buffer(2 * tall, 8, 128)]
-    return call(relax_kernel, 4, f32(3, ROWS, 1024), scratch)(mid, flow, other, mate)
+    scratch += [buffer(3, ROWS, 1024), pltpu.SemaphoreType.DMA((2,))]
+    return call(relax_kernel, 4, f32(3, ROWS, 1024), scratch, to=HBM)(mid, flow, other, mate)
 
 
 def per_device(initial_state, guessed_ends, velocity):

time: 81.5 us -> 81.4 us (level)
  no operation moved by 1% of the time
where the time goes in v12:
time: 81.4 us; the launch traced here: 81.1 us
  blocking collectives  47.4 us (58%)
  starting transfers between devices  16.8 us (21%)
  Pallas kernels  12.5 us (15%)
  waiting for transfers between devices  3.67 us (5%)
    all_to_all x1, blocking collectives, per_device(): cur = lax.all_to_all(windows.reshape(intervals, 40, 128), 'tm', 0, 0)  29.2 us
    all_to_all x1, blocking collectives, per_device(): tiles = lax.all_to_all(tiles.reshape(intervals, 24, 128), 'tm', 0, 0)  18.2 us
    ppermute x1, starting transfers between devices, per_device(): other = lax.ppermute(other, 'gy', others)  6.61 us
    ppermute x1, starting transfers between devices, per_device(): other = lax.ppermute(to_other, 'gy', others)  6.34 us
    pallas_call x1, Pallas kernels, cycle(): return call(cycle_kernel, 9, f32(96, 8, 128), scratch)(other, mate, *upper)  5.74 us
    ppermute x1, waiting for transfers between devices, per_device(): other = lax.ppermute(to_other, 'gy', others)  3.32 us
    pallas_call x1, Pallas kernels, cut(): return call(cut_kernel, 3, outs, scratch, HBM, HBM, 60)(init, ends, vel)  2.35 us
    ppermute x1, starting transfers between devices, per_device(): mate = lax.ppermute(mate, 'gy', mates)  1.92 us
  transfers between devices with their start and end apart: 4, of which 2 were waited for; matrix products, arithmetic and copies ran while one was open for 0% of the time, Pallas kernels for 3%

profile of v12, /device:TPU:1, one launch (start us, length us, event | category | flops | bytes accessed | tf_op | source)
XLA Modules:
  0.0 81.1 jit_solution(9642180571335791252)
XLA Ops:
  0.6 2.4 %shard_map.50 = (f32[32,5,8,128]{3,2,1,0:T(8,128)}, f32[32,8,128]{2,1,0:T(8,128)}) custom-call(f32[3,16,1024]{2,1,0:T(8,128)} %init_hbm.1, f32[3,16,1024]{2,1,0:T(8,128)} %bitcast.13, f32[2,16,1024]{2,1,0:T(8,128)} %bitcast.16), custom_call_target="tpu_custom_call" | custom-call | tf_op jit(solution)/shard_map/pallas_call | solution.py:459
  3.0 29.2 %all_to_all.10 = f32[32,40,128]{2,1,0:T(8,128)S(1)} all-to-all(f32[32,40,128]{2,1,0:T(8,128)} %bitcast.12), channel_id=1, replica_groups=mesh['tm'=32,'gy'=16] {'tm'}, dimensions={0} | all-to-all | bytes 1310720 | tf_op jit(solution)/shard_map/all_to_all | solution.py:512
  32.2 0.2 shard_map.51
  32.4 6.3 %collective-permute-start = (f32[130,8,128]{2,1,0:T(8,128)S(1)}, f32[130,8,128]{2,1,0:T(8,128)S(1)}, u32[]{:S(2)}, u32[]{:S(2)}) collective-permute-start(f32[130,8,128]{2,1,0:T(8,128)S(1)} %get-tuple-element.18), channel_id=1, source_target_pairs={{1,2},{2,1},{3,4},{4,3},{5,6},{6,5},{7,8},{8,7},{9,10},{10,9},{11,... | collective-permute-start | bytes 1597448 | tf_op jit(solution)/shard_map/ppermute | solution.py:515
  38.8 1.9 %collective-permute-start.1 = (f32[130,8,128]{2,1,0:T(8,128)S(1)}, f32[130,8,128]{2,1,0:T(8,128)S(1)}, u32[]{:S(2)}, u32[]{:S(2)}) collective-permute-start(f32[130,8,128]{2,1,0:T(8,128)S(1)} %get-tuple-element.19), channel_id=1, source_target_pairs={{0,1},{1,0},{2,3},{3,2},{4,5},{5,4},{6,7},{7,6},{8,9},{9,8},{10,11... | collective-permute-start | bytes 1597448 | tf_op jit(solution)/shard_map/ppermute | solution.py:516
  40.7 1.7 %shard_map.52 = (f32[12,9,8,128]{3,2,1,0:T(8,128)S(1)}, f32[12,9,8,128]{3,2,1,0:T(8,128)S(1)}, f32[12,9,8,128]{3,2,1,0:T(8,128)S(1)}, f32[12,9,8,128]{3,2,1,0:T(...) custom-call(f32[160,8,128]{2,1,0:T(8,128)S(1)} %get-tuple-element.20.cur), custom_call_target="tpu_custom_call" | custom-call | tf_op jit(solution)/shard_map/pallas_call | solution.py:468
  42.4 3.3 %collective-permute-done.other = f32[130,8,128]{2,1,0:T(8,128)S(1)} collective-permute-done((f32[130,8,128]{2,1,0:T(8,128)S(1)}, f32[130,8,128]{2,1,0:T(8,128)S(1)}, u32[]{:S(2)}, u32[]{:S(2)}) %collective-permute-start) | collective-permute-done | bytes 532512 | tf_op jit(solution)/shard_map/ppermute | solution.py:515
  45.7 0.0 collective-permute-done.1.mate
  45.7 5.7 %shard_map.53 = f32[96,8,128]{2,1,0:T(8,128)S(1)} custom-call(f32[130,8,128]{2,1,0:T(8,128)S(1)} %collective-permute-done.other, f32[130,8,128]{2,1,0:T(8,128)S(1)} %collective-permute-done.1.mate, f32[12,9,8,128]{3,2,1,0:T(8,128)S(1)} %get-tuple-element.21.e0, f32[12,9,8,128]{3,2,1,0:T(8,128)S(1)} %get-tuple-element.22.e1, ...), custom_call_target="tpu_custom_call" | custom-call | tf_op jit(solution)/shard_map/pallas_call | solution.py:486
  51.5 0.0 copy-start
  51.5 18.2 %all_to_all.11 = f32[32,24,128]{2,1,0:T(8,128)S(1)} all-to-all(f32[32,24,128]{2,1,0:T(8,128)S(1)} %bitcast.11), channel_id=1, replica_groups=mesh['tm'=32,'gy'=16] {'tm'}, dimensions={0} | all-to-all | bytes 786432 | tf_op jit(solution)/shard_map/all_to_all | solution.py:518
  69.7 0.0 copy-done
  69.7 0.2 shard_map.55
  69.9 6.6 %collective-permute-start.2 = (f32[20,8,128]{2,1,0:T(8,128)S(1)}, f32[20,8,128]{2,1,0:T(8,128)S(1)}, u32[]{:S(2)}, u32[]{:S(2)}) collective-permute-start(f32[20,8,128]{2,1,0:T(8,128)S(1)} %get-tuple-element.30), channel_id=1, source_target_pairs={{1,2},{2,1},{3,4},{4,3},{5,6},{6,5},{7,8},{8,7},{9,10},{10,9},{11,... | collective-permute-start | bytes 245768 | tf_op jit(solution)/shard_map/ppermute | solution.py:522
  76.5 1.9 %collective-permute-start.3 = (f32[20,8,128]{2,1,0:T(8,128)S(1)}, f32[20,8,128]{2,1,0:T(8,128)S(1)}, u32[]{:S(2)}, u32[]{:S(2)}) collective-permute-start(f32[20,8,128]{2,1,0:T(8,128)S(1)} %get-tuple-element.31), channel_id=1, source_target_pairs={{0,1},{1,0},{2,3},{3,2},{4,5},{5,4},{6,7},{7,6},{8,9},{9,8},{10,11... | collective-permute-start | bytes 245768 | tf_op jit(solution)/shard_map/ppermute | solution.py:521
  78.4 0.9 %shard_map.54 = f32[3,16,1024]{2,1,0:T(8,128)} custom-call(f32[96,8,128]{2,1,0:T(8,128)S(1)} %bitcast.9), custom_call_target="tpu_custom_call" | custom-call | tf_op jit(solution)/shard_map/pallas_call | solution.py:495
  79.3 0.0 collective-permute-done.2.other
  79.3 0.3 collective-permute-done.3.mate
  79.7 1.4 %shard_map.56 = f32[3,16,1024]{2,1,0:T(8,128)} custom-call(f32[48,8,128]{2,1,0:T(8,128)S(1)} %get-tuple-element.29.mid, f32[32,8,128]{2,1,0:T(8,128)S(1)} %copy-done, f32[20,8,128]{2,1,0:T(8,128)S(1)} %collective-permute-done.2.other, f32[20,8,128]{2,1,0:T(8,128)S(1)} %collective-permute-done.3.mate), custom_call_target="tpu_custom_call" | custom-call | tf_op jit(solution)/shard_map/pallas_call | solution.py:502
Async XLA Ops:
  32.4 13.3 %collective-permute-start = (f32[130,8,128]{2,1,0:T(8,128)S(1)}, f32[130,8,128]{2,1,0:T(8,128)S(1)}, u32[]{:S(2)}, u32[]{:S(2)}) collective-permute-start(f32[130,8,128]{2,1,0:T(8,128)S(1)} %get-tuple-element.18), channel_id=1, source_target_pairs={{1,2},{2,1},{3,4},{4,3},{5,6},{6,5},{7,8},{8,7},{9,10},{10,9},{11,... | collective-permute-start | bytes 1597448 | tf_op jit(solution)/shard_map/ppermute | solution.py:515
  38.8 6.9 %collective-permute-start.1 = (f32[130,8,128]{2,1,0:T(8,128)S(1)}, f32[130,8,128]{2,1,0:T(8,128)S(1)}, u32[]{:S(2)}, u32[]{:S(2)}) collective-permute-start(f32[130,8,128]{2,1,0:T(8,128)S(1)} %get-tuple-element.19), channel_id=1, source_target_pairs={{0,1},{1,0},{2,3},{3,2},{4,5},{5,4},{6,7},{7,6},{8,9},{9,8},{10,11... | collective-permute-start | bytes 1597448 | tf_op jit(solution)/shard_map/ppermute | solution.py:516
  51.5 18.2 %copy-start = (f32[32,8,128]{2,1,0:T(8,128)S(1)}, f32[32,8,128]{2,1,0:T(8,128)}, u32[]{:S(2)}) copy-start(f32[32,8,128]{2,1,0:T(8,128)} %get-tuple-element.28.flow) | copy-start | bytes 393220
  69.9 9.4 %collective-permute-start.2 = (f32[20,8,128]{2,1,0:T(8,128)S(1)}, f32[20,8,128]{2,1,0:T(8,128)S(1)}, u32[]{:S(2)}, u32[]{:S(2)}) collective-permute-start(f32[20,8,128]{2,1,0:T(8,128)S(1)} %get-tuple-element.30), channel_id=1, source_target_pairs={{1,2},{2,1},{3,4},{4,3},{5,6},{6,5},{7,8},{8,7},{9,10},{10,9},{11,... | collective-permute-start | bytes 245768 | tf_op jit(solution)/shard_map/ppermute | solution.py:522
  76.5 3.2 %collective-permute-start.3 = (f32[20,8,128]{2,1,0:T(8,128)S(1)}, f32[20,8,128]{2,1,0:T(8,128)S(1)}, u32[]{:S(2)}, u32[]{:S(2)}) collective-permute-start(f32[20,8,128]{2,1,0:T(8,128)S(1)} %get-tuple-element.31), channel_id=1, source_target_pairs={{0,1},{1,0},{2,3},{3,2},{4,5},{5,4},{6,7},{7,6},{8,9},{9,8},{10,11... | collective-permute-start | bytes 245768 | tf_op jit(solution)/shard_map/ppermute | solution.py:521
